TPU v7x, 32 devices: a whole 2x2x4 slice. The times are simulated.
32 devices in a mesh: dp: 4 (over y, x), row: 2 (over core), col: 4 (over z).
Axes of the slice: x: 2, y: 2, z: 4, core: 2. Of those that a mesh axis runs over, the one named last changes fastest.
Arguments:
- hidden: bfloat16 [16384, 1024], P(('dp', 'row'), 'col'), may hold values from -6 to 6
- encoder: bfloat16 [16384, 1024], P(('dp', 'row'), 'col'), may hold values from -6 to 6
- cotangent: bfloat16 [16384, 1024], P(('dp', 'row'), 'col'), may hold values from -6 to 6
- answer_length: int32 [16], P('dp'), may hold values from 256 to 1024, as said below
- passage_length: int32 [16], P('dp'), may hold values from 256 to 1024, as said below
- self_input: bfloat16 [1024, 3, 1024], P('col', None, 'row'), may hold values from -0.1875 to 0.1875
- self_output: bfloat16 [1024, 1024], P('row', 'col'), may hold values from -1.5 to 1.5
- cross_query: bfloat16 [1024, 1024], P('col', 'row'), may hold values from -0.1875 to 0.1875
- cross_memory: bfloat16 [1024, 2, 1024], P('col', None, 'row'), may hold values from -0.1875 to 0.1875
- cross_output: bfloat16 [1024, 1024], P('row', 'col'), may hold values from -3 to 3
- expand_weight: bfloat16 [1024, 4096], P('col', 'row'), may hold values from -0.1875 to 0.1875
- shrink_weight: bfloat16 [4096, 1024], P('row', 'col'), may hold values from -0.09375 to 0.09375
- head_bias: float32 [4, 1024], P(None, 'row'), may hold values from -2 to 2
- expand_bias: float32 [4096], P('row'), may hold values from -2 to 2
- model_bias: float32 [3, 1024], P(None, 'col'), may hold values from -2 to 2
- norm_gain: float32 [3, 1024], P(None, 'col'), may hold values from 0.5 to 1.5
- norm_shift: float32 [3, 1024], P(None, 'col'), may hold values from -1.5 to 1.5
Outputs:
- output: float32 [16384, 1024], P(('dp', 'row'), 'col')
- grad_hidden: float32 [16384, 1024], P(('dp', 'row'), 'col')
- grad_encoder: float32 [16384, 1024], P(('dp', 'row'), 'col')
- grad_self_input: float32 [1024, 3, 1024], P('col', None, 'row')
- grad_self_output: float32 [1024, 1024], P('row', 'col')
- grad_cross_query: float32 [1024, 1024], P('col', 'row')
- grad_cross_memory: float32 [1024, 2, 1024], P('col', None, 'row')
- grad_cross_output: float32 [1024, 1024], P('row', 'col')
- grad_expand: float32 [1024, 4096], P('col', 'row')
- grad_shrink: float32 [4096, 1024], P('row', 'col')
- grad_head_bias: float32 [4, 1024], P(None, 'row')
- grad_expand_bias: float32 [4096], P('row')
- grad_model_bias: float32 [3, 1024], P(None, 'col')
- grad_norm_gain: float32 [3, 1024], P(None, 'col')
- grad_norm_shift: float32 [3, 1024], P(None, 'col')
Inputs may be any that keep to these rules, and one draw needn't show every extreme that they name: `answer_length`: in every draw one sequence has 1024 live decoder tokens and one has 256. `passage_length`: in every draw one sequence has 1024 live encoder tokens and one has 256.
All inputs are finite; a program needn't handle non-finite values.
Results may differ from a plain program's by a relative error of at most 0.023.
Values may be sent and summed in bfloat16 or wider, within the bound.
No kernel may reach another device: no remote copies, remote signals or barrier semaphores. Data moves between devices by JAX's collectives and lax.ppermute only.
A program may use at most 448 MiB of HBM per device.

v0:
```python
import math

import jax
import jax.numpy as jnp
from jax import lax
from jax.sharding import PartitionSpec as P

D = 1024
HEAD_DIM = 64
SLOT = 1024
SEQ_BLK = 1


def gather_rows(values):
    return lax.all_gather(values, "row", axis=0, tiled=True)


def gather_cols(values):
    return lax.all_gather(values, "col", axis=0, tiled=True)


def multiply(row_piece, matrix, flipped):
    if flipped:
        return lax.dot_general(
            row_piece, matrix, (((1,), (1,)), ((), ())), preferred_element_type=jnp.float32
        )
    return jnp.dot(row_piece, matrix, preferred_element_type=jnp.float32)


def scatter_cols(gathered, matrix, flipped):
    return lax.psum_scatter(
        multiply(gathered, matrix, flipped), "col", scatter_dimension=0, tiled=True
    )


def scatter_rows(gathered, matrix, flipped):
    return lax.psum_scatter(
        multiply(gathered, matrix, flipped), "row", scatter_dimension=0, tiled=True
    )


def outer_sum(left, right):
    return lax.dot_general(
        left, right, (((0,), (0,)), ((), ())), preferred_element_type=jnp.float32
    )


def row_sum(values):
    return jnp.sum(values, axis=0, dtype=jnp.float32)


def column_sums(first_term, second_term):
    return lax.psum((jnp.sum(first_term, axis=-1), jnp.sum(second_term, axis=-1)), "col")


def normalize(residual, gain_row, shift_row):
    row_total, squares = column_sums(residual, residual * residual)
    center = row_total / D
    spread = squares / D - center * center
    inverse = lax.rsqrt(spread + 1e-05)
    normal = (residual - center[:, None]) * inverse[:, None]
    return (normal * gain_row + shift_row, normal, inverse)


def norm_back(upstream, normal, inverse, gain_row):
    scaled = upstream * gain_row
    plain_sum, cross_sum = column_sums(scaled, scaled * normal)
    return inverse[:, None] * (scaled - plain_sum[:, None] / D - normal * (cross_sum[:, None] / D))


def exact_gelu(values):
    return jax.nn.gelu(values, approximate=False)


def build_mask(length_limit, causal):
    places = jnp.arange(SLOT)
    allowed = jnp.broadcast_to(places[None, :] < length_limit, (SLOT, SLOT))
    if causal:
        allowed = allowed & (places[None, :] <= places[:, None])
    return allowed


def score_block(query_seq, key_seq, length_limit, causal):
    factor = 1.0 / math.sqrt(HEAD_DIM)
    scores = (
        jnp.einsum("qhd,khd->hqk", query_seq, key_seq, preferred_element_type=jnp.float32) * factor
    )
    return jnp.where(build_mask(length_limit, causal)[None], scores, -1000000000.0)


def attention_forward(query, key_rows, value_rows, lengths, causal):
    layout = (lengths.shape[0], SLOT, query.shape[1] // HEAD_DIM, HEAD_DIM)

    def single(member):
        scores = score_block(member[0], member[1], member[3], causal)
        highest = jnp.max(scores, axis=-1, keepdims=True)
        raised = jnp.exp(scores - highest)
        denominator = jnp.sum(raised, axis=-1, keepdims=True)
        weights = (raised / denominator).astype(jnp.bfloat16)
        mixture = jnp.einsum("hqk,khd->qhd", weights, member[2], preferred_element_type=jnp.float32)
        return (mixture, (highest + jnp.log(denominator))[..., 0])

    mixture, logsum = lax.map(
        single,
        (query.reshape(layout), key_rows.reshape(layout), value_rows.reshape(layout), lengths),
    )
    return (mixture.reshape(query.shape).astype(jnp.bfloat16), logsum)


def attention_backward(query, key_rows, value_rows, lengths, causal, logsum, upstream):
    layout = (lengths.shape[0], SLOT, query.shape[1] // HEAD_DIM, HEAD_DIM)
    factor = 1.0 / math.sqrt(HEAD_DIM)

    def single(member):
        query_seq, key_seq, value_seq, length_limit, logsum_seq, upstream_seq = member
        scores = score_block(query_seq, key_seq, length_limit, causal)
        weights = jnp.exp(scores - logsum_seq[..., None])
        value_grad = jnp.einsum(
            "hqk,qhd->khd",
            weights.astype(jnp.bfloat16),
            upstream_seq,
            preferred_element_type=jnp.float32,
        )
        weight_grad = jnp.einsum(
            "qhd,khd->hqk", upstream_seq, value_seq, preferred_element_type=jnp.float32
        )
        score_grad = weights * (
            weight_grad - jnp.sum(weights * weight_grad, axis=-1, keepdims=True)
        )
        score_grad = score_grad.astype(jnp.bfloat16)
        query_grad = (
            jnp.einsum("hqk,khd->qhd", score_grad, key_seq, preferred_element_type=jnp.float32)
            * factor
        )
        key_grad = (
            jnp.einsum("hqk,qhd->khd", score_grad, query_seq, preferred_element_type=jnp.float32)
            * factor
        )
        return (query_grad, key_grad, value_grad)

    gradients = lax.map(
        single,
        (
            query.reshape(layout),
            key_rows.reshape(layout),
            value_rows.reshape(layout),
            lengths,
            logsum,
            upstream.reshape(layout),
        ),
    )
    return tuple((portion.reshape(query.shape[0], -1) for portion in gradients))


def body(
    hidden,
    encoder,
    cotangent,
    answer_length,
    passage_length,
    self_input,
    self_output,
    cross_query,
    cross_memory,
    cross_output,
    expand_weight,
    shrink_weight,
    head_bias,
    expand_bias,
    model_bias,
    norm_gain,
    norm_shift,
):
    col_index = lax.axis_index("col")
    row_index = lax.axis_index("row")
    local_rows = hidden.shape[0]
    head_width = self_output.shape[0]
    model_width = self_output.shape[1]
    answers = lax.dynamic_slice_in_dim(answer_length, col_index * SEQ_BLK, SEQ_BLK)
    passages = lax.dynamic_slice_in_dim(passage_length, col_index * SEQ_BLK, SEQ_BLK)
    positions = row_index * local_rows + jnp.arange(local_rows, dtype=jnp.int32)
    matches = (positions // SLOT)[:, None] == jnp.arange(answer_length.shape[0], dtype=jnp.int32)[
        None, :
    ]
    own_length = jnp.sum(jnp.where(matches, answer_length[None, :], 0), axis=1)
    valid_rows = (positions % SLOT < own_length).astype(jnp.float32)[:, None]
    self_matrix = self_input.reshape(model_width, 3 * head_width)
    memory_matrix = cross_memory.reshape(model_width, 2 * head_width)
    gathered_x = gather_rows(hidden)
    packed = scatter_cols(gathered_x, self_matrix, False)
    query = (packed[:, :head_width] + head_bias[0]).astype(jnp.bfloat16)
    key_rows = packed[:, head_width : 2 * head_width].astype(jnp.bfloat16)
    value_rows = (packed[:, 2 * head_width :] + head_bias[1]).astype(jnp.bfloat16)
    mixture, self_logsum = attention_forward(query, key_rows, value_rows, answers, True)
    gathered_mixture = gather_cols(mixture)
    self_branch = scatter_rows(gathered_mixture, self_output, False) + model_bias[0]
    normed_one, normal_one, inverse_one = normalize(
        hidden.astype(jnp.float32) + self_branch, norm_gain[0], norm_shift[0]
    )
    first_norm = normed_one.astype(jnp.bfloat16)
    gathered_first = gather_rows(first_norm)
    cross_rows = (scatter_cols(gathered_first, cross_query, False) + head_bias[2]).astype(
        jnp.bfloat16
    )
    gathered_enc = gather_rows(encoder)
    memory = scatter_cols(gathered_enc, memory_matrix, False)
    cross_keys = memory[:, :head_width].astype(jnp.bfloat16)
    cross_values = (memory[:, head_width:] + head_bias[3]).astype(jnp.bfloat16)
    recall, cross_logsum = attention_forward(cross_rows, cross_keys, cross_values, passages, False)
    gathered_recall = gather_cols(recall)
    cross_branch = scatter_rows(gathered_recall, cross_output, False) + model_bias[1]
    normed_two, normal_two, inverse_two = normalize(
        first_norm.astype(jnp.float32) + cross_branch, norm_gain[1], norm_shift[1]
    )
    second_norm = normed_two.astype(jnp.bfloat16)
    gathered_second = gather_rows(second_norm)
    expanded = scatter_cols(gathered_second, expand_weight, False) + expand_bias
    gelu_value, gelu_pull = jax.vjp(exact_gelu, expanded)
    activated = gelu_value.astype(jnp.bfloat16)
    gathered_act = gather_cols(activated)
    shrink_branch = scatter_rows(gathered_act, shrink_weight, False) + model_bias[2]
    final_norm, normal_three, inverse_three = normalize(
        second_norm.astype(jnp.float32) + shrink_branch, norm_gain[2], norm_shift[2]
    )
    output = final_norm * valid_rows
    upstream_three = cotangent.astype(jnp.float32) * valid_rows
    resid_three_grad = norm_back(upstream_three, normal_three, inverse_three, norm_gain[2])
    shrink_rounded = resid_three_grad.astype(jnp.bfloat16)
    bias_two_part = row_sum(shrink_rounded)
    gathered_dshrink = gather_rows(shrink_rounded)
    act_grad = scatter_cols(gathered_dshrink, shrink_weight, True)
    shrink_grad = outer_sum(gathered_act, gathered_dshrink)
    expanded_grad = gelu_pull(act_grad)[0].astype(jnp.bfloat16)
    gathered_dexpand = gather_cols(expanded_grad)
    second_grad = scatter_rows(gathered_dexpand, expand_weight, True)
    expand_grad = outer_sum(gathered_second, gathered_dexpand)
    expand_bias_grad = row_sum(gathered_dexpand)
    upstream_two = resid_three_grad + second_grad
    resid_two_grad = norm_back(upstream_two, normal_two, inverse_two, norm_gain[1])
    gathered_dcross = gather_rows(resid_two_grad.astype(jnp.bfloat16))
    recall_grad = scatter_cols(gathered_dcross, cross_output, True).astype(jnp.bfloat16)
    cross_output_grad = outer_sum(gathered_recall, gathered_dcross)
    bias_one_grad = row_sum(gathered_dcross)
    crossq_grad, crossk_grad, crossv_grad = attention_backward(
        cross_rows, cross_keys, cross_values, passages, False, cross_logsum, recall_grad
    )
    gathered_dcq = gather_cols(crossq_grad.astype(jnp.bfloat16))
    first_grad = scatter_rows(gathered_dcq, cross_query, True)
    memory_rounded = jnp.concatenate([crossk_grad, crossv_grad], axis=1).astype(jnp.bfloat16)
    gathered_dmem = gather_cols(memory_rounded)
    grad_encoder = scatter_rows(gathered_dmem, memory_matrix, True)
    cross_query_grad = outer_sum(gathered_first, gathered_dcq)
    memory_grad = outer_sum(gathered_enc, gathered_dmem)
    head_two_grad = row_sum(gathered_dcq)
    head_three_grad = row_sum(gathered_dmem[:, head_width:])
    upstream_one = resid_two_grad + first_grad
    resid_one_grad = norm_back(upstream_one, normal_one, inverse_one, norm_gain[0])
    gathered_dattn = gather_rows(resid_one_grad.astype(jnp.bfloat16))
    mixture_grad = scatter_cols(gathered_dattn, self_output, True).astype(jnp.bfloat16)
    self_output_grad = outer_sum(gathered_mixture, gathered_dattn)
    bias_zero_grad = row_sum(gathered_dattn)
    query_grad, key_grad, value_grad = attention_backward(
        query, key_rows, value_rows, answers, True, self_logsum, mixture_grad
    )
    packed_grad = jnp.concatenate([query_grad, key_grad, value_grad], axis=1).astype(jnp.bfloat16)
    gathered_dpacked = gather_cols(packed_grad)
    hidden_part = scatter_rows(gathered_dpacked, self_matrix, True)
    self_input_grad = outer_sum(gathered_x, gathered_dpacked)
    head_zero_grad = row_sum(gathered_dpacked[:, :head_width])
    head_one_grad = row_sum(gathered_dpacked[:, 2 * head_width :])
    (
        self_input_grad,
        self_output_grad,
        cross_query_grad,
        memory_grad,
        cross_output_grad,
        expand_grad,
        shrink_grad,
        head_zero_grad,
        head_one_grad,
        head_two_grad,
        head_three_grad,
        expand_bias_grad,
        bias_zero_grad,
        bias_one_grad,
    ) = (
        lax.psum(self_input_grad.astype(jnp.bfloat16), "dp").astype(jnp.float32),
        lax.psum(self_output_grad.astype(jnp.bfloat16), "dp").astype(jnp.float32),
        lax.psum(cross_query_grad.astype(jnp.bfloat16), "dp").astype(jnp.float32),
        lax.psum(memory_grad.astype(jnp.bfloat16), "dp").astype(jnp.float32),
        lax.psum(cross_output_grad.astype(jnp.bfloat16), "dp").astype(jnp.float32),
        lax.psum(expand_grad.astype(jnp.bfloat16), "dp").astype(jnp.float32),
        lax.psum(shrink_grad.astype(jnp.bfloat16), "dp").astype(jnp.float32),
        lax.psum(head_zero_grad.astype(jnp.bfloat16), "dp").astype(jnp.float32),
        lax.psum(head_one_grad.astype(jnp.bfloat16), "dp").astype(jnp.float32),
        lax.psum(head_two_grad.astype(jnp.bfloat16), "dp").astype(jnp.float32),
        lax.psum(head_three_grad.astype(jnp.bfloat16), "dp").astype(jnp.float32),
        lax.psum(expand_bias_grad.astype(jnp.bfloat16), "dp").astype(jnp.float32),
        lax.psum(bias_zero_grad.astype(jnp.bfloat16), "dp").astype(jnp.float32),
        lax.psum(bias_one_grad.astype(jnp.bfloat16), "dp").astype(jnp.float32),
    )
    gain_part = jnp.stack(
        [
            jnp.sum(upstream_one * normal_one, axis=0),
            jnp.sum(upstream_two * normal_two, axis=0),
            jnp.sum(upstream_three * normal_three, axis=0),
        ]
    )
    shift_part = jnp.stack(
        [
            jnp.sum(upstream_one, axis=0),
            jnp.sum(upstream_two, axis=0),
            jnp.sum(upstream_three, axis=0),
        ]
    )
    gain_total, shift_total, bias_two_grad = lax.psum(
        (gain_part, shift_part, bias_two_part), ("dp", "row")
    )
    grad_hidden = resid_one_grad + hidden_part
    return (
        output,
        grad_hidden,
        grad_encoder,
        self_input_grad.reshape(self_input.shape),
        self_output_grad,
        cross_query_grad,
        memory_grad.reshape(cross_memory.shape),
        cross_output_grad,
        expand_grad,
        shrink_grad,
        jnp.stack([head_zero_grad, head_one_grad, head_two_grad, head_three_grad]),
        expand_bias_grad,
        jnp.stack([bias_zero_grad, bias_one_grad, bias_two_grad]),
        gain_total,
        shift_total,
    )


def solution(mesh):
    placed = (
        P(("dp", "row"), "col"),
        P(("dp", "row"), "col"),
        P(("dp", "row"), "col"),
        P("dp"),
        P("dp"),
        P("col", None, "row"),
        P("row", "col"),
        P("col", "row"),
        P("col", None, "row"),
        P("row", "col"),
        P("col", "row"),
        P("row", "col"),
        P(None, "row"),
        P("row"),
        P(None, "col"),
        P(None, "col"),
        P(None, "col"),
    )
    return jax.shard_map(
        body,
        mesh=mesh,
        in_specs=placed,
        out_specs=(
            P(("dp", "row"), "col"),
            P(("dp", "row"), "col"),
            P(("dp", "row"), "col"),
            P("col", None, "row"),
            P("row", "col"),
            P("col", "row"),
            P("col", None, "row"),
            P("row", "col"),
            P("col", "row"),
            P("row", "col"),
            P(None, "row"),
            P("row"),
            P(None, "col"),
            P(None, "col"),
            P(None, "col"),
        ),
        check_vma=False,
    )
```

profile of v0, /device:TPU:0, one launch (start us, length us, event | category | flops | bytes accessed | tf_op | source)
XLA Modules:
  0.0 4155.2 jit_solution(12830015760340592398)
XLA Ops:
  37.9 412.5 %reduce-scatter.15.cloned.1.call-done = f32[1024,1536]{1,0:T(8,128)} async-done(((f32[4096,1536]{1,0:T(8,128)}), f32[1024,1536]{1,0:T(8,128)}) %reduce-scatter.15.cloned.1.call-update) | async-done | bytes 6291472 | tf_op jit(solution)/shard_map/reduce_scatter | solution.py:31
  461.9 14.7 fusion.54
  489.8 14.6 fusion.32
  504.7 82.4 %all-gather.17.cloned.1.call-done = bf16[4096,512]{0,1:T(8,128)(2,1)} async-done(((bf16[1024,512]{0,1:T(8,128)(2,1)}), bf16[4096,512]{0,1:T(8,128)(2,1)}) %all-gather.17.cloned.1.call-update) | async-done | bytes 4194320 | tf_op jit(solution)/shard_map/all_gather | solution.py:19
  605.9 19.1 all-reduce.6
  647.8 271.7 %reduce-scatter.19.cloned.1.call-done = f32[1024,1024]{1,0:T(8,128)} async-done(((f32[4096,1024]{1,0:T(8,128)}), f32[1024,1024]{1,0:T(8,128)}) %reduce-scatter.19.cloned.1.call-update) | async-done | bytes 4194320 | tf_op jit(solution)/shard_map/reduce_scatter | solution.py:31
  929.5 137.6 %reduce-scatter.21.cloned.1.call-done = f32[1024,512]{1,0:T(8,128)} async-done(((f32[4096,512]{1,0:T(8,128)}), f32[1024,512]{1,0:T(8,128)}) %reduce-scatter.21.cloned.1.call-update) | async-done | bytes 2097168 | tf_op jit(solution)/shard_map/reduce_scatter | solution.py:31
  1072.2 15.1 fusion.55
  1115.2 81.6 %all-gather.23.cloned.1.call-done = bf16[4096,512]{0,1:T(8,128)(2,1)} async-done(((bf16[1024,512]{0,1:T(8,128)(2,1)}), bf16[4096,512]{0,1:T(8,128)(2,1)}) %all-gather.23.cloned.1.call-update) | async-done | bytes 4194320 | tf_op jit(solution)/shard_map/all_gather | solution.py:19
  1216.4 19.3 all-reduce.5
  1247.3 14.8 fusion.61
  1262.2 553.3 %reduce-scatter.25.cloned.1.call-done = f32[1024,2048]{1,0:T(8,128)} async-done(((f32[4096,2048]{1,0:T(8,128)}), f32[1024,2048]{1,0:T(8,128)}) %reduce-scatter.25.cloned.1.call-update) | async-done | bytes 8388624 | tf_op jit(solution)/shard_map/reduce_scatter | solution.py:31
  1815.5 21.0 multiply_convert_fusion.2
  1836.6 287.6 %all-gather.27.cloned.1.call-done = bf16[4096,2048]{1,0:T(8,128)(2,1)} async-done(((bf16[1024,2048]{1,0:T(8,128)(2,1)}), bf16[4096,2048]{1,0:T(8,128)(2,1)}) %all-gather.27.cloned.1.call-update) | async-done | bytes 16777232 | tf_op jit(solution)/shard_map/all_gather | solution.py:19
  2148.1 19.1 all-reduce.4
  2170.8 16.1 all-reduce.3
  2202.0 14.8 fusion.63
  2216.9 553.3 %reduce-scatter.29.cloned.1.call-done = f32[1024,2048]{1,0:T(8,128)} async-done(((f32[4096,2048]{1,0:T(8,128)}), f32[1024,2048]{1,0:T(8,128)}) %reduce-scatter.29.cloned.1.call-update) | async-done | bytes 8388624 | tf_op jit(solution)/shard_map/reduce_scatter | solution.py:31
  2782.6 287.6 %all-gather.31.cloned.1.call-done = bf16[4096,2048]{1,0:T(8,128)(2,1)} async-done(((bf16[1024,2048]{1,0:T(8,128)(2,1)}), bf16[4096,2048]{1,0:T(8,128)(2,1)}) %all-gather.31.cloned.1.call-update) | async-done | bytes 16777232 | tf_op jit(solution)/shard_map/all_gather | solution.py:19
  3097.2 19.1 all-reduce.2
  3136.3 145.5 %reduce-scatter.33.cloned.1.call-done = f32[1024,512]{1,0:T(8,128)} async-done(((f32[4096,512]{1,0:T(8,128)}), f32[1024,512]{1,0:T(8,128)}) %reduce-scatter.33.cloned.1.call-update) | async-done | bytes 2097168 | tf_op jit(solution)/shard_map/reduce_scatter | solution.py:31
  3284.1 22.4 multiply_reduce_fusion.1
  3306.5 28.2 multiply_convert_fusion.1
  3344.6 81.6 %all-gather.35.cloned.1.call-done = bf16[4096,512]{0,1:T(8,128)(2,1)} async-done(((bf16[1024,512]{0,1:T(8,128)(2,1)}), bf16[4096,512]{0,1:T(8,128)(2,1)}) %all-gather.35.cloned.1.call-update) | async-done | bytes 4194320 | tf_op jit(solution)/shard_map/all_gather | solution.py:19
  3446.8 19.1 all-reduce.1
  3513.5 118.1 %reduce-scatter.37.cloned.1.call-done = f32[1024,512]{1,0:T(8,128)} async-done(((f32[4096,512]{1,0:T(8,128)}), f32[1024,512]{1,0:T(8,128)}) %reduce-scatter.37.cloned.1.call-update) | async-done | bytes 2097168 | tf_op jit(solution)/shard_map/reduce_scatter | solution.py:31
  3633.9 22.5 multiply_reduce_fusion
  3656.3 28.5 multiply_convert_fusion
  3751.5 32.7 all-gather.41.cloned.1.call-done
  3796.5 205.6 %all-gather.39.cloned.1.call-done = bf16[4096,1536]{0,1:T(8,128)(2,1)} async-done(((bf16[1024,1536]{0,1:T(8,128)(2,1)}), bf16[4096,1536]{0,1:T(8,128)(2,1)}) %all-gather.39.cloned.1.call-update) | async-done | bytes 12582928 | tf_op jit(solution)/shard_map/all_gather | solution.py:19
  4049.0 15.4 all-reduce
  4085.1 32.5 all-reduce.11.cloned.1.call-done
  (321 shorter events, 532.4 us)
Async XLA Ops:
  7.2 2117.0 %copy-start = (bf16[2048,256]{1,0:T(8,128)(2,1)S(1)}, bf16[2048,256]{1,0:T(8,128)(2,1)}, u32[]{:S(2)}) copy-start(bf16[2048,256]{1,0:T(8,128)(2,1)} %param.28) | copy-start | bytes 3145732
  7.2 15.7 all-gather.15.cloned.1.call-start
  7.9 442.5 %reduce-scatter.15.cloned.1.call-start = ((), (), s32[]{:S(2)}) async-start(), calls=%async_computation.15 | async-start | bytes 31457280 | tf_op jit(solution)/shard_map/reduce_scatter | solution.py:31
  34.7 552.5 %all-gather.17.cloned.1.call-start = ((), (), s32[]{:S(2)}) async-start(), calls=%async_computation.16 | async-start | bytes 5242880 | tf_op jit(solution)/shard_map/all_gather | solution.py:19
  504.5 99.0 %reduce-scatter.17.cloned.1.call-start = ((), (), s32[]{:S(2)}) async-start(), calls=%async_computation.17 | async-start | bytes 6291456 | tf_op jit(solution)/shard_map/reduce_scatter | solution.py:37
  592.8 35.9 all-gather.19.cloned.1.call-start
  593.3 45.3 %all-gather.21.cloned.1.call-start = ((), (), s32[]{:S(2)}) async-start(), calls=%async_computation.20 | async-start | bytes 3145728 | tf_op jit(solution)/shard_map/all_gather | solution.py:15
  594.5 618.4 %copy-start.51 = (f32[1,256]{1,0:T(1,128)}, f32[1,256]{1,0:T(1,128)S(1)}, u32[]{:S(2)}) copy-start(f32[1,256]{1,0:T(1,128)S(1)} %get-tuple-element.193) | copy-start | bytes 3076
  605.9 607.0 %copy-start.2 = (f32[2048,256]{1,0:T(8,128)}, f32[2048,256]{1,0:T(8,128)S(1)}, u32[]{:S(2)}) copy-start(f32[2048,256]{1,0:T(8,128)S(1)} %get-tuple-element.178) | copy-start | bytes 6291460
  626.6 292.8 %reduce-scatter.19.cloned.1.call-start = ((), (), s32[]{:S(2)}) async-start(), calls=%async_computation.19 | async-start | bytes 20971520 | tf_op jit(solution)/shard_map/reduce_scatter | solution.py:31
  638.6 428.5 %reduce-scatter.21.cloned.1.call-start = ((), (), s32[]{:S(2)}) async-start(), calls=%async_computation.21 | async-start | bytes 10485760 | tf_op jit(solution)/shard_map/reduce_scatter | solution.py:31
  645.9 550.8 %all-gather.23.cloned.1.call-start = ((), (), s32[]{:S(2)}) async-start(), calls=%async_computation.22 | async-start | bytes 5242880 | tf_op jit(solution)/shard_map/all_gather | solution.py:19
  1115.1 97.8 %reduce-scatter.23.cloned.1.call-start = ((), (), s32[]{:S(2)}) async-start(), calls=%async_computation.23 | async-start | bytes 6291456 | tf_op jit(solution)/shard_map/reduce_scatter | solution.py:37
  1202.2 45.1 %all-gather.25.cloned.1.call-start = ((), (), s32[]{:S(2)}) async-start(), calls=%async_computation.24 | async-start | bytes 3145728 | tf_op jit(solution)/shard_map/all_gather | solution.py:15
  1238.4 577.1 %reduce-scatter.25.cloned.1.call-start = ((), (), s32[]{:S(2)}) async-start(), calls=%async_computation.25 | async-start | bytes 41943040 | tf_op jit(solution)/shard_map/reduce_scatter | solution.py:31
  1262.1 862.1 %all-gather.27.cloned.1.call-start = ((), (), s32[]{:S(2)}) async-start(), calls=%async_computation.26 | async-start | bytes 20971520 | tf_op jit(solution)/shard_map/all_gather | solution.py:19
  1836.6 308.2 %reduce-scatter.27.cloned.1.call-start = ((), (), s32[]{:S(2)}) async-start(), calls=%async_computation.27 | async-start | bytes 6291456 | tf_op jit(solution)/shard_map/reduce_scatter | solution.py:37
  2134.3 67.7 %all-gather.29.cloned.1.call-start = ((), (), s32[]{:S(2)}) async-start(), calls=%async_computation.28 | async-start | bytes 3145728 | tf_op jit(solution)/shard_map/all_gather | solution.py:15
  2192.8 577.5 %reduce-scatter.29.cloned.1.call-start = ((), (), s32[]{:S(2)}) async-start(), calls=%async_computation.29 | async-start | bytes 41943040 | tf_op jit(solution)/shard_map/reduce_scatter | solution.py:31
  2216.9 853.3 %all-gather.31.cloned.1.call-start = ((), (), s32[]{:S(2)}) async-start(), calls=%async_computation.30 | async-start | bytes 20971520 | tf_op jit(solution)/shard_map/all_gather | solution.py:19
  2782.5 308.2 %reduce-scatter.31.cloned.1.call-start = ((), (), s32[]{:S(2)}) async-start(), calls=%async_computation.31 | async-start | bytes 6291456 | tf_op jit(solution)/shard_map/reduce_scatter | solution.py:37
  3080.3 49.6 %all-gather.33.cloned.1.call-start = ((), (), s32[]{:S(2)}) async-start(), calls=%async_computation.32 | async-start | bytes 3145728 | tf_op jit(solution)/shard_map/all_gather | solution.py:15
  3121.0 160.8 %reduce-scatter.33.cloned.1.call-start = ((), (), s32[]{:S(2)}) async-start(), calls=%async_computation.33 | async-start | bytes 10485760 | tf_op jit(solution)/shard_map/reduce_scatter | solution.py:31
  3136.0 290.2 %all-gather.35.cloned.1.call-start = ((), (), s32[]{:S(2)}) async-start(), calls=%async_computation.34 | async-start | bytes 5242880 | tf_op jit(solution)/shard_map/all_gather | solution.py:19
  3344.6 97.9 %reduce-scatter.35.cloned.1.call-start = ((), (), s32[]{:S(2)}) async-start(), calls=%async_computation.35 | async-start | bytes 6291456 | tf_op jit(solution)/shard_map/reduce_scatter | solution.py:37
  3431.8 47.8 %all-gather.37.cloned.1.call-start = ((), (), s32[]{:S(2)}) async-start(), calls=%async_computation.36 | async-start | bytes 3145728 | tf_op jit(solution)/shard_map/all_gather | solution.py:15
  3470.7 160.9 %reduce-scatter.37.cloned.1.call-start = ((), (), s32[]{:S(2)}) async-start(), calls=%async_computation.37 | async-start | bytes 10485760 | tf_op jit(solution)/shard_map/reduce_scatter | solution.py:31
  3485.8 298.4 %all-gather.41.cloned.1.call-start = ((), (), s32[]{:S(2)}) async-start(), calls=%async_computation.40 | async-start | bytes 10485760 | tf_op jit(solution)/shard_map/all_gather | solution.py:19
  3513.0 489.1 %all-gather.39.cloned.1.call-start = ((), (), s32[]{:S(2)}) async-start(), calls=%async_computation.38 | async-start | bytes 15728640 | tf_op jit(solution)/shard_map/all_gather | solution.py:19
  3724.3 393.3 %all-reduce.11.cloned.1.call-start = ((), (), s32[]{:S(2)}) async-start(), calls=%async_computation.42 | async-start | bytes 8388608 | tf_op jit(solution)/shard_map/psum | solution.py:287
  4012.0 120.0 %reduce-scatter.39.cloned.1.call-start = ((), (), s32[]{:S(2)}) async-start(), calls=%async_computation.39 | async-start | bytes 6291456 | tf_op jit(solution)/shard_map/reduce_scatter | solution.py:37
  4023.2 125.1 %reduce-scatter.41.cloned.1.call-start = ((), (), s32[]{:S(2)}) async-start(), calls=%async_computation.41 | async-start | bytes 6291456 | tf_op jit(solution)/shard_map/reduce_scatter | solution.py:37
  (66 other events, 3193.3 us)
Sparse Core Ops, SparseCore 0:
  9.6 13.2 all-gather.14
  34.8 415.5 reduce-scatter.14
  504.6 82.5 all-gather.16
  592.9 10.5 reduce-scatter.16
  604.8 11.8 all-gather.18
  626.8 8.7 all-gather.20
  638.7 280.7 reduce-scatter.18
  921.9 145.1 reduce-scatter.20
  1115.2 81.4 all-gather.22
  1202.4 10.5 reduce-scatter.22
  1238.5 8.7 all-gather.24
  1262.3 553.2 reduce-scatter.24
  1836.7 287.4 all-gather.26
  2134.4 10.2 reduce-scatter.26
  2192.9 9.0 all-gather.28
  2217.0 553.2 reduce-scatter.28
  2782.6 287.4 all-gather.30
  3080.4 10.2 reduce-scatter.30
  3121.1 8.7 all-gather.32
  3136.1 145.6 reduce-scatter.32
  3344.7 81.4 all-gather.34
  3431.9 10.5 reduce-scatter.34
  3470.8 8.6 all-gather.36
  3485.9 145.6 reduce-scatter.36
  3633.8 150.3 all-gather.40
  3785.7 216.3 all-gather.38
  4012.1 105.4 all-reduce.10
  4119.9 12.0 reduce-scatter.38
  4135.0 13.3 reduce-scatter.40
where the time goes:
time: 4170 us; the launch traced here: 4160 us
  waiting for transfers between devices  3400 us (82%)
  matrix products  346 us (8%)
  other arithmetic  218 us (5%)
  blocking collectives  141 us (3%)
    reduce_scatter x7, waiting for transfers between devices, scatter_cols(): lax.psum_scatter(multiply(gathered, matrix, flipped), 'col', scatter_dime...  2190 us
    all_gather x7, waiting for transfers between devices, gather_cols(): return lax.all_gather(values, 'col', axis=0, tiled=True)  1060 us
    psum x6, blocking collectives, column_sums(): lax.psum((jnp.sum(first_term, axis=-1), jnp.sum(second_term, axis=-1)), '...  112 us
  transfers between devices with their start and end apart: 29, of which 27 were waited for; matrix products, arithmetic and copies ran while one was open for 6% of the time, Pallas kernels for 0%

commit v1 on v0

v1 whole, which is shorter than its diff:
```python
import math

import jax
import jax.numpy as jnp
from jax import lax
from jax.sharding import PartitionSpec as P

HEAD_DIM = 64
SLOT = 1024
BF = jnp.bfloat16
F32 = jnp.float32


def dot(left, right):
    return jnp.dot(left, right, preferred_element_type=F32)


def dot_flip(left, right):
    return lax.dot_general(left, right, (((1,), (1,)), ((), ())), preferred_element_type=F32)


def outer_sum(left, right):
    return lax.dot_general(left, right, (((0,), (0,)), ((), ())), preferred_element_type=F32)


class Plan:
    def __init__(self, mesh):
        self.n_row = mesh.shape["row"]
        self.n_col = mesh.shape["col"]
        self.n_dp = mesh.shape["dp"]
        self.share = SLOT // self.n_row
        self.row = lax.axis_index("row")
        self.col = lax.axis_index("col")
        self.pair = self.n_row == 2
        self.offset = self.row * self.share if self.pair else jnp.int32(0)
        self.positions = (jnp.arange(SLOT, dtype=jnp.int32) + self.offset) % SLOT
        self.own_positions = self.row * self.share + jnp.arange(self.share, dtype=jnp.int32)

    def swap(self, values):
        return lax.ppermute(values, "row", [(0, 1), (1, 0)])

    def gather_rows(self, values):
        if self.pair:
            return jnp.concatenate([values, self.swap(values)], axis=0)
        return lax.all_gather(values, "row", axis=0, tiled=True)

    def scatter_product(self, left, right, flipped=False):
        times = dot_flip if flipped else dot
        if self.pair:
            away = self.swap(times(left[self.share :], right))
            return times(left[: self.share], right) + away
        return lax.psum_scatter(times(left, right), "row", scatter_dimension=0, tiled=True)

    def spread(self, values):
        width = values.shape[1]
        if self.pair:
            seqs = self.n_col // 2
            parts = values.reshape(seqs, 2, self.share, width)
            keep = lax.dynamic_index_in_dim(parts, self.row, 1, keepdims=False)
            give = lax.dynamic_index_in_dim(parts, 1 - self.row, 1, keepdims=False)
            take = self.swap(give)
            first = self.row == 0
            ordered = jnp.concatenate(
                [jnp.where(first, keep, take), jnp.where(first, take, keep)], axis=0
            )
        else:
            whole = lax.all_gather(values, "row", axis=0, tiled=True)
            parts = whole.reshape(self.n_col, self.n_row, self.share, width)
            ordered = lax.dynamic_index_in_dim(parts, self.row, 1, keepdims=False)
        moved = lax.all_to_all(ordered, "col", 0, 2, tiled=True)
        return moved.reshape(self.share, width * self.n_col)

    def collect(self, values):
        width = values.shape[1] // self.n_col
        moved = lax.all_to_all(values.reshape(1, self.share, -1), "col", 2, 0, tiled=True)
        if self.pair:
            seqs = self.n_col // 2
            first = self.row == 0
            low, high = moved[:seqs], moved[seqs:]
            keep = jnp.where(first, low, high)
            take = self.swap(jnp.where(first, high, low))
            parts = jnp.stack(
                [jnp.where(first, keep, take), jnp.where(first, take, keep)], axis=1
            )
            return parts.reshape(-1, width)
        whole = lax.all_gather(moved, "row", axis=1, tiled=True).reshape(-1, width)
        rows = whole.shape[0] // self.n_row
        return lax.dynamic_slice_in_dim(whole, self.row * rows, rows, axis=0)


def normalize(residual, gain_row, shift_row):
    center = jnp.mean(residual, axis=-1, keepdims=True)
    moved = residual - center
    inverse = lax.rsqrt(jnp.mean(moved * moved, axis=-1, keepdims=True) + 1e-05)
    normal = moved * inverse
    return normal * gain_row + shift_row, normal, inverse


def norm_back(upstream, normal, inverse, gain_row):
    scaled = upstream * gain_row
    plain = jnp.mean(scaled, axis=-1, keepdims=True)
    cross = jnp.mean(scaled * normal, axis=-1, keepdims=True)
    return inverse * (scaled - plain - normal * cross)


def exact_gelu(values):
    return jax.nn.gelu(values, approximate=False)


def build_mask(positions, length, causal):
    allowed = jnp.broadcast_to(positions[None, :] < length, (SLOT, SLOT))
    if causal:
        allowed = allowed & (positions[None, :] <= positions[:, None])
    return allowed


def score_block(query, key, allowed):
    factor = 1.0 / math.sqrt(HEAD_DIM)
    scores = jnp.einsum("qhd,khd->hqk", query, key, preferred_element_type=F32) * factor
    return jnp.where(allowed[None], scores, -1000000000.0)


def split_heads(values):
    return values.reshape(SLOT, -1, HEAD_DIM)


def attention_forward(query, key, value, allowed):
    query, key, value = (split_heads(v) for v in (query, key, value))
    scores = score_block(query, key, allowed)
    highest = jnp.max(scores, axis=-1, keepdims=True)
    raised = jnp.exp(scores - highest)
    denominator = jnp.sum(raised, axis=-1, keepdims=True)
    weights = (raised / denominator).astype(BF)
    mixture = jnp.einsum("hqk,khd->qhd", weights, value, preferred_element_type=F32)
    return mixture.reshape(SLOT, -1).astype(BF), highest + jnp.log(denominator)


def attention_backward(query, key, value, allowed, logsum, upstream):
    query, key, value, upstream = (split_heads(v) for v in (query, key, value, upstream))
    factor = 1.0 / math.sqrt(HEAD_DIM)
    weights = jnp.exp(score_block(query, key, allowed) - logsum)
    value_grad = jnp.einsum("hqk,qhd->khd", weights.astype(BF), upstream, preferred_element_type=F32)
    weight_grad = jnp.einsum("qhd,khd->hqk", upstream, value, preferred_element_type=F32)
    inner = jnp.sum(weights * weight_grad, axis=-1, keepdims=True)
    score_grad = (weights * (weight_grad - inner)).astype(BF)
    query_grad = jnp.einsum("hqk,khd->qhd", score_grad, key, preferred_element_type=F32) * factor
    key_grad = jnp.einsum("hqk,qhd->khd", score_grad, query, preferred_element_type=F32) * factor
    return tuple(g.reshape(SLOT, -1).astype(BF) for g in (query_grad, key_grad, value_grad))


def gather_weight(piece, axis):
    return lax.all_gather(piece, "col", axis=axis, tiled=True)


def reduce_grad(grad, axis):
    part = lax.psum_scatter(grad.astype(BF), "col", scatter_dimension=axis, tiled=True)
    return lax.psum(part, "dp").astype(F32)


def layer(mesh):
    def body(
        hidden,
        encoder,
        cotangent,
        answer_length,
        passage_length,
        self_input,
        self_output,
        cross_query,
        cross_memory,
        cross_output,
        expand_weight,
        shrink_weight,
        head_bias,
        expand_bias,
        model_bias,
        norm_gain,
        norm_shift,
    ):
        plan = Plan(mesh)
        heads = self_output.shape[0]
        answers = lax.dynamic_index_in_dim(answer_length, plan.col, keepdims=False)
        passages = lax.dynamic_index_in_dim(passage_length, plan.col, keepdims=False)
        valid = (plan.own_positions < answers).astype(F32)[:, None]
        norms = lax.all_gather(
            jnp.concatenate([model_bias, norm_gain, norm_shift]), "col", axis=1, tiled=True
        )
        bias_rows, gain_rows, shift_rows = norms[:3], norms[3:6], norms[6:]

        own_x = plan.spread(hidden)
        w_self = gather_weight(self_input, 0).reshape(-1, 3 * heads)
        own_encoder = plan.spread(encoder)
        own_cotangent = plan.spread(cotangent)
        w_self_out = gather_weight(self_output, 1)
        w_query = gather_weight(cross_query, 0)
        w_memory = gather_weight(cross_memory, 0).reshape(-1, 2 * heads)
        w_cross_out = gather_weight(cross_output, 1)
        w_expand = gather_weight(expand_weight, 0)
        w_shrink = gather_weight(shrink_weight, 1)

        full_x = plan.gather_rows(own_x)
        packed = dot(full_x, w_self)
        query = (packed[:, :heads] + head_bias[0]).astype(BF)
        key = packed[:, heads : 2 * heads].astype(BF)
        value = (packed[:, 2 * heads :] + head_bias[1]).astype(BF)
        self_mask = build_mask(plan.positions, answers, True)
        mixture, self_logsum = attention_forward(query, key, value, self_mask)
        branch = plan.scatter_product(mixture, w_self_out) + bias_rows[0]
        normed, normal_one, inverse_one = normalize(own_x.astype(F32) + branch, gain_rows[0], shift_rows[0])
        own_first = normed.astype(BF)
        full_first = plan.gather_rows(own_first)
        cross_q = (dot(full_first, w_query) + head_bias[2]).astype(BF)
        full_encoder = plan.gather_rows(own_encoder)
        memory = dot(full_encoder, w_memory)
        cross_k = memory[:, :heads].astype(BF)
        cross_v = (memory[:, heads:] + head_bias[3]).astype(BF)
        cross_mask = build_mask(plan.positions, passages, False)
        recall, cross_logsum = attention_forward(cross_q, cross_k, cross_v, cross_mask)
        branch = plan.scatter_product(recall, w_cross_out) + bias_rows[1]
        normed, normal_two, inverse_two = normalize(own_first.astype(F32) + branch, gain_rows[1], shift_rows[1])
        own_second = normed.astype(BF)
        full_second = plan.gather_rows(own_second)
        expanded = dot(full_second, w_expand) + expand_bias
        gelu_value, gelu_pull = jax.vjp(exact_gelu, expanded)
        activated = gelu_value.astype(BF)
        branch = plan.scatter_product(activated, w_shrink) + bias_rows[2]
        normed, normal_three, inverse_three = normalize(
            own_second.astype(F32) + branch, gain_rows[2], shift_rows[2]
        )
        output = plan.collect((normed * valid).astype(BF)).astype(F32)

        up_three = own_cotangent.astype(F32) * valid
        resid_three = norm_back(up_three, normal_three, inverse_three, gain_rows[2])
        own_dshrink = resid_three.astype(BF)
        full_dshrink = plan.gather_rows(own_dshrink)
        g_shrink = reduce_grad(outer_sum(activated, full_dshrink), 1)
        d_expanded = gelu_pull(dot_flip(full_dshrink, w_shrink))[0].astype(BF)
        g_expand = reduce_grad(outer_sum(full_second, d_expanded), 0)
        up_two = resid_three + plan.scatter_product(d_expanded, w_expand, True)
        resid_two = norm_back(up_two, normal_two, inverse_two, gain_rows[1])
        own_dcross = resid_two.astype(BF)
        full_dcross = plan.gather_rows(own_dcross)
        d_recall = dot_flip(full_dcross, w_cross_out).astype(BF)
        g_cross_out = reduce_grad(outer_sum(recall, full_dcross), 1)
        d_cross_q, d_cross_k, d_cross_v = attention_backward(
            cross_q, cross_k, cross_v, cross_mask, cross_logsum, d_recall
        )
        up_one = resid_two + plan.scatter_product(d_cross_q, w_query, True)
        g_query = reduce_grad(outer_sum(full_first, d_cross_q), 0)
        d_memory = jnp.concatenate([d_cross_k, d_cross_v], axis=1)
        g_encoder = plan.collect(plan.scatter_product(d_memory, w_memory, True).astype(BF)).astype(F32)
        g_memory = reduce_grad(outer_sum(full_encoder, d_memory), 0)
        resid_one = norm_back(up_one, normal_one, inverse_one, gain_rows[0])
        own_dself = resid_one.astype(BF)
        full_dself = plan.gather_rows(own_dself)
        d_mixture = dot_flip(full_dself, w_self_out).astype(BF)
        g_self_out = reduce_grad(outer_sum(mixture, full_dself), 1)
        d_query, d_key, d_value = attention_backward(
            query, key, value, self_mask, self_logsum, d_mixture
        )
        d_packed = jnp.concatenate([d_query, d_key, d_value], axis=1)
        g_hidden = plan.collect(
            (resid_one + plan.scatter_product(d_packed, w_self, True)).astype(BF)
        ).astype(F32)
        g_self = reduce_grad(outer_sum(full_x, d_packed), 0)

        def rows_of(values):
            return jnp.sum(values, axis=0, dtype=F32)

        wide = jnp.stack(
            [rows_of(v) for v in (own_dself, own_dcross, own_dshrink)]
            + [rows_of(u * n) for u, n in ((up_one, normal_one), (up_two, normal_two), (up_three, normal_three))]
            + [rows_of(v) for v in (up_one, up_two, up_three)]
        )
        narrow = jnp.concatenate(
            [rows_of(v) for v in (d_query, d_value, d_cross_q, d_cross_v, d_expanded)]
        )
        wide = lax.psum(wide, ("dp", "row", "col"))
        narrow = lax.psum(narrow, ("dp", "col"))
        width = model_bias.shape[1]
        wide = lax.dynamic_slice_in_dim(wide, plan.col * width, width, axis=1)
        return (
            output,
            g_hidden,
            g_encoder,
            g_self.reshape(self_input.shape),
            g_self_out,
            g_query,
            g_memory.reshape(cross_memory.shape),
            g_cross_out,
            g_expand,
            g_shrink,
            narrow[: 4 * heads].reshape(4, heads),
            narrow[4 * heads :],
            wide[:3],
            wide[3:6],
            wide[6:],
        )

    return body


def solution(mesh):
    rows = P(("dp", "row"), "col")
    weights = (
        P("col", None, "row"),
        P("row", "col"),
        P("col", "row"),
        P("col", None, "row"),
        P("row", "col"),
        P("col", "row"),
        P("row", "col"),
        P(None, "row"),
        P("row"),
        P(None, "col"),
        P(None, "col"),
        P(None, "col"),
    )
    return jax.shard_map(
        layer(mesh),
        mesh=mesh,
        in_specs=(rows, rows, rows, P("dp"), P("dp")) + weights,
        out_specs=(rows, rows, rows) + weights,
        check_vma=False,
    )
```

time: 4170 us -> 1210 us (0.29)
  waiting for transfers between devices: 3400 us -> 428 us
  other arithmetic: 218 us -> 145 us
  local copies, waits for them, and re-layouts: 32.4 us -> 91.6 us
    reduce_scatter x14 -> x7, waiting for transfers between devices: 2260 us -> 225 us  [reduce_grad(): lax.psum_scatter(grad.astype(BF), 'col', scatter_dimension=axis, tiled=True)]
    all_gather x14 -> x7, waiting for transfers between devices: 1110 us -> 121 us  [gather_weight(): return lax.all_gather(piece, 'col', axis=axis, tiled=True)]
    all_to_all x0 -> x6, waiting for transfers between devices: none -> 66.5 us  [the longest x3 53.5 us: spread(): moved = lax.all_to_all(ordered, 'col', 0, 2, tiled=True)]
    convert_element_type x20 -> x16, other arithmetic: 126 us -> 71.3 us  [the longest x2 56.6 us: attention_backward(): score_grad = (weights * (weight_grad - inner)).astype(BF)]
    all_gather x0 -> x1, blocking collectives: none -> 44.8 us  [body(): lax.all_gather(jnp.concatenate([model_bias, norm_gain, norm_shift]), 'col...]
    psum x8 -> x2, blocking collectives: 141 us -> 120 us  [the longest x1 76.8 us: body(): narrow = lax.psum(narrow, ('dp', 'col'))]
    dot_general x26 -> x33, matrix products: 300 us -> 284 us  [the longest x10 61.4 us: dot(): return jnp.dot(left, right, preferred_element_type=F32)]
  transfers between devices with their start and end apart: 29 -> 41, of which waited for: 27 -> 15; matrix products, arithmetic and copies ran while one was open for 6% -> 36% of each run, Pallas kernels for 0% -> 0%
where the time goes in v1:
time: 1210 us; the launch traced here: 1200 us
  waiting for transfers between devices  428 us (35%)
  matrix products  326 us (27%)
  blocking collectives  165 us (14%)
  other arithmetic  145 us (12%)
  local copies, waits for them, and re-layouts  91.6 us (8%)
  starting transfers between devices  33.2 us (3%)
  between operations  15.6 us (1%)
    reduce_scatter x7, waiting for transfers between devices, reduce_grad(): lax.psum_scatter(grad.astype(BF), 'col', scatter_dimension=axis, tiled=True)  225 us
    all_gather x7, waiting for transfers between devices, gather_weight(): return lax.all_gather(piece, 'col', axis=axis, tiled=True)  121 us
    psum x1, blocking collectives, body(): narrow = lax.psum(narrow, ('dp', 'col'))  76.8 us
    dot_general x10, matrix products, dot(): return jnp.dot(left, right, preferred_element_type=F32)  61.4 us
    convert_element_type x2, other arithmetic, attention_backward(): score_grad = (weights * (weight_grad - inner)).astype(BF)  56.6 us
    all_to_all x3, waiting for transfers between devices, spread(): moved = lax.all_to_all(ordered, 'col', 0, 2, tiled=True)  53.5 us
    dot_general x11, matrix products, dot_flip(): lax.dot_general(left, right, (((1,), (1,)), ((), ())), preferred_element_...  49.7 us
    dot_general x2, matrix products, attention_backward(): jnp.einsum('qhd,khd->hqk', upstream, value, preferred_element_type=F32)  45 us
  transfers between devices with their start and end apart: 41, of which 15 were waited for; matrix products, arithmetic and copies ran while one was open for 36% of the time, Pallas kernels for 0%

profile of v1, /device:TPU:0, one launch (start us, length us, event | category | flops | bytes accessed | tf_op | source)
XLA Modules:
  0.0 1203.8 jit_solution(4708785778143488882)
XLA Ops:
  21.7 53.5 %all-to-all-done = bf16[4,512,256]{2,1,0:T(8,128)(2,1)S(1)} async-done(((bf16[4,512,256]{2,1,0:T(8,128)(2,1)}), bf16[4,512,256]{2,1,0:T(8,128)(2,1)S(1)}, u32[]{:S(2)}, u32[]{:S(2)}) %all-to-all-start) | async-done | bytes 1048608 | tf_op jit(solution)/shard_map/all_to_all | solution.py:70
  88.1 9.7 all-gather.8.cloned.1.call-done
  111.6 13.7 %fusion.98 = (f32[8,1024]{1,0:T(8,128)S(1)}, f32[8,1024,1024]{1,2,0:T(8,128)}) fusion(bf16[1024,8,64]{0,2,1:T(8,128)(2,1)S(1)} %bitcast.233, bf16[1024,8,64]{0,2,1:T(8,128)(2,1)S(1)} %bitcast.231, pred[1024,1024]{0,1:T(8,128)(4,1)S(1)} %compare_and_fusion), kind=kOutput, calls=%fused_computation.232 | convolution fusion | flops 1098899456 | bytes 36732928 | tf_op jit(solution)/shard_map/qhd,khd->hqk/dot_general | solution.py:119
  125.2 13.4 %fusion = f32[8,1024]{1,0:T(8,128)S(1)} fusion(f32[8,1024,1024]{1,2,0:T(8,128)} %get-tuple-element.137, f32[8,1024]{1,0:T(8,128)S(1)} %get-tuple-element.136), kind=kLoop, calls=%fused_computation.12 | loop fusion | flops 16769024 | bytes 33619968 | tf_op jit(solution)/shard_map/reduce_sum | solution.py:132
  138.7 13.9 %fusion.50 = bf16[8,64,1024]{2,1,0:T(8,128)(2,1)S(1)} fusion(bf16[1024,8,64]{0,2,1:T(8,128)(2,1)S(1)} %bitcast.259, f32[8,1024,1024]{1,2,0:T(8,128)} %get-tuple-element.137, f32[8,1024]{1,0:T(8,128)S(1)} %fusion, f32[8,1024]{1,0:T(8,128)S(1)} %get-tuple-element.136), kind=kOutput, calls=%fused_computation.131 | convolution fusion | flops 1099431936 | bytes 35717120 | tf_op jit(solution)/shard_map/hqk,khd->qhd/dot_general | solution.py:134
  166.4 44.8 %all_gather.26 = f32[9,1024]{1,0:T(8,128)S(1)} all-gather(f32[9,256]{1,0:T(8,128)S(1)} %pad_maximum_fusion.28), channel_id=1, replica_groups=mesh['dp'=4,'row'=2,'col'=4] {'col'}, dimensions={1}, use_global_device_ids=true | all-gather | bytes 46080 | tf_op jit(solution)/shard_map/all_gather | solution.py:185
  230.6 14.1 %fusion.100 = (f32[8,1024]{1,0:T(8,128)S(1)}, f32[8,1024,1024]{1,2,0:T(8,128)}) fusion(bf16[1024,8,64]{0,2,1:T(8,128)(2,1)S(1)} %bitcast.253, bf16[1024,8,64]{0,2,1:T(8,128)(2,1)S(1)} %bitcast.235, pred[1024]{0:T(1024)(128)(4,1)S(1)} %broadcast_compare_fusion), kind=kOutput, calls=%fused_computation.234 | convolution fusion | flops 1098899456 | bytes 35685376 | tf_op jit(solution)/shard_map/qhd,khd->hqk/dot_general | solution.py:119
  244.7 13.7 %fusion.1 = f32[8,1024]{1,0:T(8,128)S(1)} fusion(f32[8,1024,1024]{1,2,0:T(8,128)} %get-tuple-element.141, f32[8,1024]{1,0:T(8,128)S(1)} %get-tuple-element.140), kind=kLoop, calls=%fused_computation.13 | loop fusion | flops 16769024 | bytes 33619968 | tf_op jit(solution)/shard_map/reduce_sum | solution.py:132
  258.4 13.8 %fusion.49 = bf16[8,64,1024]{2,1,0:T(8,128)(2,1)S(1)} fusion(bf16[1024,8,64]{0,2,1:T(8,128)(2,1)S(1)} %bitcast.261, f32[8,1024,1024]{1,2,0:T(8,128)} %get-tuple-element.141, f32[8,1024]{1,0:T(8,128)S(1)} %fusion.1, f32[8,1024]{1,0:T(8,128)S(1)} %get-tuple-element.140), kind=kOutput, calls=%fused_computation.130 | convolution fusion | flops 1099431936 | bytes 35717120 | tf_op jit(solution)/shard_map/hqk,khd->qhd/dot_general | solution.py:134
  290.9 58.0 %all-gather.18.cloned.1.call-done = bf16[1024,2048]{1,0:T(8,128)(2,1)} async-done(((bf16[256,2048]{1,0:T(8,128)(2,1)}), bf16[1024,2048]{1,0:T(8,128)(2,1)}) %all-gather.18.cloned.1.call-update) | async-done | bytes 4194320 | tf_op jit(solution)/shard_map/all_gather | solution.py:152
  348.9 27.8 %multiply_convert_fusion.2 = (bf16[1024,2048]{1,0:T(8,128)(2,1)}, f32[1024,2048]{1,0:T(8,128)}, f32[1024,2048]{1,0:T(8,128)}) fusion(f32[2048]{0:T(1024)S(1)} %copy-done.86, bf16[1024,2048]{1,0:T(8,128)(2,1)} %all-gather.18.cloned.1.call-done, bf16[512,1024]{1,0:T(8,128)(2,1)} %collective-permute-done.7, bf16[512,1024]{1,0:T(8,128)(2,1)} %add_convert_fusion.3), kind=kOutput, calls=%fused_computation.26 | convolution fusion | flops 4437573632 | bytes 27271168 | tf_op jit(solution)/shard_map/dot_general | solution.py:15
  376.8 52.7 %all-gather.20.cloned.1.call-done = bf16[2048,1024]{1,0:T(8,128)(2,1)} async-done(((bf16[2048,256]{1,0:T(8,128)(2,1)}), bf16[2048,1024]{1,0:T(8,128)(2,1)}) %all-gather.20.cloned.1.call-update) | async-done | bytes 4194320 | tf_op jit(solution)/shard_map/all_gather | solution.py:152
  452.0 14.6 %convert_reduce_fusion = (f32[2048]{0:T(1024)}, bf16[1024,2048]{1,0:T(8,128)(2,1)}) fusion(f32[1024,2048]{1,0:T(8,128)} %get-tuple-element.89, bf16[2048,1024]{1,0:T(8,128)(2,1)S(1)} %copy-done.82, bf16[512,1024]{1,0:T(8,128)(2,1)S(1)} %collective-permute-done.11, bf16[512,1024]{1,0:T(8,128)(2,1)S(1)} %get-tuple-element.80, ...), kind=kOutput, calls=%fused_computation.24 | convolution fusion | flops 4334811136 | bytes 27279360 | tf_op jit(solution)/shard_map/dot_general | solution.py:19
  485.3 22.1 %multiply_reduce_fusion.1 = (f32[8,1024]{1,0:T(8,128)S(1)}, f32[8,1024,1024]{1,2,0:T(8,128)}) fusion(f32[8,1024,1024]{1,2,0:T(8,128)} %get-tuple-element.141, f32[8,1024]{1,0:T(8,128)S(1)} %log_add_fusion.1, bf16[1024,8,64]{0,2,1:T(8,128)(2,1)S(1)} %bitcast.255, bf16[1024,8,64]{0,2,1:T(8,128)(2,1)S(1)} %bitcast.262), kind=kOutput, calls=%fused_computation.4 | convolution fusion | flops 1098899456 | bytes 69271552 | tf_op jit(solution)/shard_map/qhd,khd->hqk/dot_general | solution.py:143
  507.4 28.2 %multiply_convert_fusion.1 = bf16[8,1024,1024]{1,2,0:T(8,128)(2,1)} fusion(f32[8,1024,1024]{1,2,0:T(8,128)} %get-tuple-element.149, f32[8,1024,1024]{1,2,0:T(8,128)} %get-tuple-element.141, f32[8,1024]{1,0:T(8,128)S(1)} %get-tuple-element.148, f32[8,1024]{1,0:T(8,128)S(1)} %log_add_fusion.1), kind=kLoop, calls=%fused_computation.3 | loop fusion | flops 33554432 | bytes 83951616 | tf_op jit(solution)/shard_map/convert_element_type | solution.py:145
  535.6 9.5 convert_reduce_fusion.5
  548.6 14.8 %convert_reduce_fusion.4 = (f32[8,64]{1,0:T(8,128)S(1)}, bf16[8,64,1024]{2,1,0:T(8,128)(2,1)}) fusion(bf16[1024,8,64]{0,2,1:T(8,128)(2,1)S(1)} %bitcast.256, f32[8,1024,1024]{1,2,0:T(8,128)} %get-tuple-element.141, f32[8,1024]{1,0:T(8,128)S(1)} %log_add_fusion.1), kind=kOutput, calls=%fused_computation.85 | convolution fusion | flops 1092091392 | bytes 35686400 | tf_op jit(solution)/shard_map/hqk,qhd->khd/dot_general | solution.py:142
  570.3 12.0 multiply_convert_fusion.3
  591.0 22.9 %multiply_reduce_fusion = (f32[8,1024]{1,0:T(8,128)S(1)}, f32[8,1024,1024]{1,2,0:T(8,128)}) fusion(f32[8,1024,1024]{1,2,0:T(8,128)} %get-tuple-element.137, f32[8,1024]{1,0:T(8,128)S(1)} %log_add_fusion, bf16[1024,8,64]{0,2,1:T(8,128)(2,1)S(1)} %bitcast.257, bf16[1024,8,64]{0,2,1:T(8,128)(2,1)S(1)} %bitcast.260), kind=kOutput, calls=%fused_computation.1 | convolution fusion | flops 1098899456 | bytes 69271552 | tf_op jit(solution)/shard_map/qhd,khd->hqk/dot_general | solution.py:143
  613.8 28.5 %multiply_convert_fusion = bf16[8,1024,1024]{1,2,0:T(8,128)(2,1)} fusion(f32[8,1024,1024]{1,2,0:T(8,128)} %get-tuple-element.152, f32[8,1024,1024]{1,2,0:T(8,128)} %get-tuple-element.137, f32[8,1024]{1,0:T(8,128)S(1)} %get-tuple-element.151, f32[8,1024]{1,0:T(8,128)S(1)} %log_add_fusion), kind=kLoop, calls=%fused_computation | loop fusion | flops 33554432 | bytes 83951616 | tf_op jit(solution)/shard_map/convert_element_type | solution.py:145
  642.3 12.0 multiply_convert_fusion.4
  654.3 8.9 convert_reduce_fusion.7
  663.2 15.0 %convert_reduce_fusion.6 = (f32[8,64]{1,0:T(8,128)S(1)}, bf16[8,64,1024]{2,1,0:T(8,128)(2,1)}) fusion(bf16[1024,8,64]{0,2,1:T(8,128)(2,1)S(1)} %bitcast.258, f32[8,1024,1024]{1,2,0:T(8,128)} %get-tuple-element.137, f32[8,1024]{1,0:T(8,128)S(1)} %log_add_fusion), kind=kOutput, calls=%fused_computation.87 | convolution fusion | flops 1092091392 | bytes 35686400 | tf_op jit(solution)/shard_map/hqk,qhd->khd/dot_general | solution.py:142
  698.1 8.4 convolution_convert_fusion.1
  706.9 9.4 convolution_convert_fusion.2
  764.1 13.0 %all-to-all-done.2 = bf16[4,2,65536]{2,1,0:T(2,128)(2,1)S(1)} async-done(((bf16[4,2,65536]{2,1,0:T(2,128)(2,1)}), bf16[4,2,65536]{2,1,0:T(2,128)(2,1)S(1)}, u32[]{:S(2)}, u32[]{:S(2)}) %all-to-all-start.2) | async-done | bytes 1048608 | tf_op jit(solution)/shard_map/all_to_all | solution.py:75
  786.0 38.4 %reduce-scatter.12.cloned.1.call-done = bf16[256,512]{1,0:T(8,128)(2,1)} async-done(((bf16[1024,512]{1,0:T(8,128)(2,1)}), bf16[256,512]{1,0:T(8,128)(2,1)}) %reduce-scatter.12.cloned.1.call-update) | async-done | bytes 262160 | tf_op jit(solution)/shard_map/reduce_scatter | solution.py:156
  824.3 28.9 %reduce-scatter.10.cloned.1.call-done = bf16[512,256]{1,0:T(8,128)(2,1)} async-done(((bf16[512,1024]{1,0:T(8,128)(2,1)}), bf16[512,256]{1,0:T(8,128)(2,1)}) %reduce-scatter.10.cloned.1.call-update) | async-done | bytes 262160 | tf_op jit(solution)/shard_map/reduce_scatter | solution.py:156
  853.2 77.7 %reduce-scatter.20.cloned.1.call-done = bf16[2048,256]{1,0:T(8,128)(2,1)} async-done(((bf16[2048,1024]{1,0:T(8,128)(2,1)}), bf16[2048,256]{1,0:T(8,128)(2,1)}) %reduce-scatter.20.cloned.1.call-update) | async-done | bytes 1048592 | tf_op jit(solution)/shard_map/reduce_scatter | solution.py:156
  931.0 79.5 %reduce-scatter.18.cloned.1.call-done = bf16[256,2048]{1,0:T(8,128)(2,1)} async-done(((bf16[1024,2048]{1,0:T(8,128)(2,1)}), bf16[256,2048]{1,0:T(8,128)(2,1)}) %reduce-scatter.18.cloned.1.call-update) | async-done | bytes 1048592 | tf_op jit(solution)/shard_map/reduce_scatter | solution.py:156
  1045.2 43.5 %psum.71 = f32[9,1024]{1,0:T(8,128)S(1)} all-reduce(f32[9,1024]{1,0:T(8,128)S(1)} %stack.75), channel_id=1, replica_groups=mesh['dp'=4,'row'=2,'col'=4] {'dp','row','col'}, use_global_device_ids=true, to_apply=%region_47.48 | all-reduce | flops 9216 | bytes 73728 | tf_op jit(solution)/shard_map/psum | solution.py:278
  1093.3 76.8 %psum.70 = f32[4096]{0:T(1024)S(1)} all-reduce(f32[4096]{0:T(1024)S(1)} %constant_dynamic-update-slice_fusion.4), channel_id=1, replica_groups=mesh['dp'=4,'row'=2,'col'=4] {'dp','col'}, use_global_device_ids=true, to_apply=%region_37.38 | all-reduce | flops 4096 | bytes 32768 | tf_op jit(solution)/shard_map/psum | solution.py:279
  (419 shorter events, 295.1 us)
Async XLA Ops:
  7.2 90.6 %all-gather.8.cloned.1.call-start = ((), (), s32[]{:S(2)}) async-start(), calls=%async_computation.13 | async-start | bytes 3932160 | tf_op jit(solution)/shard_map/all_gather | solution.py:152
  14.6 60.6 %all-to-all-start = ((bf16[4,512,256]{2,1,0:T(8,128)(2,1)}), bf16[4,512,256]{2,1,0:T(8,128)(2,1)S(1)}, u32[]{:S(2)}, u32[]{:S(2)}) async-start(bf16[4,512,256]{2,1,0:T(8,128)(2,1)} %copy.106), calls=%async_computation | async-start | bytes 2097152 | tf_op jit(solution)/shard_map/all_to_all | solution.py:70
  21.0 133.5 %all-gather.10.cloned.1.call-start = ((), (), s32[]{:S(2)}) async-start(), calls=%async_computation.14 | async-start | bytes 1310720 | tf_op jit(solution)/shard_map/all_gather | solution.py:152
  21.7 198.4 %all-gather.12.cloned.1.call-start = ((), (), s32[]{:S(2)}) async-start(), calls=%async_computation.15 | async-start | bytes 2621440 | tf_op jit(solution)/shard_map/all_gather | solution.py:152
  76.3 9.5 collective-permute-start.1
  78.3 80.0 %collective-permute-start.3 = (bf16[2,512,256]{1,2,0:T(8,128)(2,1)}, bf16[2,512,256]{1,2,0:T(8,128)(2,1)}, u32[]{:S(2)}, u32[]{:S(2)}) collective-permute-start(bf16[2,512,256]{1,2,0:T(8,128)(2,1)} %bitcast.20), channel_id=1, source_target_pairs={{0,4},{4,0},{1,5},{5,1},{2,6},{6,2},{3,7},{7,3},{8,12},{12,8},{9,1... | collective-permute-start | bytes 1572872 | tf_op jit(solution)/shard_map/ppermute | solution.py:40
  81.8 76.4 %collective-permute-start.10 = (bf16[2,512,256]{1,2,0:T(8,128)(2,1)}, bf16[2,512,256]{1,2,0:T(8,128)(2,1)}, u32[]{:S(2)}, u32[]{:S(2)}) collective-permute-start(bf16[2,512,256]{1,2,0:T(8,128)(2,1)} %bitcast.50), channel_id=1, source_target_pairs={{0,4},{4,0},{1,5},{5,1},{2,6},{6,2},{3,7},{7,3},{8,12},{12,8},{9,1... | collective-permute-start | bytes 1572872 | tf_op jit(solution)/shard_map/ppermute | solution.py:40
  81.9 145.3 %all-gather.14.cloned.1.call-start = ((), (), s32[]{:S(2)}) async-start(), calls=%async_computation.16 | async-start | bytes 1310720 | tf_op jit(solution)/shard_map/all_gather | solution.py:152
  157.7 56.0 %collective-permute-start.2 = (f32[512,1024]{1,0:T(8,128)}, f32[512,1024]{1,0:T(8,128)}, u32[]{:S(2)}, u32[]{:S(2)}) collective-permute-start(f32[512,1024]{1,0:T(8,128)} %fusion.104), channel_id=1, source_target_pairs={{0,4},{4,0},{1,5},{5,1},{2,6},{6,2},{3,7},{7,3},{8,12},{12,8},{9,1... | collective-permute-start | bytes 6291464 | tf_op jit(solution)/shard_map/ppermute | solution.py:40
  162.0 50.5 %all-to-all-start.1 = ((bf16[4,512,256]{2,1,0:T(8,128)(2,1)}), bf16[4,512,256]{2,1,0:T(8,128)(2,1)S(1)}, u32[]{:S(2)}, u32[]{:S(2)}) async-start(bf16[4,512,256]{2,1,0:T(8,128)(2,1)} %copy.115), calls=%async_computation.1 | async-start | bytes 2097152 | tf_op jit(solution)/shard_map/all_to_all | solution.py:70
  165.8 108.3 %all-gather.16.cloned.1.call-start = ((), (), s32[]{:S(2)}) async-start(), calls=%async_computation.17 | async-start | bytes 1310720 | tf_op jit(solution)/shard_map/all_gather | solution.py:152
  166.3 182.6 %all-gather.18.cloned.1.call-start = ((), (), s32[]{:S(2)}) async-start(), calls=%async_computation.18 | async-start | bytes 5242880 | tf_op jit(solution)/shard_map/all_gather | solution.py:152
  218.8 210.7 %all-gather.20.cloned.1.call-start = ((), (), s32[]{:S(2)}) async-start(), calls=%async_computation.19 | async-start | bytes 5242880 | tf_op jit(solution)/shard_map/all_gather | solution.py:152
  283.1 65.8 %collective-permute-start.7 = (bf16[512,1024]{1,0:T(8,128)(2,1)}, bf16[512,1024]{1,0:T(8,128)(2,1)}, u32[]{:S(2)}, u32[]{:S(2)}) collective-permute-start(bf16[512,1024]{1,0:T(8,128)(2,1)} %add_convert_fusion.3), channel_id=1, source_target_pairs={{0,4},{4,0},{1,5},{5,1},{2,6},{6,2},{3,7},{7,3},{8,12},{12,8},{9,1... | collective-permute-start | bytes 3145736 | tf_op jit(solution)/shard_map/ppermute | solution.py:40
  285.9 150.7 %all-to-all-start.3 = ((bf16[4,512,256]{2,1,0:T(8,128)(2,1)}), bf16[4,512,256]{2,1,0:T(8,128)(2,1)S(1)}, u32[]{:S(2)}, u32[]{:S(2)}) async-start(bf16[4,512,256]{2,1,0:T(8,128)(2,1)} %copy.122), calls=%async_computation.3 | async-start | bytes 2097152 | tf_op jit(solution)/shard_map/all_to_all | solution.py:70
  290.9 490.5 %reduce-scatter.14.cloned.1.call-start = ((), (), s32[]{:S(2)}) async-start(), calls=%async_computation.23 | async-start | bytes 2621440 | tf_op jit(solution)/shard_map/reduce_scatter | solution.py:156
  548.2 15.2 %collective-permute-start.14 = (f32[512,1024]{1,0:T(8,128)}, f32[512,1024]{1,0:T(8,128)}, u32[]{:S(2)}, u32[]{:S(2)}) collective-permute-start(f32[512,1024]{1,0:T(8,128)} %fusion.106), channel_id=1, source_target_pairs={{0,4},{4,0},{1,5},{5,1},{2,6},{6,2},{3,7},{7,3},{8,12},{12,8},{9,1... | collective-permute-start | bytes 6291464 | tf_op jit(solution)/shard_map/ppermute | solution.py:40
  570.1 17.9 %collective-permute-start.15 = (bf16[512,1024]{1,0:T(8,128)(2,1)}, bf16[512,1024]{1,0:T(8,128)(2,1)}, u32[]{:S(2)}, u32[]{:S(2)}) collective-permute-start(bf16[512,1024]{1,0:T(8,128)(2,1)} %get-tuple-element.86), channel_id=1, source_target_pairs={{0,4},{4,0},{1,5},{5,1},{2,6},{6,2},{3,7},{7,3},{8,12},{12,8},{9,1... | collective-permute-start | bytes 3145736 | tf_op jit(solution)/shard_map/ppermute | solution.py:40
  588.0 195.7 %reduce-scatter.8.cloned.1.call-start = ((), (), s32[]{:S(2)}) async-start(), calls=%async_computation.20 | async-start | bytes 3932160 | tf_op jit(solution)/shard_map/reduce_scatter | solution.py:156
  685.2 100.8 %reduce-scatter.16.cloned.1.call-start = ((), (), s32[]{:S(2)}) async-start(), calls=%async_computation.24 | async-start | bytes 1310720 | tf_op jit(solution)/shard_map/reduce_scatter | solution.py:156
  690.3 134.0 %reduce-scatter.12.cloned.1.call-start = ((), (), s32[]{:S(2)}) async-start(), calls=%async_computation.22 | async-start | bytes 1310720 | tf_op jit(solution)/shard_map/reduce_scatter | solution.py:156
  694.0 159.2 %reduce-scatter.10.cloned.1.call-start = ((), (), s32[]{:S(2)}) async-start(), calls=%async_computation.21 | async-start | bytes 1310720 | tf_op jit(solution)/shard_map/reduce_scatter | solution.py:156
  698.1 232.9 %reduce-scatter.20.cloned.1.call-start = ((), (), s32[]{:S(2)}) async-start(), calls=%async_computation.26 | async-start | bytes 5242880 | tf_op jit(solution)/shard_map/reduce_scatter | solution.py:156
  706.6 303.9 %reduce-scatter.18.cloned.1.call-start = ((), (), s32[]{:S(2)}) async-start(), calls=%async_computation.25 | async-start | bytes 5242880 | tf_op jit(solution)/shard_map/reduce_scatter | solution.py:156
  721.8 21.5 %collective-permute-start.18 = (f32[512,1024]{1,0:T(8,128)}, f32[512,1024]{1,0:T(8,128)}, u32[]{:S(2)}, u32[]{:S(2)}) collective-permute-start(f32[512,1024]{1,0:T(8,128)} %fusion.64), channel_id=1, source_target_pairs={{0,4},{4,0},{1,5},{5,1},{2,6},{6,2},{3,7},{7,3},{8,12},{12,8},{9,1... | collective-permute-start | bytes 6291464 | tf_op jit(solution)/shard_map/ppermute | solution.py:40
  733.6 43.5 %all-to-all-start.2 = ((bf16[4,2,65536]{2,1,0:T(2,128)(2,1)}), bf16[4,2,65536]{2,1,0:T(2,128)(2,1)S(1)}, u32[]{:S(2)}, u32[]{:S(2)}) async-start(bf16[4,2,65536]{2,1,0:T(2,128)(2,1)} %reshape.403), calls=%async_computation.2 | async-start | bytes 2097152 | tf_op jit(solution)/shard_map/all_to_all | solution.py:75
  743.0 271.5 %collective-permute-start.16 = (f32[512,1024]{1,0:T(8,128)}, f32[512,1024]{1,0:T(8,128)}, u32[]{:S(2)}, u32[]{:S(2)}) collective-permute-start(f32[512,1024]{1,0:T(8,128)} %fusion.35), channel_id=1, source_target_pairs={{0,4},{4,0},{1,5},{5,1},{2,6},{6,2},{3,7},{7,3},{8,12},{12,8},{9,1... | collective-permute-start | bytes 6291464 | tf_op jit(solution)/shard_map/ppermute | solution.py:40
  777.1 260.3 %all-to-all-start.5 = ((bf16[4,2,65536]{2,1,0:T(2,128)(2,1)}), bf16[4,2,65536]{2,1,0:T(2,128)(2,1)}, u32[]{:S(2)}, u32[]{:S(2)}) async-start(bf16[4,2,65536]{2,1,0:T(2,128)(2,1)} %reshape.407), calls=%async_computation.5 | async-start | bytes 2097152 | tf_op jit(solution)/shard_map/all_to_all | solution.py:75
  781.4 403.2 %all-reduce.3.cloned.1.call-start = ((), (), s32[]{:S(2)}) async-start(), calls=%async_computation.27 | async-start | bytes 8388608 | tf_op jit(solution)/shard_map/psum | solution.py:157
  1014.5 27.2 %collective-permute-start.9 = (bf16[2,512,256]{1,2,0:T(8,128)(2,1)}, bf16[2,512,256]{1,2,0:T(8,128)(2,1)}, u32[]{:S(2)}, u32[]{:S(2)}) collective-permute-start(bf16[2,512,256]{1,2,0:T(8,128)(2,1)} %select_bitcast_fusion.2), channel_id=1, source_target_pairs={{0,4},{4,0},{1,5},{5,1},{2,6},{6,2},{3,7},{7,3},{8,12},{12,8},{9,1... | collective-permute-start | bytes 1572872 | tf_op jit(solution)/shard_map/ppermute | solution.py:40
  1037.4 132.7 %all-to-all-start.4 = ((bf16[4,2,65536]{2,1,0:T(2,128)(2,1)}), bf16[4,2,65536]{2,1,0:T(2,128)(2,1)}, u32[]{:S(2)}, u32[]{:S(2)}) async-start(bf16[4,2,65536]{2,1,0:T(2,128)(2,1)} %reshape.405), calls=%async_computation.4 | async-start | bytes 2097152 | tf_op jit(solution)/shard_map/all_to_all | solution.py:75
  1093.3 84.7 %collective-permute-start.19 = (bf16[2,512,256]{1,2,0:T(8,128)(2,1)}, bf16[2,512,256]{1,2,0:T(8,128)(2,1)S(1)}, u32[]{:S(2)}, u32[]{:S(2)}) collective-permute-start(bf16[2,512,256]{1,2,0:T(8,128)(2,1)} %select_bitcast_fusion), channel_id=1, source_target_pairs={{0,4},{4,0},{1,5},{5,1},{2,6},{6,2},{3,7},{7,3},{8,12},{12,8},{9,1... | collective-permute-start | bytes 1572872 | tf_op jit(solution)/shard_map/ppermute | solution.py:40
  (100 other events, 1188.1 us)
Sparse Core Ops, SparseCore 0:
  10.1 87.6 all-gather.7
  99.4 30.2 all-gather.9
  131.3 52.6 all-gather.11
  185.4 30.5 all-gather.13
  217.4 28.7 all-gather.15
  247.6 101.3 all-gather.17
  350.5 78.9 all-gather.19
  588.1 42.0 reduce-scatter.13
  685.3 58.4 reduce-scatter.7
  746.0 37.0 reduce-scatter.15
  785.4 38.9 reduce-scatter.11
  826.6 26.6 reduce-scatter.9
  855.5 75.4 reduce-scatter.19
  933.2 77.2 reduce-scatter.17
  1015.4 107.9 all-reduce.2

commit v2 on v1

v2 whole, which is shorter than its diff:
```python
import functools
import math

import jax
import jax.numpy as jnp
from jax import lax
from jax.experimental import pallas as pl
from jax.experimental.pallas import tpu as pltpu
from jax.sharding import PartitionSpec as P

HEAD_DIM = 64
SLOT = 1024
BF = jnp.bfloat16
F32 = jnp.float32


def tie(*values):
    return lax.optimization_barrier(values)


def dot(left, right):
    return jnp.dot(left, right, preferred_element_type=F32)


def dot_flip(left, right):
    return lax.dot_general(left, right, (((1,), (1,)), ((), ())), preferred_element_type=F32)


def outer_sum(left, right):
    return lax.dot_general(left, right, (((0,), (0,)), ((), ())), preferred_element_type=F32)

def in_vmem(body, name, scalars, arrays, outs):
    count = len(arrays)

    def kernel(info, *refs):
        body(info, refs[:count], refs[count:])

    def spec(shape):
        return pl.BlockSpec(shape, lambda i, info: (0,) * len(shape))

    return pl.pallas_call(
        kernel,
        out_shape=outs,
        grid_spec=pltpu.PrefetchScalarGridSpec(
            num_scalar_prefetch=1,
            grid=(1,),
            in_specs=[spec(a.shape) for a in arrays],
            out_specs=[spec(o.shape) for o in outs],
        ),
        compiler_params=pltpu.CompilerParams(vmem_limit_bytes=56 * 2**20),
        cost_estimate=small_cost(),
        name=name,
    )(scalars, *arrays)


def lanes_at(start):
    return pl.ds(pl.multiple_of(start, 128), 128)


def join_columns(pieces, places):
    rows, width = pieces[0].shape

    def body(info, ins, outs):
        for i, piece in enumerate(ins):
            start = pl.multiple_of(info[i] * width, width)
            outs[0][:, pl.ds(start, width)] = piece[...]

    out = jax.ShapeDtypeStruct((rows, width * len(pieces)), pieces[0].dtype)
    return in_vmem(body, "join_columns", jnp.stack(places), pieces, [out])[0]


def join_rows(pieces, places):
    rows, width = pieces[0].shape

    def body(info, ins, outs):
        for i, piece in enumerate(ins):
            start = pl.multiple_of(info[i] * rows, rows)
            outs[0][pl.ds(start, rows), :] = piece[...].astype(F32)

    out = jax.ShapeDtypeStruct((rows * len(pieces), width), F32)
    return in_vmem(body, "join_rows", jnp.stack(places), pieces, [out])[0]


def sum_blocks(terms, axis, n_col, col):
    shape = terms[0].shape
    width = shape[axis] // n_col
    block = (shape[0], width) if axis == 1 else (width, shape[1])

    def body(info, ins, outs):
        for owner in range(n_col):
            start = pl.multiple_of(lax.rem(info[0] - owner + n_col, n_col) * width, width)
            at = (slice(None), pl.ds(start, width)) if axis == 1 else (pl.ds(start, width), slice(None))
            outs[0][owner] = sum(t[at].astype(F32) for t in ins).astype(BF)

    out = jax.ShapeDtypeStruct((n_col, *block), BF)
    return in_vmem(body, "sum_blocks", col[None], terms, [out])[0]


class Plan:
    def __init__(self, mesh):
        self.n_row = mesh.shape["row"]
        self.n_col = mesh.shape["col"]
        self.share = SLOT // self.n_row
        self.row = lax.axis_index("row")
        self.col = lax.axis_index("col")
        self.pair = self.n_row == 2
        self.offset = self.row * self.share if self.pair else jnp.int32(0)
        self.positions = (jnp.arange(SLOT, dtype=jnp.int32) + self.offset) % SLOT
        self.own_positions = self.row * self.share + jnp.arange(self.share, dtype=jnp.int32)

    def swap(self, values):
        return lax.ppermute(values, "row", [(0, 1), (1, 0)])

    def shift(self, values, k):
        n = self.n_col
        return lax.ppermute(values, "col", [(i, (i + k) % n) for i in range(n)])

    def block(self, other):
        return (self.col - other) % self.n_col

    def reorder(self, blocks):
        return jnp.stack(
            [lax.dynamic_index_in_dim(blocks, self.block(i), 0, keepdims=False) for i in range(self.n_col)]
        )

    def gather_rows(self, values):
        if self.pair:
            return jnp.concatenate([values, self.swap(values)], axis=0)
        return lax.all_gather(values, "row", axis=0, tiled=True)

    def scatter_product(self, left, right, flipped=False):
        times = dot_flip if flipped else dot
        if self.pair:
            away = self.swap(times(left[self.share :], right))
            return times(left[: self.share], right) + away
        return lax.psum_scatter(times(left, right), "row", scatter_dimension=0, tiled=True)

    def turn(self, t, back=False):
        pairs = []
        for r in range(2):
            for z in range(self.n_col):
                h, j = divmod(z ^ t, 2)
                pairs.append((r * self.n_col + z, h * self.n_col + 2 * r + j))
        return [(b, a) for a, b in pairs] if back else pairs

    def spread(self, values):
        width = values.shape[1]
        if self.pair and self.n_col == 4:
            parts = values.reshape(4, self.share, width)
            takes = []
            for t in range(4):
                h, j = (self.col ^ t) // 2, (self.col ^ t) % 2
                give = lax.dynamic_index_in_dim(parts, 2 * j + h, 0, keepdims=False)
                takes.append(lax.ppermute(give, ("row", "col"), self.turn(t)))
            return tuple(takes)
        whole = lax.all_gather(values, "row", axis=0, tiled=True)
        parts = whole.reshape(self.n_col, self.n_row, self.share, width)
        ordered = lax.dynamic_index_in_dim(parts, self.row, 1, keepdims=False)
        moved = self.reorder(lax.all_to_all(ordered, "col", 0, 0, tiled=True))
        return (jnp.transpose(moved, (1, 0, 2)).reshape(self.share, -1),)

    def spread_end(self, takes):
        if len(takes) == 1:
            return takes[0]
        seen = 2 * self.row + self.col % 2
        return join_columns(takes, [self.block(t ^ seen) for t in range(4)])

    def collect(self, values):
        width = values.shape[1] // self.n_col
        if self.pair and self.n_col == 4:
            seen = 2 * self.row + self.col % 2
            takes = []
            for t in range(4):
                give = lax.dynamic_slice_in_dim(values, self.block(t ^ seen) * width, width, axis=1)
                takes.append(lax.ppermute(give, ("row", "col"), self.turn(t, back=True)))
            return tuple(takes)
        blocks = jnp.transpose(values.reshape(self.share, self.n_col, width), (1, 0, 2))
        moved = lax.all_to_all(self.reorder(blocks), "col", 0, 0, tiled=True)
        whole = lax.all_gather(moved, "row", axis=1, tiled=True).reshape(-1, width)
        rows = whole.shape[0] // self.n_row
        return (lax.dynamic_slice_in_dim(whole, self.row * rows, rows, axis=0),)

    def collect_end(self, takes):
        if len(takes) == 1:
            return takes[0].astype(F32)
        places = [2 * ((self.col ^ t) % 2) + (self.col ^ t) // 2 for t in range(4)]
        return join_rows(takes, places)


def normalize(residual, gain_row, shift_row):
    center = jnp.mean(residual, axis=-1, keepdims=True)
    moved = residual - center
    inverse = lax.rsqrt(jnp.mean(moved * moved, axis=-1, keepdims=True) + 1e-05)
    normal = moved * inverse
    return normal * gain_row + shift_row, normal, inverse


def norm_back(upstream, normal, inverse, gain_row):
    scaled = upstream * gain_row
    plain = jnp.mean(scaled, axis=-1, keepdims=True)
    cross = jnp.mean(scaled * normal, axis=-1, keepdims=True)
    return inverse * (scaled - plain - normal * cross)


def gelu_and_slope(values):
    cdf = 0.5 + 0.5 * lax.erf(values * math.sqrt(0.5))
    density = jnp.exp(-0.5 * values * values) * (1.0 / math.sqrt(2.0 * math.pi))
    return (values * cdf).astype(BF), (cdf + values * density).astype(BF)


LANES = 2 * HEAD_DIM
SPAN = 256
NEVER = -1000000000.0


def dot_last(left, right):
    return lax.dot_general(left, right, (((1,), (1,)), ((), ())), preferred_element_type=F32)


def place_of(start, offset):
    return pl.multiple_of(lax.rem(start + offset, SLOT), SPAN)


def heads_apart(rows):
    low = lax.broadcasted_iota(jnp.int32, rows.shape, 1) < HEAD_DIM
    none = jnp.zeros_like(rows)
    return jnp.where(low, rows, none), jnp.where(low, none, rows)


def key_spans(count):
    if count == 1:
        return [(0, SPAN)]
    return [(0, (count - 1) * SPAN), ((count - 1) * SPAN, count * SPAN)]


def score_spans(keys_ref, query, count, limit):
    parts = []
    for start, stop in key_spans(count):
        scores = dot_last(keys_ref[start:stop, :], query)
        if stop == count * SPAN:
            places = lax.broadcasted_iota(jnp.int32, scores.shape, 0)
            if limit is None:
                allowed = places <= lax.broadcasted_iota(jnp.int32, scores.shape, 1)
            else:
                allowed = places < limit - start
            scores = jnp.where(allowed, scores, NEVER)
        parts.append(scores)
    return parts


def for_each_block(causal, query_length, key_length, run, skip):
    blocks = SLOT // SPAN
    if causal:
        for i in range(blocks):
            pl.when(i * SPAN < query_length)(functools.partial(run, i * SPAN, i + 1))
            pl.when(i * SPAN >= query_length)(functools.partial(skip, i * SPAN))
        return
    live = lax.div(query_length + (SPAN - 1), SPAN)
    spans = lax.div(key_length + (SPAN - 1), SPAN)
    for count in range(1, blocks + 1):

        @pl.when(spans == count)
        def _(count=count):
            @pl.loop(0, live)
            def _(i):
                run(pl.multiple_of(i * SPAN, SPAN), count)

    @pl.loop(live, blocks)
    def _(i):
        skip(pl.multiple_of(i * SPAN, SPAN))


def forward_kernel(causal, info, query_ref, key_ref, value_ref, out_ref, logsum_ref, keys, values_t):
    offset, query_length, key_length = info[0], info[1], info[2]
    half = SLOT // 2
    for start in (0, half):
        stored = place_of(start, offset)
        keys[start : start + half, :] = key_ref[pl.ds(stored, half), :]
        values_t[:, start : start + half] = value_ref[pl.ds(stored, half), :].T

    def run(start, count):
        stored = place_of(start, offset)
        scaled = query_ref[pl.ds(stored, SPAN), :] * (1.0 / math.sqrt(HEAD_DIM))
        outs = []
        for head, query in enumerate(heads_apart(scaled)):
            parts = score_spans(keys, query, count, None if causal else key_length)
            highest = functools.reduce(jnp.maximum, [jnp.max(s, axis=0, keepdims=True) for s in parts])
            raised = [jnp.exp(s - highest) for s in parts]
            below = sum(jnp.sum(e, axis=0, keepdims=True) for e in raised)
            mixed = sum(
                jnp.dot(
                    values_t[head * HEAD_DIM : (head + 1) * HEAD_DIM, a:b],
                    e.astype(BF),
                    preferred_element_type=F32,
                )
                for (a, b), e in zip(key_spans(count), raised)
            )
            outs.append(mixed * (1.0 / below))
            logsum_ref[0, head : head + 1, pl.ds(start, SPAN)] = highest + jnp.log(below)
        out_ref[pl.ds(stored, SPAN), :] = jnp.concatenate(outs, axis=0).T.astype(BF)

    def skip(start):
        out_ref[pl.ds(place_of(start, offset), SPAN), :] = jnp.zeros((SPAN, LANES), BF)

    for_each_block(causal, query_length, key_length, run, skip)


def backward_kernel(
    causal, info, query_ref, key_ref, value_ref, up_ref, logsum_ref, *refs
):
    if causal:
        packed_ref, keys, keys_t, values, key_sum, value_sum = refs
        query_out, other_out = packed_ref, packed_ref
        base = LANES
    else:
        query_out, other_out, keys, keys_t, values, key_sum, value_sum = refs
        base = 0
    offset, query_length, key_length = info[0], info[1], info[2]
    half = SLOT // 2
    for start in (0, half):
        stored = place_of(start, offset)
        block = key_ref[pl.ds(stored, half), :]
        keys[start : start + half, :] = block
        keys_t[:, start : start + half] = block.T
        values[start : start + half, :] = value_ref[pl.ds(stored, half), :]
    key_sum[...] = jnp.zeros_like(key_sum)
    value_sum[...] = jnp.zeros_like(value_sum)
    factor = 1.0 / math.sqrt(HEAD_DIM)

    def run(start, count):
        stored = place_of(start, offset)
        queries = heads_apart(query_ref[pl.ds(stored, SPAN), :] * factor)
        ups = heads_apart(up_ref[pl.ds(stored, SPAN), :])
        spans = key_spans(count)
        weights, grads, outs = [], [], []
        for head in range(2):
            logsum = logsum_ref[0, head : head + 1, pl.ds(start, SPAN)]
            parts = score_spans(keys, queries[head], count, None if causal else key_length)
            parts = [jnp.exp(s - logsum) for s in parts]
            pulls = [dot_last(values[a:b, :], ups[head]) for a, b in spans]
            inner = sum(jnp.sum(p * g, axis=0, keepdims=True) for p, g in zip(parts, pulls))
            pulls = [(p * (g - inner)).astype(BF) for p, g in zip(parts, pulls)]
            outs.append(
                sum(
                    jnp.dot(
                        keys_t[head * HEAD_DIM : (head + 1) * HEAD_DIM, a:b],
                        g,
                        preferred_element_type=F32,
                    )
                    for (a, b), g in zip(spans, pulls)
                )
            )
            weights.append([p.astype(BF) for p in parts])
            grads.append(pulls)
        query_out[pl.ds(stored, SPAN), 0:LANES] = (
            jnp.concatenate(outs, axis=0) * factor
        ).T.astype(BF)
        for at, (a, b) in enumerate(spans):
            for head in range(2):
                value_sum[a:b, :] += jnp.dot(weights[head][at], ups[head], preferred_element_type=F32)
                key_sum[a:b, :] += jnp.dot(grads[head][at], queries[head], preferred_element_type=F32)

    def skip(start):
        query_out[pl.ds(place_of(start, offset), SPAN), 0:LANES] = jnp.zeros((SPAN, LANES), BF)

    for_each_block(causal, query_length, key_length, run, skip)
    for start in (0, half):
        stored = place_of(start, offset)
        other_out[pl.ds(stored, half), base : base + LANES] = key_sum[start : start + half, :].astype(BF)
        other_out[pl.ds(stored, half), base + LANES : base + 2 * LANES] = value_sum[
            start : start + half, :
        ].astype(BF)


def column_block(width, of):
    return pl.BlockSpec((SLOT, width), lambda i, info: (0, of(i)))


LOGSUM_BLOCK = pl.BlockSpec((1, 2, SLOT), lambda i, info: (i, 0, 0))


def small_cost():
    return pl.CostEstimate(flops=0, bytes_accessed=2**16, transcendentals=0)


def attend(causal, info, query, keys, pairs):
    step = 3 if causal else 2
    first = 1 if causal else 0
    return pl.pallas_call(
        functools.partial(forward_kernel, causal),
        out_shape=(
            jax.ShapeDtypeStruct((SLOT, pairs * LANES), BF),
            jax.ShapeDtypeStruct((pairs, 2, SLOT), F32),
        ),
        grid_spec=pltpu.PrefetchScalarGridSpec(
            num_scalar_prefetch=1,
            grid=(pairs,),
            in_specs=[
                column_block(LANES, (lambda i: 3 * i) if causal else (lambda i: i)),
                column_block(LANES, lambda i: step * i + first),
                column_block(LANES, lambda i: step * i + first + 1),
            ],
            out_specs=(column_block(LANES, lambda i: i), LOGSUM_BLOCK),
            scratch_shapes=[pltpu.VMEM((SLOT, LANES), BF), pltpu.VMEM((LANES, SLOT), BF)],
        ),
        compiler_params=pltpu.CompilerParams(vmem_limit_bytes=48 * 2**20),
        cost_estimate=small_cost(),
        name="attend",
    )(info, query, keys, keys)


def attend_back(causal, info, query, keys, logsum, upstream, pairs):
    step = 3 if causal else 2
    first = 1 if causal else 0
    if causal:
        out_shape = jax.ShapeDtypeStruct((SLOT, pairs * 3 * LANES), BF)
        out_specs = column_block(3 * LANES, lambda i: i)
    else:
        out_shape = (
            jax.ShapeDtypeStruct((SLOT, pairs * LANES), BF),
            jax.ShapeDtypeStruct((SLOT, pairs * 2 * LANES), BF),
        )
        out_specs = (column_block(LANES, lambda i: i), column_block(2 * LANES, lambda i: i))
    return pl.pallas_call(
        functools.partial(backward_kernel, causal),
        out_shape=out_shape,
        grid_spec=pltpu.PrefetchScalarGridSpec(
            num_scalar_prefetch=1,
            grid=(pairs,),
            in_specs=[
                column_block(LANES, (lambda i: 3 * i) if causal else (lambda i: i)),
                column_block(LANES, lambda i: step * i + first),
                column_block(LANES, lambda i: step * i + first + 1),
                column_block(LANES, lambda i: i),
                LOGSUM_BLOCK,
            ],
            out_specs=out_specs,
            scratch_shapes=[
                pltpu.VMEM((SLOT, LANES), BF),
                pltpu.VMEM((LANES, SLOT), BF),
                pltpu.VMEM((SLOT, LANES), BF),
                pltpu.VMEM((SLOT, LANES), F32),
                pltpu.VMEM((SLOT, LANES), F32),
            ],
        ),
        compiler_params=pltpu.CompilerParams(vmem_limit_bytes=48 * 2**20),
        cost_estimate=small_cost(),
        name="attend_back",
    )(info, query, keys, keys, upstream, logsum)


def build_mask(positions, length, causal):
    allowed = jnp.broadcast_to(positions[None, :] < length, (SLOT, SLOT))
    if causal:
        allowed = allowed & (positions[None, :] <= positions[:, None])
    return allowed


def score_block(query, key, allowed):
    factor = 1.0 / math.sqrt(HEAD_DIM)
    scores = jnp.einsum("qhd,khd->hqk", query, key, preferred_element_type=F32) * factor
    return jnp.where(allowed[None], scores, -1000000000.0)


def split_heads(values):
    return values.reshape(SLOT, -1, HEAD_DIM)


def attention_forward(query, key, value, allowed):
    query, key, value = (split_heads(v) for v in (query, key, value))
    scores = score_block(query, key, allowed)
    highest = jnp.max(scores, axis=-1, keepdims=True)
    raised = jnp.exp(scores - highest)
    denominator = jnp.sum(raised, axis=-1, keepdims=True)
    weights = (raised / denominator).astype(BF)
    mixture = jnp.einsum("hqk,khd->qhd", weights, value, preferred_element_type=F32)
    return mixture.reshape(SLOT, -1).astype(BF), highest + jnp.log(denominator)


def attention_backward(query, key, value, allowed, logsum, upstream):
    query, key, value, upstream = (split_heads(v) for v in (query, key, value, upstream))
    factor = 1.0 / math.sqrt(HEAD_DIM)
    weights = jnp.exp(score_block(query, key, allowed) - logsum)
    value_grad = jnp.einsum("hqk,qhd->khd", weights.astype(BF), upstream, preferred_element_type=F32)
    weight_grad = jnp.einsum("qhd,khd->hqk", upstream, value, preferred_element_type=F32)
    inner = jnp.sum(weights * weight_grad, axis=-1, keepdims=True)
    score_grad = (weights * (weight_grad - inner)).astype(BF)
    query_grad = jnp.einsum("hqk,khd->qhd", score_grad, key, preferred_element_type=F32) * factor
    key_grad = jnp.einsum("hqk,qhd->khd", score_grad, query, preferred_element_type=F32) * factor
    return tuple(g.reshape(SLOT, -1).astype(BF) for g in (query_grad, key_grad, value_grad))


def interleave(arrays, n):
    rows = arrays[0].shape[0]
    return jnp.stack([a.reshape(rows, n, -1) for a in arrays], axis=2).reshape(rows, -1)


def apart(array, n, count):
    rows = array.shape[0]
    parts = array.reshape(rows, n, count, -1)
    return [parts[:, :, i].reshape(rows, -1) for i in range(count)]


def self_attention(plan, packed, length, n):
    if packed.shape[1] == 3 * n * LANES:
        info = jnp.stack([plan.offset, length, length])
        return attend(True, info, packed, packed, n)
    mask = build_mask(plan.positions, length, True)
    return attention_forward(*apart(packed, n, 3), mask)


def self_attention_back(plan, packed, length, n, logsum, upstream):
    if packed.shape[1] == 3 * n * LANES:
        info = jnp.stack([plan.offset, length, length])
        return attend_back(True, info, packed, packed, logsum, upstream, n)
    mask = build_mask(plan.positions, length, True)
    return interleave(attention_backward(*apart(packed, n, 3), mask, logsum, upstream), n)


def cross_attention(plan, query, memory, query_length, key_length, n):
    if query.shape[1] == n * LANES:
        info = jnp.stack([plan.offset, query_length, key_length])
        return attend(False, info, query, memory, n)
    mask = build_mask(plan.positions, key_length, False)
    return attention_forward(query, *apart(memory, n, 2), mask)


def cross_attention_back(plan, query, memory, query_length, key_length, n, logsum, upstream):
    if query.shape[1] == n * LANES:
        info = jnp.stack([plan.offset, query_length, key_length])
        return attend_back(False, info, query, memory, logsum, upstream, n)
    mask = build_mask(plan.positions, key_length, False)
    first, *rest = attention_backward(query, *apart(memory, n, 2), mask, logsum, upstream)
    return first, interleave(rest, n)


ORDER = (0, 2, 3, 1)


class Group:
    def __init__(self, weights, n):
        self.weights = weights
        self.n = n
        self.plans = []
        row = 0
        for axis, groups, local in weights:
            if axis == 0:
                tall, count = local.shape[0], local.shape[1] // n // 128
            else:
                tall, count = local.shape[0] // n, local.shape[1] // 128
            self.plans.append((row, tall, count))
            row += tall * count
        self.rows = row

    def fits(self):
        return all(
            (local.shape[1] % (groups * self.n * 128) == 0 if axis == 0 else local.shape[0] % (self.n * 128) == 0)
            for axis, groups, local in self.weights
        )

    def local_block(self, ref, at, which, block):
        axis, groups, local = self.weights[at]
        _, tall, count = self.plans[at]
        if axis == 0:
            per = count // groups
            i, b = divmod(block, per)
            return ref[:, lanes_at((i * self.n * per + b) * 128 + which * (per * 128))]
        return ref[pl.ds(pl.multiple_of(which * tall, tall), tall), block * 128 : (block + 1) * 128]

    def pack(self, me):
        def body(info, ins, outs):
            for at, (row, tall, count) in enumerate(self.plans):
                for block in range(count):
                    start = row + block * tall
                    outs[0][start : start + tall, :] = self.local_block(ins[at], at, info[0], block)

        out = jax.ShapeDtypeStruct((self.rows, 128), BF)
        return in_vmem(body, "pack", me[None], [w[2] for w in self.weights], [out])[0]

    def assemble(self, me, n_col, moved):
        half = self.rows * (n_col - 1) // 2
        count_w = len(self.weights)
        outs = []
        for axis, groups, local in self.weights:
            shape = (local.shape[0] * n_col, local.shape[1]) if axis == 0 else (local.shape[0], local.shape[1] * n_col)
            outs.append(jax.ShapeDtypeStruct(shape, BF))

        def body(info, ins, outs):
            local_refs, moved_refs = ins[:count_w], ins[count_w:]
            for at, (row, tall, count) in enumerate(self.plans):
                axis = self.weights[at][0]
                width = self.weights[at][2].shape[1]
                for place, j in enumerate(ORDER):
                    for k in range(n_col):
                        for block in range(count):
                            if k == 0:
                                value = self.local_block(local_refs[at], at, info[j], block)
                            else:
                                start = (k - 1) * self.rows + row + block * tall
                                ref = moved_refs[j]
                                if j == 3 and start >= half:
                                    ref, start = moved_refs[4], start - half
                                value = ref[start : start + tall, :]
                            if axis == 0:
                                column = (place * count + block) * 128
                                outs[at][k * tall : (k + 1) * tall, column : column + 128] = value
                            else:
                                column = k * width + block * 128
                                outs[at][place * tall : (place + 1) * tall, column : column + 128] = value

        which = jnp.stack([me ^ j for j in range(self.n)])
        return in_vmem(body, "assemble", which, [w[2] for w in self.weights] + list(moved), outs)


def pick_others(every, n_col, col):
    rows = every.shape[0] // n_col
    return pl.pallas_call(
        lambda info, source, target: target.__setitem__(Ellipsis, source[...]),
        out_shape=jax.ShapeDtypeStruct(((n_col - 1) * rows, every.shape[1]), every.dtype),
        grid_spec=pltpu.PrefetchScalarGridSpec(
            num_scalar_prefetch=1,
            grid=(n_col - 1,),
            in_specs=[
                pl.BlockSpec(
                    (rows, every.shape[1]), lambda k, info: (lax.rem(info[0] - k - 1 + n_col, n_col), 0)
                )
            ],
            out_specs=pl.BlockSpec((rows, every.shape[1]), lambda k, info: (k, 0)),
        ),
        name="pick_others",
    )(col[None], every)


class Blocks:
    def __init__(self, mesh, plan):
        self.n = mesh.shape["dp"]
        assert self.n == len(ORDER)
        self.plan = plan
        self.me = lax.axis_index("dp")

    def hop(self, values, step):
        return lax.ppermute(values, "dp", [(i, i ^ step) for i in range(self.n)])

    def own(self, values, axis, j=0, wait=0):
        shape = values.shape
        parts = values.reshape(shape[:axis] + (self.n, shape[axis] // self.n) + shape[axis + 1 :])
        return lax.dynamic_index_in_dim(parts, (self.me ^ j) + wait, axis, keepdims=False)

    def weave(self, values):
        return jnp.stack([self.own(values, values.ndim - 1, j) for j in ORDER], axis=-2)

    def unweave(self, values):
        order = jnp.array([ORDER.index(j) for j in range(self.n)])
        return jnp.concatenate(
            [
                lax.dynamic_index_in_dim(values, order[self.me ^ q], 0, keepdims=False)
                for q in range(self.n)
            ]
        )

    def others_by_shift(self, piece):
        return jnp.concatenate([self.plan.shift(piece, k) for k in range(1, self.plan.n_col)], axis=0)

    def others_by_gather(self, piece):
        every = lax.all_gather(piece, "col", axis=0, tiled=True)
        return pick_others(every, self.plan.n_col, self.plan.col)

    def hops(self, others):
        return self.hop(others, 1), self.hop(others, 2)

    def corner(self, over):
        half = over[0].shape[0] // 2
        return self.hop(over[1][:half], 1), self.hop(over[0][half:], 2)

    def whole(self, weight):
        axis, groups, local = weight
        every = self.plan.reorder(lax.all_gather(local, "col", axis=0))
        if axis == 0:
            every = every.reshape(-1, groups, local.shape[1] // groups)
            return jnp.stack([self.weave(every[:, i]) for i in range(groups)], axis=2).reshape(every.shape[0], -1)
        every = jnp.moveaxis(every, 0, 1).reshape(local.shape[0], -1)
        parts = every.reshape(self.n, -1, every.shape[1])
        picked = [lax.dynamic_index_in_dim(parts, self.me ^ j, 0, keepdims=False) for j in ORDER]
        return jnp.concatenate(picked, axis=0)

    def reduce_start(self, product, first):
        return self.hop(product(2, 4) if first == 1 else product(1, 3), first)

    def reduce_next(self, product, first, axis, got):
        got = jnp.split(got, 2, axis=axis)
        to_middle, to_base = got if first == 1 else got[::-1]
        middle = product(1, 2) if first == 1 else product(3, 4)
        return product(0, 1), to_base, self.hop(middle + to_middle, 3 - first)

    def reduce_col(self, terms, axis, offload):
        shape = terms[0].shape
        if offload and all(s % 128 == 0 for s in shape):
            parts = sum_blocks(terms, axis, self.plan.n_col, self.plan.col)
            return lax.psum_scatter(parts, "col", scatter_dimension=0, tiled=False)
        part = sum(t.astype(F32) for t in terms).astype(BF)
        parts = part.reshape(shape[:axis] + (self.plan.n_col, -1) + shape[axis + 1 :])
        if offload:
            parts = self.plan.reorder(jnp.moveaxis(parts, axis, 0))
            return lax.psum_scatter(parts, "col", scatter_dimension=0, tiled=False)
        blocks = [lax.index_in_dim(parts, k, axis, keepdims=False) for k in range(self.plan.n_col)]
        got = [blocks[0]] + [self.plan.shift(blocks[k], -k) for k in range(1, self.plan.n_col)]
        return sum(g.astype(F32) for g in got).astype(BF)

    def share_parts(self, part):
        return lax.all_gather(part, "dp", axis=0)


def total(values, mesh, axes):
    for axis in axes:
        size = mesh.shape[axis]
        step = 1
        while step < size:
            values = values + lax.ppermute(values, axis, [(i, i ^ step) for i in range(size)])
            step *= 2
    return values


def layer(mesh):
    def body(
        hidden,
        encoder,
        cotangent,
        answer_length,
        passage_length,
        self_input,
        self_output,
        cross_query,
        cross_memory,
        cross_output,
        expand_weight,
        shrink_weight,
        head_bias,
        expand_bias,
        model_bias,
        norm_gain,
        norm_shift,
    ):
        plan = Plan(mesh)
        blocks = Blocks(mesh, plan)
        n = blocks.n
        me = blocks.me
        width = model_bias.shape[1]
        heads = self_output.shape[0]
        part = heads // n
        hidden_part = expand_bias.shape[0] // n
        answers = lax.dynamic_index_in_dim(answer_length, plan.col, keepdims=False)
        passages = lax.dynamic_index_in_dim(passage_length, plan.col, keepdims=False)
        valid = (plan.own_positions < answers).astype(F32)[:, None]

        group_one = Group([(0, 3, self_input.reshape(width, -1)), (1, 1, self_output)], n)
        group_two = Group(
            [(0, 1, cross_query), (0, 2, cross_memory.reshape(width, -1)), (1, 1, cross_output)], n
        )
        group_three = Group([(0, 1, expand_weight), (1, 1, shrink_weight)], n)
        tiled = group_one.fits() and group_two.fits() and group_three.fits()
        if tiled:
            others_one = blocks.others_by_shift(group_one.pack(me))
            over_one = blocks.hops(others_one)
            corner_one = blocks.corner(over_one)
            w_self, w_self_out = group_one.assemble(me, plan.n_col, (others_one, *over_one, *corner_one))
        else:
            w_self, w_self_out = (blocks.whole(w) for w in group_one.weights)
            w_query, w_memory, w_cross_out = (blocks.whole(w) for w in group_two.weights)
            w_expand, w_shrink = (blocks.whole(w) for w in group_three.weights)
        x_takes = plan.spread(hidden)
        if tiled:
            pieces = [group_two.pack(me), group_three.pack(me)]
            x_takes, pieces = tie(x_takes, pieces)
            others_two, others_three = (blocks.others_by_gather(p) for p in pieces)
        own_norms = jnp.concatenate([model_bias, norm_gain, norm_shift])
        norms = jnp.concatenate(
            [own_norms] + [plan.shift(own_norms, k) for k in range(1, plan.n_col)], axis=1
        )
        bias_rows, gain_rows, shift_rows = norms[:3], norms[3:6], norms[6:]

        head_parts = blocks.weave(head_bias)
        none = jnp.zeros((n, part), F32)
        self_bias = jnp.stack([head_parts[0], none, head_parts[1]], axis=1).reshape(-1)
        query_bias = head_parts[2].reshape(-1)
        memory_bias = jnp.stack([none, head_parts[3]], axis=1).reshape(-1)
        hidden_bias = blocks.weave(expand_bias).reshape(-1)

        own_x = plan.spread_end(x_takes)
        full_x = plan.gather_rows(own_x)
        packed = (dot(full_x, w_self) + self_bias).astype(BF)
        if tiled:
            packed, encoder, others_two = tie(packed, encoder, others_two)
            over_two = blocks.hops(others_two)
        encoder_takes = plan.spread(encoder)
        mixture, self_logsum = self_attention(plan, packed, answers, n)
        if tiled:
            mixture, encoder_takes, over_two = tie(mixture, encoder_takes, over_two)
            corner_two = blocks.corner(over_two)
        branch = plan.scatter_product(mixture, w_self_out) + bias_rows[0]
        normed, normal_one, inverse_one = normalize(own_x.astype(F32) + branch, gain_rows[0], shift_rows[0])
        own_first = normed.astype(BF)
        if tiled:
            own_first, corner_two, others_three, cotangent = tie(
                own_first, corner_two, others_three, cotangent
            )
            over_three = blocks.hops(others_three)
        own_encoder = plan.spread_end(encoder_takes)
        full_encoder = plan.gather_rows(own_encoder)
        full_first = plan.gather_rows(own_first)
        if tiled:
            w_query, w_memory, w_cross_out = group_two.assemble(
                me, plan.n_col, (others_two, *over_two, *corner_two)
            )
        memory = (dot(full_encoder, w_memory) + memory_bias).astype(BF)
        cross_q = (dot(full_first, w_query) + query_bias).astype(BF)
        cotangent_takes = plan.spread(cotangent)
        recall, cross_logsum = cross_attention(plan, cross_q, memory, answers, passages, n)
        if tiled:
            recall, over_three, cotangent_takes = tie(recall, over_three, cotangent_takes)
            corner_three = blocks.corner(over_three)
        branch = plan.scatter_product(recall, w_cross_out) + bias_rows[1]
        normed, normal_two, inverse_two = normalize(own_first.astype(F32) + branch, gain_rows[1], shift_rows[1])
        own_second = normed.astype(BF)
        full_second = plan.gather_rows(own_second)
        if tiled:
            w_expand, w_shrink = group_three.assemble(
                me, plan.n_col, (others_three, *over_three, *corner_three)
            )
        expanded = dot(full_second, w_expand) + hidden_bias
        activated, slope = gelu_and_slope(expanded)
        branch = plan.scatter_product(activated, w_shrink) + bias_rows[2]
        normed, normal_three, inverse_three = normalize(
            own_second.astype(F32) + branch, gain_rows[2], shift_rows[2]
        )
        output_takes = plan.collect((normed * valid).astype(BF))

        def across(*entries):
            def product(a, b):
                pieces = [
                    outer_sum(left[:, a * size : b * size], right).astype(BF).reshape(b - a, size, -1)
                    for left, size, right in entries
                ]
                whole = pieces[0] if len(pieces) == 1 else jnp.concatenate(pieces, axis=1)
                return whole.reshape(-1, whole.shape[-1])

            return product

        def along(left, right, size):
            return lambda a, b: outer_sum(left, right[:, a * size : b * size]).astype(BF)

        own_cotangent = plan.spread_end(cotangent_takes)
        up_three = own_cotangent.astype(F32) * valid
        resid_three = norm_back(up_three, normal_three, inverse_three, gain_rows[2])
        own_dshrink = resid_three.astype(BF)
        full_dshrink = plan.gather_rows(own_dshrink)
        of_shrink = across((activated, hidden_part, full_dshrink))
        got_shrink = blocks.reduce_start(of_shrink, 1)
        d_expanded = (dot_flip(full_dshrink, w_shrink) * slope.astype(F32)).astype(BF)
        of_expand = along(full_second, d_expanded, hidden_part)
        got_expand = blocks.reduce_start(of_expand, 2)
        up_two = resid_three + plan.scatter_product(d_expanded, w_expand, True)
        resid_two = norm_back(up_two, normal_two, inverse_two, gain_rows[1])
        own_dcross = resid_two.astype(BF)
        full_dcross = plan.gather_rows(own_dcross)
        d_recall = dot_flip(full_dcross, w_cross_out).astype(BF)
        d_cross_q, d_memory = cross_attention_back(
            plan, cross_q, memory, answers, passages, n, cross_logsum, d_recall
        )
        d_cross_q, d_memory, got_shrink, got_expand, output_takes = tie(
            d_cross_q, d_memory, got_shrink, got_expand, output_takes
        )
        terms_shrink = blocks.reduce_next(of_shrink, 1, 0, got_shrink)
        terms_expand = blocks.reduce_next(of_expand, 2, 1, got_expand)
        up_one = resid_two + plan.scatter_product(d_cross_q, w_query, True)
        resid_one = norm_back(up_one, normal_one, inverse_one, gain_rows[0])
        own_dself = resid_one.astype(BF)
        full_dself = plan.gather_rows(own_dself)
        d_mixture = dot_flip(full_dself, w_self_out).astype(BF)
        encoder_grad_takes = plan.collect(plan.scatter_product(d_memory, w_memory, True).astype(BF))
        of_cross = across(
            (d_cross_q, part, full_first),
            (d_memory, 2 * part, full_encoder),
            (recall, part, full_dcross),
            (mixture, part, full_dself),
        )
        got_cross = blocks.reduce_start(of_cross, 1)
        d_mixture, terms_shrink, terms_expand = tie(d_mixture, terms_shrink, terms_expand)
        mine_shrink = blocks.reduce_col(terms_shrink, 1, True)
        mine_expand = blocks.reduce_col(terms_expand, 0, True)
        d_packed = self_attention_back(plan, packed, answers, n, self_logsum, d_mixture)
        d_packed, got_cross, encoder_grad_takes = tie(d_packed, got_cross, encoder_grad_takes)
        middle = full_x.shape[1] // 2
        of_low = along(full_x[:, :middle], d_packed, 3 * part)
        of_high = along(full_x[:, middle:], d_packed, 3 * part)
        got_low, got_high = blocks.reduce_start(of_low, 1), blocks.reduce_start(of_high, 2)
        hidden_takes = plan.collect(
            (resid_one + plan.scatter_product(d_packed, w_self, True)).astype(BF)
        )
        got_low, got_high, got_cross = tie(got_low, got_high, got_cross)
        terms_cross = blocks.reduce_next(of_cross, 1, 0, got_cross)
        g_shrink = blocks.share_parts(mine_shrink)
        g_expand = blocks.share_parts(mine_expand)
        halves = zip(
            blocks.reduce_next(of_low, 1, 1, got_low), blocks.reduce_next(of_high, 2, 1, got_high)
        )
        terms_self = [jnp.concatenate(h, axis=0) for h in halves]
        terms_self, terms_cross = tie(terms_self, terms_cross)
        g_cross = blocks.share_parts(blocks.reduce_col(terms_cross, 1, True))
        g_self = blocks.share_parts(blocks.reduce_col(terms_self, 0, False))
        output, g_encoder, g_hidden = (
            plan.collect_end(t) for t in (output_takes, encoder_grad_takes, hidden_takes)
        )

        def rows_of(values):
            return jnp.sum(values, axis=0, dtype=F32)

        wide = jnp.stack(
            [rows_of(v) for v in (own_dself, own_dcross, own_dshrink)]
            + [rows_of(u * v) for u, v in ((up_one, normal_one), (up_two, normal_two), (up_three, normal_three))]
            + [rows_of(v) for v in (up_one, up_two, up_three)]
        )
        packed_sums = rows_of(d_packed).reshape(n, 3, part)
        memory_sums = rows_of(d_memory).reshape(n, 2, part)
        narrow = jnp.concatenate(
            [
                blocks.unweave(v)
                for v in (
                    packed_sums[:, 0],
                    packed_sums[:, 2],
                    rows_of(d_cross_q).reshape(n, part),
                    memory_sums[:, 1],
                    rows_of(d_expanded).reshape(n, hidden_part),
                )
            ]
        )
        wide = total(wide.reshape(-1), mesh, ("row",))
        small = total(jnp.concatenate([wide, narrow]), mesh, ("dp",))
        wide = small[: wide.shape[0]].reshape(9, -1)
        narrow = total(small[wide.size :], mesh, ("col",))
        wide = sum(
            [wide[:, :width]]
            + [plan.shift(wide[:, k * width : (k + 1) * width], -k) for k in range(1, plan.n_col)]
        )

        def turned(grad, count=1):
            taken = grad.reshape(n, width, count, -1)
            return jnp.transpose(taken, (1, 2, 0, 3)).reshape(width, count, -1).astype(F32)

        def straight(grad):
            return grad.reshape(-1, width).astype(F32)

        def straight_turned(grad, count=1):
            taken = grad.reshape(n, count, -1, width)
            return jnp.transpose(taken, (3, 1, 0, 2)).reshape(width, count, -1).astype(F32)

        return (
            output,
            g_hidden,
            g_encoder,
            turned(g_self, 3),
            straight(g_cross[:, 4 * part :]),
            straight_turned(g_cross[:, :part])[:, 0],
            straight_turned(g_cross[:, part : 3 * part], 2),
            straight(g_cross[:, 3 * part : 4 * part]),
            turned(g_expand)[:, 0],
            straight(g_shrink),
            narrow[: 4 * heads].reshape(4, heads),
            narrow[4 * heads :],
            wide[:3],
            wide[3:6],
            wide[6:],
        )

    return body


def solution(mesh):
    rows = P(("dp", "row"), "col")
    weights = (
        P("col", None, "row"),
        P("row", "col"),
        P("col", "row"),
        P("col", None, "row"),
        P("row", "col"),
        P("col", "row"),
        P("row", "col"),
        P(None, "row"),
        P("row"),
        P(None, "col"),
        P(None, "col"),
        P(None, "col"),
    )
    return jax.shard_map(
        layer(mesh),
        mesh=mesh,
        in_specs=(rows, rows, rows, P("dp"), P("dp")) + weights,
        out_specs=(rows, rows, rows) + weights,
        check_vma=False,
    )
```

time: 1210 us -> 735 us (0.61)
  waiting for transfers between devices: 428 us -> 218 us
  matrix products: 326 us -> 136 us
  blocking collectives: 165 us -> 11.2 us
  Pallas kernels: 0 us -> 118 us
  other arithmetic: 145 us -> 36 us
  starting transfers between devices: 33.2 us -> 133 us
  local copies, waits for them, and re-layouts: 91.6 us -> 47 us
    reduce_scatter x7 -> x3, waiting for transfers between devices: 225 us -> 0.01 us  [reduce_col(): return lax.psum_scatter(parts, 'col', scatter_dimension=0, tiled=False)]
    ppermute x0 -> x63, waiting for transfers between devices: none -> 209 us  [the longest x22 121 us: hop(): return lax.ppermute(values, 'dp', [(i, i ^ step) for i in range(self.n)])]
    dot_general x12 -> x0, matrix products: 173 us -> none  [the longest x2 45 us: attention_backward(): jnp.einsum('qhd,khd->hqk', upstream, value, preferred_element_type=F32)]
    psum x2 -> x0, blocking collectives: 120 us -> none  [the longest x1 76.8 us: body(): narrow = lax.psum(narrow, ('dp', 'col'))]
    all_gather x7 -> x5, waiting for transfers between devices: 121 us -> 0.31 us  [the longest x2 0.31 us: others_by_gather(): every = lax.all_gather(piece, 'col', axis=0, tiled=True)]
    pallas_call x0 -> x21, Pallas kernels: none -> 118 us  [the longest x15 56.5 us: in_vmem(): pl.pallas_call(kernel, out_shape=outs, grid_spec=pltpu.PrefetchScalarGrid...]
    ppermute x0 -> x63, starting transfers between devices: none -> 98.8 us  [the longest x22 50.1 us: hop(): return lax.ppermute(values, 'dp', [(i, i ^ step) for i in range(self.n)])]
    all_to_all x6 -> x0, waiting for transfers between devices: 66.5 us -> none  [the longest x3 53.5 us: spread(): moved = lax.all_to_all(ordered, 'col', 0, 2, tiled=True)]
  transfers between devices with their start and end apart: 41 -> 85, of which waited for: 15 -> 32; matrix products, arithmetic and copies ran while one was open for 36% -> 22% of each run, Pallas kernels for 0% -> 15%
where the time goes in v2:
time: 735 us; the launch traced here: 723 us
  waiting for transfers between devices  218 us (30%)
  matrix products  136 us (19%)
  starting transfers between devices  133 us (18%)
  Pallas kernels  118 us (16%)
  local copies, waits for them, and re-layouts  47 us (6%)
  other arithmetic  36 us (5%)
  between operations  24 us (3%)
  blocking collectives  11.2 us (2%)
    ppermute x22, waiting for transfers between devices, hop(): return lax.ppermute(values, 'dp', [(i, i ^ step) for i in range(self.n)])  121 us
    pallas_call x15, Pallas kernels, in_vmem(): pl.pallas_call(kernel, out_shape=outs, grid_spec=pltpu.PrefetchScalarGrid...  56.5 us
    dot_general x24, matrix products, outer_sum(): lax.dot_general(left, right, (((0,), (0,)), ((), ())), preferred_element_...  55.6 us
    ppermute x22, starting transfers between devices, hop(): return lax.ppermute(values, 'dp', [(i, i ^ step) for i in range(self.n)])  50.1 us
    dot_general x11, matrix products, dot_flip(): lax.dot_general(left, right, (((1,), (1,)), ((), ())), preferred_element_...  44.2 us
    ppermute x12, waiting for transfers between devices, shift(): return lax.ppermute(values, 'col', [(i, (i + k) % n) for i in range(n)])  38.3 us
    dot_general x10, matrix products, dot(): return jnp.dot(left, right, preferred_element_type=F32)  36.5 us
    ppermute x14, starting transfers between devices, swap(): return lax.ppermute(values, 'row', [(0, 1), (1, 0)])  33.6 us
  transfers between devices with their start and end apart: 85, of which 32 were waited for; matrix products, arithmetic and copies ran while one was open for 22% of the time, Pallas kernels for 15%

profile of v2, /device:TPU:0, one launch (start us, length us, event | category | flops | bytes accessed | tf_op | source)
XLA Modules:
  0.0 723.1 jit_solution(4418482447366350489)
XLA Ops:
  18.9 5.3 collective-permute-done.5
  24.3 18.8 %collective-permute-done.6 = bf16[1024,128]{1,0:T(8,128)(2,1)S(1)} collective-permute-done((bf16[1024,128]{1,0:T(8,128)(2,1)}, bf16[1024,128]{1,0:T(8,128)(2,1)S(1)}, u32[]{:S(2)}, u32[]{:S(2)}) %collective-permute-start.6) | collective-permute-done | bytes 262176 | tf_op jit(solution)/shard_map/ppermute | solution.py:116
  53.6 8.6 %collective-permute-done.2.refs_2_ = bf16[512,256]{1,0:T(8,128)(2,1)} collective-permute-done((bf16[512,256]{1,0:T(8,128)(2,1)}, bf16[512,256]{1,0:T(8,128)(2,1)}, u32[]{:S(2)}, u32[]{:S(2)}) %collective-permute-start.2) | collective-permute-done | bytes 262176 | tf_op jit(solution)/shard_map/ppermute | solution.py:154
  65.2 5.4 collective-permute-start.4
  73.4 8.5 %collective-permute-done.10.refs_5_ = bf16[1536,128]{1,0:T(8,128)(2,1)S(1)} collective-permute-done((bf16[1536,128]{1,0:T(8,128)(2,1)S(1)}, bf16[1536,128]{1,0:T(8,128)(2,1)S(1)}, u32[]{:S(2)}, u32[]{:S(2)}) %collective-permute-start.10) | collective-permute-done | bytes 393248 | tf_op jit(solution)/shard_map/ppermute | solution.py:642
  83.4 5.7 assemble.3
  89.1 5.6 add_convert_fusion.query_ref.key_ref.value_ref
  104.5 12.4 %collective-permute-done.15.refs_3_ = bf16[512,256]{1,0:T(8,128)(2,1)S(1)} collective-permute-done((bf16[512,256]{1,0:T(8,128)(2,1)S(1)}, bf16[512,256]{1,0:T(8,128)(2,1)S(1)}, u32[]{:S(2)}, u32[]{:S(2)}) %collective-permute-start.15) | collective-permute-done | bytes 262176 | tf_op jit(solution)/shard_map/ppermute | solution.py:154
  121.8 8.7 %attend.2 = (bf16[1024,512]{1,0:T(8,128)(2,1)S(1)}, f32[4,2,1024]{2,1,0:T(2,128)S(1)}) custom-call(s32[3]{0:T(128)S(1)} %pad_add_fusion.4.info, bf16[1024,1536]{1,0:T(8,128)(2,1)S(1)} %add_convert_fusion.query_ref.key_ref.value_ref, bf16[1024,1536]{1,0:T(8,128)(2,1)S(1)} %add_convert_fusion.query_ref.key_ref.value_ref, ...), custom_call_target="tpu_custom_call" | custom-call | bytes 65536 | tf_op jit(solution)/shard_map/attend/pallas_call | solution.py:389
  130.6 7.6 %collective-permute-done.14.refs_2_ = bf16[512,256]{1,0:T(8,128)(2,1)} collective-permute-done((bf16[512,256]{1,0:T(8,128)(2,1)}, bf16[512,256]{1,0:T(8,128)(2,1)}, u32[]{:S(2)}, u32[]{:S(2)}) %collective-permute-start.14) | collective-permute-done | bytes 262176 | tf_op jit(solution)/shard_map/ppermute | solution.py:154
  140.3 25.3 %collective-permute-start.18 = (f32[512,1024]{1,0:T(8,128)}, f32[512,1024]{1,0:T(8,128)}, u32[]{:S(2)}, u32[]{:S(2)}) collective-permute-start(f32[512,1024]{1,0:T(8,128)} %fusion.85), channel_id=1, source_target_pairs={{0,4},{4,0},{1,5},{5,1},{2,6},{6,2},{3,7},{7,3},{8,12},{12,8},{9,1... | collective-permute-start | bytes 6291464 | tf_op jit(solution)/shard_map/ppermute | solution.py:112
  193.8 6.0 assemble.4
  208.9 13.1 %attend.3 = (bf16[1024,512]{1,0:T(8,128)(2,1)S(1)}, f32[4,2,1024]{2,1,0:T(2,128)S(1)}) custom-call(s32[3]{0:T(128)S(1)} %pad_add_fusion.1.info, bf16[1024,512]{1,0:T(8,128)(2,1)S(1)} %add_convert_fusion.5.query_ref, bf16[1024,1024]{1,0:T(8,128)(2,1)S(1)} %add_convert_fusion.1.key_ref.value_ref, bf16[1024,1024]{1,0:T(8,128)(2,1)S(1)} %add_convert_fusion.1.key_ref.value_ref), custom_call_target="tpu_custom_call" | custom-call | bytes 65536 | tf_op jit(solution)/shard_map/attend/pallas_call | solution.py:389
  236.7 10.9 %collective-permute-start.34 = (bf16[3072,128]{1,0:T(8,128)(2,1)}, bf16[3072,128]{1,0:T(8,128)(2,1)}, u32[]{:S(2)}, u32[]{:S(2)}) collective-permute-start(bf16[3072,128]{1,0:T(8,128)(2,1)} %slice.298), channel_id=1, source_target_pairs={{0,8},{8,0},{16,24},{24,16},{1,9},{9,1},{17,25},{25,17},{2,10},{10... | collective-permute-start | bytes 2359304 | tf_op jit(solution)/shard_map/ppermute | solution.py:642
  247.6 18.1 %collective-permute-done.34.refs_5_ = bf16[3072,128]{1,0:T(8,128)(2,1)} collective-permute-done((bf16[3072,128]{1,0:T(8,128)(2,1)}, bf16[3072,128]{1,0:T(8,128)(2,1)}, u32[]{:S(2)}, u32[]{:S(2)}) %collective-permute-start.34) | collective-permute-done | bytes 786464 | tf_op jit(solution)/shard_map/ppermute | solution.py:642
  267.2 9.6 %assemble.5 = (bf16[1024,2048]{1,0:T(8,128)(2,1)}, bf16[2048,1024]{1,0:T(8,128)(2,1)}) custom-call(s32[4]{0:T(128)} %pad_add_fusion.5.info, bf16[256,2048]{1,0:T(8,128)(2,1)} %refs_0_.7, bf16[2048,256]{1,0:T(8,128)(2,1)} %refs_1_.7, bf16[6144,128]{1,0:T(8,128)(2,1)} %pick_others.3.refs_2_, bf16[6144,128]{1,0:T(8,128)(2,1)} %collective-permute-done.26.refs_3_, ...), custom_call_target="tpu_custom_call" | custom-call | bytes 65536 | tf_op jit(solution)/shard_map/assemble/pallas_call | solution.py:41
  276.8 10.6 %multiply_convert_fusion.1 = (bf16[1024,2048]{1,0:T(8,128)(2,1)S(1)}, f32[1024,2048]{1,0:T(8,128)}) fusion(f32[2048]{0:T(1024)S(1)} %bitcast.274, bf16[1024,2048]{1,0:T(8,128)(2,1)} %get-tuple-element.117, bf16[512,1024]{1,0:T(8,128)(2,1)} %collective-permute-done.33, bf16[512,1024]{1,0:T(8,128)(2,1)} %add_convert_fusion.4), kind=kOutput, calls=%fused_computation.8 | convolution fusion | flops 4311744512 | bytes 18882560 | tf_op jit(solution)/shard_map/dot_general | solution.py:22
  295.5 5.0 fusion.127
  307.6 11.8 %convert_reduce_fusion = (f32[2048]{0:T(1024)S(1)}, bf16[1024,2048]{1,0:T(8,128)(2,1)}) fusion(f32[1024,2048]{1,0:T(8,128)} %get-tuple-element.316, f32[2048]{0:T(1024)S(1)} %bitcast.275, bf16[2048,1024]{1,0:T(8,128)(2,1)S(1)} %copy-done.76, bf16[512,1024]{1,0:T(8,128)(2,1)S(1)} %collective-permute-done.37, bf16[512,1024]{1,0:T(8,128)(2,1)S(1)} %get-tuple-element.230), kind=kOutput, calls=%fused_computation.6 | convolution fusion | flops 4330616832 | bytes 18890752 | tf_op jit(solution)/shard_map/dot_general | solution.py:26
  327.9 5.5 fusion.23
  341.1 10.3 %collective-permute-done.45.refs_3_ = bf16[512,256]{1,0:T(8,128)(2,1)S(1)} collective-permute-done((bf16[512,256]{1,0:T(8,128)(2,1)S(1)}, bf16[512,256]{1,0:T(8,128)(2,1)S(1)}, u32[]{:S(2)}, u32[]{:S(2)}) %collective-permute-start.45) | collective-permute-done | bytes 262176 | tf_op jit(solution)/shard_map/ppermute | solution.py:175
  356.5 20.8 %attend_back.2 = (bf16[1024,512]{1,0:T(8,128)(2,1)S(1)}, bf16[1024,1024]{1,0:T(8,128)(2,1)S(1)}) custom-call(s32[3]{0:T(128)S(1)} %pad_add_fusion.1.info, bf16[1024,512]{1,0:T(8,128)(2,1)S(1)} %add_convert_fusion.5.query_ref, bf16[1024,1024]{1,0:T(8,128)(2,1)} %copy-done.1, bf16[1024,1024]{1,0:T(8,128)(2,1)} %copy-done.1, ...), custom_call_target="tpu_custom_call" | custom-call | bytes 65536 | tf_op jit(solution)/shard_map/attend_back/pallas_call | solution.py:424
  394.3 18.3 %collective-permute-start.49 = (bf16[1024,512]{1,0:T(8,128)(2,1)S(1)}, bf16[1024,512]{1,0:T(8,128)(2,1)S(1)}, u32[]{:S(2)}, u32[]{:S(2)}) collective-permute-start(bf16[1024,512]{1,0:T(8,128)(2,1)S(1)} %fusion.46), channel_id=1, source_target_pairs={{0,8},{8,0},{16,24},{24,16},{1,9},{9,1},{17,25},{25,17},{2,10},{10... | collective-permute-start | bytes 3145736 | tf_op jit(solution)/shard_map/ppermute | solution.py:642
  427.8 8.6 %collective-permute-done.49.refs_2_ = bf16[1024,512]{1,0:T(8,128)(2,1)S(1)} collective-permute-done((bf16[1024,512]{1,0:T(8,128)(2,1)S(1)}, bf16[1024,512]{1,0:T(8,128)(2,1)S(1)}, u32[]{:S(2)}, u32[]{:S(2)}) %collective-permute-start.49) | collective-permute-done | bytes 1048608 | tf_op jit(solution)/shard_map/ppermute | solution.py:642
  492.9 12.1 %attend_back.3 = bf16[1024,1536]{1,0:T(8,128)(2,1)S(1)} custom-call(s32[3]{0:T(128)S(1)} %pad_add_fusion.4.info, bf16[1024,1536]{1,0:T(8,128)(2,1)} %copy-done, bf16[1024,1536]{1,0:T(8,128)(2,1)} %copy-done, bf16[1024,1536]{1,0:T(8,128)(2,1)} %copy-done, bf16[1024,512]{1,0:T(8,128)(2,1)S(1)} %copy-done.10, f32[4,2,1024]{2,1,0:T(2,128)S(1)} %get-tuple-element.134.logsum_ref), custom_call_target="tpu_custom_call" | custom-call | bytes 65536 | tf_op jit(solution)/shard_map/attend_back/pallas_call | solution.py:424
  509.1 29.3 %collective-permute-done.50 = bf16[1280,1024]{1,0:T(8,128)(2,1)} collective-permute-done((bf16[1280,1024]{1,0:T(8,128)(2,1)}, bf16[1280,1024]{1,0:T(8,128)(2,1)}, u32[]{:S(2)}, u32[]{:S(2)}) %collective-permute-start.50) | collective-permute-done | bytes 2621472 | tf_op jit(solution)/shard_map/ppermute | solution.py:642
  551.7 11.7 %collective-permute-done.61 = bf16[512,768]{1,0:T(8,128)(2,1)S(1)} collective-permute-done((bf16[512,768]{1,0:T(8,128)(2,1)S(1)}, bf16[512,768]{1,0:T(8,128)(2,1)S(1)}, u32[]{:S(2)}, u32[]{:S(2)}) %collective-permute-start.61) | collective-permute-done | bytes 786464 | tf_op jit(solution)/shard_map/ppermute | solution.py:642
  582.5 28.1 %collective-permute-done.63 = bf16[512,384]{1,0:T(8,128)(2,1)S(1)} collective-permute-done((bf16[512,384]{1,0:T(8,128)(2,1)S(1)}, bf16[512,384]{1,0:T(8,128)(2,1)S(1)}, u32[]{:S(2)}, u32[]{:S(2)}) %collective-permute-start.63) | collective-permute-done | bytes 393248 | tf_op jit(solution)/shard_map/ppermute | solution.py:642
  626.9 5.1 fusion.30
  671.0 9.4 %collective-permute-start.58 = (bf16[512,256]{1,0:T(8,128)(2,1)}, bf16[512,256]{1,0:T(8,128)(2,1)}, u32[]{:S(2)}, u32[]{:S(2)}) collective-permute-start(bf16[512,256]{1,0:T(8,128)(2,1)} %get-tuple-element.247), channel_id=1, source_target_pairs={{1,0},{0,1},{5,2},{4,3},{3,4},{2,5},{7,6},{6,7},{9,8},{8,9},{13,10... | collective-permute-start | bytes 786440 | tf_op jit(solution)/shard_map/ppermute | solution.py:175
  681.8 10.1 %collective-permute-done.67 = bf16[256,384]{1,0:T(8,128)(2,1)S(1)} collective-permute-done((bf16[256,384]{1,0:T(8,128)(2,1)S(1)}, bf16[256,384]{1,0:T(8,128)(2,1)S(1)}, u32[]{:S(2)}, u32[]{:S(2)}) %collective-permute-start.67) | collective-permute-done | bytes 196640 | tf_op jit(solution)/shard_map/ppermute | solution.py:116
  692.0 11.2 %all-gather = bf16[1024,384]{1,0:T(8,128)(2,1)S(1)} all-gather(bf16[256,384]{1,0:T(8,128)(2,1)S(1)} %add_convert_fusion.8), channel_id=2, replica_groups=mesh['dp'=4,'row'=2,'col'=4] {'dp'}, dimensions={0}, use_global_device_ids=true | all-gather | bytes 983040 | tf_op jit(solution)/shard_map/all_gather | solution.py:710
  (534 shorter events, 321.4 us)
Async XLA Ops:
  7.2 87.9 %all-gather.7.cloned.1.call-start = ((), (), s32[]{:S(2)}) async-start(), calls=%async_computation.3 | async-start | bytes 1310720 | tf_op jit(solution)/shard_map/all_gather | solution.py:665
  70.6 109.2 %all-gather.9.cloned.1.call-start = ((), (), s32[]{:S(2)}) async-start(), calls=%async_computation.4 | async-start | bytes 2621440 | tf_op jit(solution)/shard_map/all_gather | solution.py:665
  98.0 40.2 %collective-permute-start.17 = (bf16[3072,128]{1,0:T(8,128)(2,1)}, bf16[3072,128]{1,0:T(8,128)(2,1)}, u32[]{:S(2)}, u32[]{:S(2)}) collective-permute-start(bf16[3072,128]{1,0:T(8,128)(2,1)} %pick_others.2.refs_3_), channel_id=1, source_target_pairs={{0,16},{8,24},{16,0},{24,8},{1,17},{9,25},{17,1},{25,9},{2,18},{10... | collective-permute-start | bytes 2359304 | tf_op jit(solution)/shard_map/ppermute | solution.py:642
  99.4 38.8 %collective-permute-start.16 = (bf16[3072,128]{1,0:T(8,128)(2,1)}, bf16[3072,128]{1,0:T(8,128)(2,1)}, u32[]{:S(2)}, u32[]{:S(2)}) collective-permute-start(bf16[3072,128]{1,0:T(8,128)(2,1)} %pick_others.2.refs_3_), channel_id=1, source_target_pairs={{0,8},{8,0},{16,24},{24,16},{1,9},{9,1},{17,25},{25,17},{2,10},{10... | collective-permute-start | bytes 2359304 | tf_op jit(solution)/shard_map/ppermute | solution.py:642
  100.9 381.2 %reduce-scatter.6.cloned.1.call-start = ((), (), s32[]{:S(2)}) async-start(), calls=%async_computation.7 | async-start | bytes 1310720 | tf_op jit(solution)/shard_map/reduce_scatter | solution.py:699
  103.1 35.1 %collective-permute-start.14 = (bf16[512,256]{1,0:T(8,128)(2,1)}, bf16[512,256]{1,0:T(8,128)(2,1)}, u32[]{:S(2)}, u32[]{:S(2)}) collective-permute-start(bf16[512,256]{1,0:T(8,128)(2,1)} %get-tuple-element.262), channel_id=1, source_target_pairs={{0,4},{1,5},{2,0},{3,1},{4,6},{5,7},{6,2},{7,3},{8,12},{9,13},{10,... | collective-permute-start | bytes 786440 | tf_op jit(solution)/shard_map/ppermute | solution.py:154
  104.1 34.1 %collective-permute-start.13 = (bf16[512,256]{1,0:T(8,128)(2,1)}, bf16[512,256]{1,0:T(8,128)(2,1)}, u32[]{:S(2)}, u32[]{:S(2)}) collective-permute-start(bf16[512,256]{1,0:T(8,128)(2,1)} %get-tuple-element.263), channel_id=1, source_target_pairs={{0,1},{1,0},{2,5},{3,4},{4,3},{5,2},{6,7},{7,6},{8,9},{9,8},{10,13... | collective-permute-start | bytes 786440 | tf_op jit(solution)/shard_map/ppermute | solution.py:154
  140.3 43.1 %collective-permute-start.18 = (f32[512,1024]{1,0:T(8,128)}, f32[512,1024]{1,0:T(8,128)}, u32[]{:S(2)}, u32[]{:S(2)}) collective-permute-start(f32[512,1024]{1,0:T(8,128)} %fusion.85), channel_id=1, source_target_pairs={{0,4},{4,0},{1,5},{5,1},{2,6},{6,2},{3,7},{7,3},{8,12},{12,8},{9,1... | collective-permute-start | bytes 6291464 | tf_op jit(solution)/shard_map/ppermute | solution.py:112
  188.0 36.6 %collective-permute-start.27 = (bf16[6144,128]{1,0:T(8,128)(2,1)S(1)}, bf16[6144,128]{1,0:T(8,128)(2,1)S(1)}, u32[]{:S(2)}, u32[]{:S(2)}) collective-permute-start(bf16[6144,128]{1,0:T(8,128)(2,1)S(1)} %copy-done.18), channel_id=1, source_target_pairs={{0,16},{8,24},{16,0},{24,8},{1,17},{9,25},{17,1},{25,9},{2,18},{10... | collective-permute-start | bytes 4718600 | tf_op jit(solution)/shard_map/ppermute | solution.py:642
  189.4 36.4 %collective-permute-start.26 = (bf16[6144,128]{1,0:T(8,128)(2,1)S(1)}, bf16[6144,128]{1,0:T(8,128)(2,1)}, u32[]{:S(2)}, u32[]{:S(2)}) collective-permute-start(bf16[6144,128]{1,0:T(8,128)(2,1)S(1)} %copy-done.18), channel_id=1, source_target_pairs={{0,8},{8,0},{16,24},{24,16},{1,9},{9,1},{17,25},{25,17},{2,10},{10... | collective-permute-start | bytes 4718600 | tf_op jit(solution)/shard_map/ppermute | solution.py:642
  233.5 43.3 %collective-permute-start.33 = (bf16[512,1024]{1,0:T(8,128)(2,1)}, bf16[512,1024]{1,0:T(8,128)(2,1)}, u32[]{:S(2)}, u32[]{:S(2)}) collective-permute-start(bf16[512,1024]{1,0:T(8,128)(2,1)} %add_convert_fusion.4), channel_id=1, source_target_pairs={{0,4},{4,0},{1,5},{5,1},{2,6},{6,2},{3,7},{7,3},{8,12},{12,8},{9,1... | collective-permute-start | bytes 3145736 | tf_op jit(solution)/shard_map/ppermute | solution.py:112
  236.7 29.1 %collective-permute-start.34 = (bf16[3072,128]{1,0:T(8,128)(2,1)}, bf16[3072,128]{1,0:T(8,128)(2,1)}, u32[]{:S(2)}, u32[]{:S(2)}) collective-permute-start(bf16[3072,128]{1,0:T(8,128)(2,1)} %slice.298), channel_id=1, source_target_pairs={{0,8},{8,0},{16,24},{24,16},{1,9},{9,1},{17,25},{25,17},{2,10},{10... | collective-permute-start | bytes 2359304 | tf_op jit(solution)/shard_map/ppermute | solution.py:642
  327.6 49.8 %collective-permute-start.40 = (bf16[1024,1024]{1,0:T(8,128)(2,1)}, bf16[1024,1024]{1,0:T(8,128)(2,1)}, u32[]{:S(2)}, u32[]{:S(2)}) collective-permute-start(bf16[1024,1024]{1,0:T(8,128)(2,1)} %fusion.20), channel_id=1, source_target_pairs={{0,8},{8,0},{16,24},{24,16},{1,9},{9,1},{17,25},{25,17},{2,10},{10... | collective-permute-start | bytes 6291464 | tf_op jit(solution)/shard_map/ppermute | solution.py:642
  333.4 47.9 %collective-permute-start.41 = (bf16[1024,1024]{1,0:T(8,128)(2,1)}, bf16[1024,1024]{1,0:T(8,128)(2,1)}, u32[]{:S(2)}, u32[]{:S(2)}) collective-permute-start(bf16[1024,1024]{1,0:T(8,128)(2,1)} %fusion.23), channel_id=1, source_target_pairs={{0,16},{8,24},{16,0},{24,8},{1,17},{9,25},{17,1},{25,9},{2,18},{10... | collective-permute-start | bytes 6291464 | tf_op jit(solution)/shard_map/ppermute | solution.py:642
  341.0 36.3 %collective-permute-start.44 = (bf16[512,256]{1,0:T(8,128)(2,1)S(1)}, bf16[512,256]{1,0:T(8,128)(2,1)S(1)}, u32[]{:S(2)}, u32[]{:S(2)}) collective-permute-start(bf16[512,256]{1,0:T(8,128)(2,1)S(1)} %get-tuple-element.254), channel_id=1, source_target_pairs={{4,0},{5,1},{0,2},{1,3},{6,4},{7,5},{2,6},{3,7},{12,8},{13,9},{8,1... | collective-permute-start | bytes 786440 | tf_op jit(solution)/shard_map/ppermute | solution.py:175
  385.9 41.9 %collective-permute-start.48 = (bf16[512,1024]{1,0:T(8,128)(2,1)S(1)}, bf16[512,1024]{1,0:T(8,128)(2,1)}, u32[]{:S(2)}, u32[]{:S(2)}) collective-permute-start(bf16[512,1024]{1,0:T(8,128)(2,1)S(1)} %fusion.45), channel_id=1, source_target_pairs={{0,16},{8,24},{16,0},{24,8},{1,17},{9,25},{17,1},{25,9},{2,18},{10... | collective-permute-start | bytes 3145736 | tf_op jit(solution)/shard_map/ppermute | solution.py:642
  390.0 34.5 %collective-permute-start.47 = (bf16[512,1024]{1,0:T(8,128)(2,1)S(1)}, bf16[512,1024]{1,0:T(8,128)(2,1)S(1)}, u32[]{:S(2)}, u32[]{:S(2)}) collective-permute-start(bf16[512,1024]{1,0:T(8,128)(2,1)S(1)} %get-tuple-element.235), channel_id=1, source_target_pairs={{0,4},{4,0},{1,5},{5,1},{2,6},{6,2},{3,7},{7,3},{8,12},{12,8},{9,1... | collective-permute-start | bytes 3145736 | tf_op jit(solution)/shard_map/ppermute | solution.py:112
  394.3 42.1 %collective-permute-start.49 = (bf16[1024,512]{1,0:T(8,128)(2,1)S(1)}, bf16[1024,512]{1,0:T(8,128)(2,1)S(1)}, u32[]{:S(2)}, u32[]{:S(2)}) collective-permute-start(bf16[1024,512]{1,0:T(8,128)(2,1)S(1)} %fusion.46), channel_id=1, source_target_pairs={{0,8},{8,0},{16,24},{24,16},{1,9},{9,1},{17,25},{25,17},{2,10},{10... | collective-permute-start | bytes 3145736 | tf_op jit(solution)/shard_map/ppermute | solution.py:642
  440.7 65.5 %reduce-scatter.8.cloned.1.call-start = ((), (), s32[]{:S(2)}) async-start(), calls=%async_computation.9 | async-start | bytes 1310720 | tf_op jit(solution)/shard_map/reduce_scatter | solution.py:699
  453.6 28.6 %collective-permute-start.51 = (f32[512,1024]{1,0:T(8,128)}, f32[512,1024]{1,0:T(8,128)}, u32[]{:S(2)}, u32[]{:S(2)}) collective-permute-start(f32[512,1024]{1,0:T(8,128)} %fusion.63), channel_id=1, source_target_pairs={{0,4},{4,0},{1,5},{5,1},{2,6},{6,2},{3,7},{7,3},{8,12},{12,8},{9,1... | collective-permute-start | bytes 6291464 | tf_op jit(solution)/shard_map/ppermute | solution.py:112
  464.2 182.4 %all-gather.13.cloned.1.call-start = ((), (), s32[]{:S(2)}) async-start(), calls=%async_computation.8 | async-start | bytes 1310720 | tf_op jit(solution)/shard_map/all_gather | solution.py:710
  472.9 65.5 %collective-permute-start.50 = (bf16[1280,1024]{1,0:T(8,128)(2,1)}, bf16[1280,1024]{1,0:T(8,128)(2,1)}, u32[]{:S(2)}, u32[]{:S(2)}) collective-permute-start(bf16[1280,1024]{1,0:T(8,128)(2,1)} %bitcast.49), channel_id=1, source_target_pairs={{0,8},{8,0},{16,24},{24,16},{1,9},{9,1},{17,25},{25,17},{2,10},{10... | collective-permute-start | bytes 7864328 | tf_op jit(solution)/shard_map/ppermute | solution.py:642
  482.1 166.8 %all-gather.15.cloned.1.call-start = ((), (), s32[]{:S(2)}) async-start(), calls=%async_computation.10 | async-start | bytes 1310720 | tf_op jit(solution)/shard_map/all_gather | solution.py:710
  506.2 145.4 %reduce-scatter.4.cloned.1.call-start = ((), (), s32[]{:S(2)}) async-start(), calls=%async_computation.5 | async-start | bytes 1638400 | tf_op jit(solution)/shard_map/reduce_scatter | solution.py:699
  570.4 41.1 %collective-permute-start.65 = (bf16[640,1024]{1,0:T(8,128)(2,1)S(1)}, bf16[640,1024]{1,0:T(8,128)(2,1)S(1)}, u32[]{:S(2)}, u32[]{:S(2)}) collective-permute-start(bf16[640,1024]{1,0:T(8,128)(2,1)S(1)} %get-tuple-element.239), channel_id=1, source_target_pairs={{0,16},{8,24},{16,0},{24,8},{1,17},{9,25},{17,1},{25,9},{2,18},{10... | collective-permute-start | bytes 3932168 | tf_op jit(solution)/shard_map/ppermute | solution.py:642
  576.2 34.3 %collective-permute-start.63 = (bf16[512,384]{1,0:T(8,128)(2,1)S(1)}, bf16[512,384]{1,0:T(8,128)(2,1)S(1)}, u32[]{:S(2)}, u32[]{:S(2)}) collective-permute-start(bf16[512,384]{1,0:T(8,128)(2,1)S(1)} %fusion.49), channel_id=1, source_target_pairs={{0,16},{8,24},{16,0},{24,8},{1,17},{9,25},{17,1},{25,9},{2,18},{10... | collective-permute-start | bytes 1179656 | tf_op jit(solution)/shard_map/ppermute | solution.py:642
  616.2 93.3 %all-gather.11.cloned.1.call-start = ((), (), s32[]{:S(2)}) async-start(), calls=%async_computation.6 | async-start | bytes 1638400 | tf_op jit(solution)/shard_map/all_gather | solution.py:710
  632.0 31.1 %collective-permute-start.56 = (f32[512,1024]{1,0:T(8,128)}, f32[512,1024]{1,0:T(8,128)}, u32[]{:S(2)}, u32[]{:S(2)}) collective-permute-start(f32[512,1024]{1,0:T(8,128)} %fusion.30), channel_id=1, source_target_pairs={{0,4},{4,0},{1,5},{5,1},{2,6},{6,2},{3,7},{7,3},{8,12},{12,8},{9,1... | collective-permute-start | bytes 6291464 | tf_op jit(solution)/shard_map/ppermute | solution.py:112
  661.6 30.3 %collective-permute-start.67 = (bf16[256,384]{1,0:T(8,128)(2,1)S(1)}, bf16[256,384]{1,0:T(8,128)(2,1)S(1)}, u32[]{:S(2)}, u32[]{:S(2)}) collective-permute-start(bf16[256,384]{1,0:T(8,128)(2,1)S(1)} %get-tuple-element.271), channel_id=1, source_target_pairs={{0,2},{1,3},{2,0},{3,1},{4,6},{5,7},{6,4},{7,5},{8,10},{9,11},{10,... | collective-permute-start | bytes 589832 | tf_op jit(solution)/shard_map/ppermute | solution.py:116
  668.5 37.7 %collective-permute-start.60 = (bf16[512,256]{1,0:T(8,128)(2,1)}, bf16[512,256]{1,0:T(8,128)(2,1)}, u32[]{:S(2)}, u32[]{:S(2)}) collective-permute-start(bf16[512,256]{1,0:T(8,128)(2,1)} %get-tuple-element.245), channel_id=1, source_target_pairs={{5,0},{4,1},{1,2},{0,3},{7,4},{6,5},{3,6},{2,7},{13,8},{12,9},{9,1... | collective-permute-start | bytes 786440 | tf_op jit(solution)/shard_map/ppermute | solution.py:175
  671.0 35.2 %collective-permute-start.59 = (bf16[512,256]{1,0:T(8,128)(2,1)}, bf16[512,256]{1,0:T(8,128)(2,1)}, u32[]{:S(2)}, u32[]{:S(2)}) collective-permute-start(bf16[512,256]{1,0:T(8,128)(2,1)} %get-tuple-element.246), channel_id=1, source_target_pairs={{4,0},{5,1},{0,2},{1,3},{6,4},{7,5},{2,6},{3,7},{12,8},{13,9},{8,1... | collective-permute-start | bytes 786440 | tf_op jit(solution)/shard_map/ppermute | solution.py:175
  671.0 35.2 %collective-permute-start.58 = (bf16[512,256]{1,0:T(8,128)(2,1)}, bf16[512,256]{1,0:T(8,128)(2,1)}, u32[]{:S(2)}, u32[]{:S(2)}) collective-permute-start(bf16[512,256]{1,0:T(8,128)(2,1)} %get-tuple-element.247), channel_id=1, source_target_pairs={{1,0},{0,1},{5,2},{4,3},{3,4},{2,5},{7,6},{6,7},{9,8},{8,9},{13,10... | collective-permute-start | bytes 786440 | tf_op jit(solution)/shard_map/ppermute | solution.py:175
  (145 other events, 1649.4 us)
Sparse Core Ops, SparseCore 0:
  70.8 24.2 all-gather.6
  101.0 62.1 all-gather.8
  440.8 26.2 reduce-scatter.5
  469.9 33.8 reduce-scatter.7
  505.6 35.8 all-gather.12
  543.2 33.7 all-gather.14
  616.4 29.4 reduce-scatter.3
  651.7 28.6 all-gather.10

commit v3 on v2

--- a/solution.py
+++ b/solution.py
@@ -38,19 +38,26 @@
     def spec(shape):
         return pl.BlockSpec(shape, lambda i, info: (0,) * len(shape))
 
+    def spec_in(array):
+        if not isinstance(array, tuple):
+            return spec(array.shape)
+        whole, at = array
+        rest = whole.shape[1:]
+        return pl.BlockSpec((None, *rest), lambda i, info: (at,) + (0,) * len(rest))
+
     return pl.pallas_call(
         kernel,
         out_shape=outs,
         grid_spec=pltpu.PrefetchScalarGridSpec(
             num_scalar_prefetch=1,
             grid=(1,),
-            in_specs=[spec(a.shape) for a in arrays],
+            in_specs=[spec_in(a) for a in arrays],
             out_specs=[spec(o.shape) for o in outs],
         ),
         compiler_params=pltpu.CompilerParams(vmem_limit_bytes=56 * 2**20),
         cost_estimate=small_cost(),
         name=name,
-    )(scalars, *arrays)
+    )(scalars, *[a[0] if isinstance(a, tuple) else a for a in arrays])
 
 
 def lanes_at(start):
@@ -58,42 +65,109 @@
 
 
 def join_columns(pieces, places):
-    rows, width = pieces[0].shape
+    n, rows, width = pieces.shape
 
     def body(info, ins, outs):
-        for i, piece in enumerate(ins):
+        for i in range(n):
             start = pl.multiple_of(info[i] * width, width)
-            outs[0][:, pl.ds(start, width)] = piece[...]
-
-    out = jax.ShapeDtypeStruct((rows, width * len(pieces)), pieces[0].dtype)
-    return in_vmem(body, "join_columns", jnp.stack(places), pieces, [out])[0]
-
-
-def join_rows(pieces, places):
-    rows, width = pieces[0].shape
-
-    def body(info, ins, outs):
-        for i, piece in enumerate(ins):
-            start = pl.multiple_of(info[i] * rows, rows)
-            outs[0][pl.ds(start, rows), :] = piece[...].astype(F32)
-
-    out = jax.ShapeDtypeStruct((rows * len(pieces), width), F32)
-    return in_vmem(body, "join_rows", jnp.stack(places), pieces, [out])[0]
-
-
-def sum_blocks(terms, axis, n_col, col):
-    shape = terms[0].shape
-    width = shape[axis] // n_col
-    block = (shape[0], width) if axis == 1 else (width, shape[1])
+            outs[0][:, pl.ds(start, width)] = ins[0][i]
+
+    out = jax.ShapeDtypeStruct((rows, width * n), pieces.dtype)
+    return in_vmem(body, "join_columns", jnp.stack(places), [pieces], [out])[0]
+
+
+def cut_columns(values, n_col, col):
+    rows, width = values.shape[0], values.shape[1] // n_col
 
     def body(info, ins, outs):
         for owner in range(n_col):
             start = pl.multiple_of(lax.rem(info[0] - owner + n_col, n_col) * width, width)
-            at = (slice(None), pl.ds(start, width)) if axis == 1 else (pl.ds(start, width), slice(None))
-            outs[0][owner] = sum(t[at].astype(F32) for t in ins).astype(BF)
-
-    out = jax.ShapeDtypeStruct((n_col, *block), BF)
-    return in_vmem(body, "sum_blocks", col[None], terms, [out])[0]
+            outs[0][owner] = ins[0][:, pl.ds(start, width)]
+
+    out = jax.ShapeDtypeStruct((n_col, rows, width), values.dtype)
+    return in_vmem(body, "cut_columns", col[None], [values], [out])[0]
+
+
+def join_rows(pieces, own):
+    seqs, rows, width = pieces[0].shape
+
+    def body(info, ins, outs):
+        for i in range(2):
+            share = info[0] if i == 0 else 1 - info[0]
+            for s in range(seqs):
+                start = pl.multiple_of((2 * s + share) * rows, rows)
+                outs[0][pl.ds(start, rows), :] = ins[i][s].astype(F32)
+
+    out = jax.ShapeDtypeStruct((2 * seqs * rows, width), F32)
+    return in_vmem(body, "join_rows", own[None], list(pieces), [out])[0]
+
+
+def as_chunk(entries, first, brought):
+    return entries, (brought[0], 1 if first == 1 else 0), brought[1]
+
+
+def sum_chunks(chunks, n_col, col, apart):
+    operands, plans = [], []
+    total_rows = 0
+    for entries, got, last in chunks:
+        pieces = []
+        for grad, low, high in entries:
+            pieces.append((len(operands), low, high))
+            operands.append((grad, 0))
+        plans.append((pieces, len(operands), len(operands) + 1))
+        operands += [got, last]
+        total_rows += sum(high - low for _, low, high in entries)
+    width = chunks[0][0][0][0].shape[2] // n_col
+
+    def body(info, ins, outs):
+        for k in range(n_col):
+            if apart:
+                start, target = k * width, outs[k]
+            else:
+                start, target = lax.rem(info[0] - k + n_col, n_col) * width, outs[0].at[k]
+            columns = pl.ds(pl.multiple_of(start, width), width)
+            row = 0
+            for pieces, got, last in plans:
+                inner = 0
+                for at, low, high in pieces:
+                    rows = slice(inner, inner + high - low)
+                    terms = [ins[at][low:high, columns], ins[got][rows, columns], ins[last][rows, columns]]
+                    target[row : row + high - low, :] = sum(t.astype(F32) for t in terms).astype(BF)
+                    row += high - low
+                    inner += high - low
+
+    if apart:
+        outs = [jax.ShapeDtypeStruct((total_rows, width), BF)] * n_col
+    else:
+        outs = [jax.ShapeDtypeStruct((n_col, total_rows, width), BF)]
+    return in_vmem(body, "sum_chunks", col[None], operands, outs)
+
+
+def finish(which, parts, layout, size, width):
+    n = len(parts)
+    operands = [o for part in parts for o, _ in part]
+    outs = []
+    for groups, turned in layout:
+        outs.append(jax.ShapeDtypeStruct((width, groups * n * size) if turned else (n * size, width), F32))
+
+    def body(info, ins, outs):
+        used = 0
+        for i, part in enumerate(parts):
+            refs = ins[used : used + len(part)]
+            used += len(part)
+            row = 0
+            for (groups, turned), target in zip(layout, outs):
+                for g in range(groups):
+                    at = max(x for x in range(len(part)) if part[x][1] <= row)
+                    block = refs[at][row - part[at][1] : row - part[at][1] + size, :].astype(F32)
+                    start = pl.multiple_of(info[i] * size, size)
+                    if turned:
+                        target[:, pl.ds(g * n * size + start, size)] = block.T
+                    else:
+                        target[pl.ds(start, size), :] = block
+                    row += size
+
+    return in_vmem(body, "finish", which, operands, outs)
 
 
 class Plan:
@@ -135,56 +209,44 @@
             return times(left[: self.share], right) + away
         return lax.psum_scatter(times(left, right), "row", scatter_dimension=0, tiled=True)
 
-    def turn(self, t, back=False):
-        pairs = []
-        for r in range(2):
-            for z in range(self.n_col):
-                h, j = divmod(z ^ t, 2)
-                pairs.append((r * self.n_col + z, h * self.n_col + 2 * r + j))
-        return [(b, a) for a, b in pairs] if back else pairs
-
-    def spread(self, values):
+    def sort(self, values):
         width = values.shape[1]
         if self.pair and self.n_col == 4:
-            parts = values.reshape(4, self.share, width)
-            takes = []
-            for t in range(4):
-                h, j = (self.col ^ t) // 2, (self.col ^ t) % 2
-                give = lax.dynamic_index_in_dim(parts, 2 * j + h, 0, keepdims=False)
-                takes.append(lax.ppermute(give, ("row", "col"), self.turn(t)))
-            return tuple(takes)
+            parts = values.reshape(2, 2, self.share, width)
+            keep = lax.dynamic_index_in_dim(parts, self.row, 1, keepdims=False)
+            take = self.swap(lax.dynamic_index_in_dim(parts, 1 - self.row, 1, keepdims=False))
+            ordered = jnp.zeros((4, self.share, width), BF)
+            ordered = lax.dynamic_update_slice_in_dim(ordered, keep, 2 * self.row, axis=0)
+            ordered = lax.dynamic_update_slice_in_dim(ordered, take, 2 - 2 * self.row, axis=0)
+            return ordered
         whole = lax.all_gather(values, "row", axis=0, tiled=True)
         parts = whole.reshape(self.n_col, self.n_row, self.share, width)
-        ordered = lax.dynamic_index_in_dim(parts, self.row, 1, keepdims=False)
-        moved = self.reorder(lax.all_to_all(ordered, "col", 0, 0, tiled=True))
-        return (jnp.transpose(moved, (1, 0, 2)).reshape(self.share, -1),)
+        return lax.dynamic_index_in_dim(parts, self.row, 1, keepdims=False)
+
+    def spread(self, ordered):
+        return lax.all_to_all(ordered, "col", 0, 0, tiled=True)
 
     def spread_end(self, takes):
-        if len(takes) == 1:
-            return takes[0]
-        seen = 2 * self.row + self.col % 2
-        return join_columns(takes, [self.block(t ^ seen) for t in range(4)])
+        if self.share % 128 == 0:
+            return join_columns(takes, [self.block(i) for i in range(self.n_col)])
+        return jnp.transpose(self.reorder(takes), (1, 0, 2)).reshape(self.share, -1)
 
     def collect(self, values):
         width = values.shape[1] // self.n_col
+        if self.share % 128 == 0:
+            blocks = cut_columns(values, self.n_col, self.col)
+        else:
+            blocks = self.reorder(jnp.transpose(values.reshape(self.share, self.n_col, width), (1, 0, 2)))
+        return lax.all_to_all(blocks, "col", 0, 0, tiled=True)
+
+    def collect_end(self, moved):
         if self.pair and self.n_col == 4:
-            seen = 2 * self.row + self.col % 2
-            takes = []
-            for t in range(4):
-                give = lax.dynamic_slice_in_dim(values, self.block(t ^ seen) * width, width, axis=1)
-                takes.append(lax.ppermute(give, ("row", "col"), self.turn(t, back=True)))
-            return tuple(takes)
-        blocks = jnp.transpose(values.reshape(self.share, self.n_col, width), (1, 0, 2))
-        moved = lax.all_to_all(self.reorder(blocks), "col", 0, 0, tiled=True)
-        whole = lax.all_gather(moved, "row", axis=1, tiled=True).reshape(-1, width)
+            keep = lax.dynamic_slice_in_dim(moved, 2 * self.row, 2, axis=0)
+            take = self.swap(lax.dynamic_slice_in_dim(moved, 2 - 2 * self.row, 2, axis=0))
+            return join_rows([keep, take], self.row)
+        whole = lax.all_gather(moved, "row", axis=1, tiled=True).reshape(-1, moved.shape[2])
         rows = whole.shape[0] // self.n_row
-        return (lax.dynamic_slice_in_dim(whole, self.row * rows, rows, axis=0),)
-
-    def collect_end(self, takes):
-        if len(takes) == 1:
-            return takes[0].astype(F32)
-        places = [2 * ((self.col ^ t) % 2) + (self.col ^ t) // 2 for t in range(4)]
-        return join_rows(takes, places)
+        return lax.dynamic_slice_in_dim(whole, self.row * rows, rows, axis=0).astype(F32)
 
 
 def normalize(residual, gain_row, shift_row):
@@ -379,6 +441,10 @@
 LOGSUM_BLOCK = pl.BlockSpec((1, 2, SLOT), lambda i, info: (i, 0, 0))
 
 
+def attention_cost():
+    return pl.CostEstimate(flops=2 * 10**10, bytes_accessed=2**20, transcendentals=0)
+
+
 def small_cost():
     return pl.CostEstimate(flops=0, bytes_accessed=2**16, transcendentals=0)
 
@@ -404,7 +470,7 @@
             scratch_shapes=[pltpu.VMEM((SLOT, LANES), BF), pltpu.VMEM((LANES, SLOT), BF)],
         ),
         compiler_params=pltpu.CompilerParams(vmem_limit_bytes=48 * 2**20),
-        cost_estimate=small_cost(),
+        cost_estimate=attention_cost(),
         name="attend",
     )(info, query, keys, keys)
 
@@ -444,7 +510,7 @@
             ],
         ),
         compiler_params=pltpu.CompilerParams(vmem_limit_bytes=48 * 2**20),
-        cost_estimate=small_cost(),
+        cost_estimate=attention_cost() if causal else small_cost(),
         name="attend_back",
     )(info, query, keys, keys, upstream, logsum)
 
@@ -612,21 +678,39 @@
         return in_vmem(body, "assemble", which, [w[2] for w in self.weights] + list(moved), outs)
 
 
-def pick_others(every, n_col, col):
-    rows = every.shape[0] // n_col
+def split_float(values):
+    high = lax.reduce_precision(values, 8, 7)
+    middle = lax.reduce_precision(values - high, 8, 7)
+    low = values - high - middle
+    parts = jnp.concatenate([high, middle, low], axis=0).astype(BF)
+    parts = jnp.concatenate([parts[:, i : i + 128] for i in range(0, parts.shape[1], 128)], axis=0)
+    return jnp.pad(parts, ((0, -parts.shape[0] % 16), (0, 0)))
+
+
+def join_float(rows, shape):
+    n, width = shape
+    count = width // 128
+    parts = rows[:, : 3 * n * count].reshape(rows.shape[0], count, 3, n, 128).astype(F32)
+    whole = parts[:, :, 0] + (parts[:, :, 1] + parts[:, :, 2])
+    return jnp.moveaxis(whole, 1, 2).reshape(rows.shape[0], n, width)
+
+
+def pick_others(every, rows, n_col, col):
+    width = every.shape[2]
     return pl.pallas_call(
         lambda info, source, target: target.__setitem__(Ellipsis, source[...]),
-        out_shape=jax.ShapeDtypeStruct(((n_col - 1) * rows, every.shape[1]), every.dtype),
+        out_shape=jax.ShapeDtypeStruct(((n_col - 1) * rows, width), every.dtype),
         grid_spec=pltpu.PrefetchScalarGridSpec(
             num_scalar_prefetch=1,
             grid=(n_col - 1,),
             in_specs=[
                 pl.BlockSpec(
-                    (rows, every.shape[1]), lambda k, info: (lax.rem(info[0] - k - 1 + n_col, n_col), 0)
+                    (None, rows, width), lambda k, info: (lax.rem(info[0] - k - 1 + n_col, n_col), 0, 0)
                 )
             ],
-            out_specs=pl.BlockSpec((rows, every.shape[1]), lambda k, info: (k, 0)),
+            out_specs=pl.BlockSpec((rows, width), lambda k, info: (k, 0)),
         ),
+        cost_estimate=small_cost(),
         name="pick_others",
     )(col[None], every)
 
@@ -661,9 +745,12 @@
     def others_by_shift(self, piece):
         return jnp.concatenate([self.plan.shift(piece, k) for k in range(1, self.plan.n_col)], axis=0)
 
-    def others_by_gather(self, piece):
-        every = lax.all_gather(piece, "col", axis=0, tiled=True)
-        return pick_others(every, self.plan.n_col, self.plan.col)
+    def others_by_gather(self, piece, extra):
+        rows = piece.shape[0]
+        if extra is not None:
+            piece = jnp.concatenate([piece, extra], axis=0)
+        every = lax.all_gather(piece, "col", axis=0)
+        return pick_others(every, rows, self.plan.n_col, self.plan.col), every[:, rows:]
 
     def hops(self, others):
         return self.hop(others, 1), self.hop(others, 2)
@@ -683,31 +770,37 @@
         picked = [lax.dynamic_index_in_dim(parts, self.me ^ j, 0, keepdims=False) for j in ORDER]
         return jnp.concatenate(picked, axis=0)
 
-    def reduce_start(self, product, first):
-        return self.hop(product(2, 4) if first == 1 else product(1, 3), first)
-
-    def reduce_next(self, product, first, axis, got):
-        got = jnp.split(got, 2, axis=axis)
-        to_middle, to_base = got if first == 1 else got[::-1]
-        middle = product(1, 2) if first == 1 else product(3, 4)
-        return product(0, 1), to_base, self.hop(middle + to_middle, 3 - first)
-
-    def reduce_col(self, terms, axis, offload):
-        shape = terms[0].shape
-        if offload and all(s % 128 == 0 for s in shape):
-            parts = sum_blocks(terms, axis, self.plan.n_col, self.plan.col)
-            return lax.psum_scatter(parts, "col", scatter_dimension=0, tiled=False)
-        part = sum(t.astype(F32) for t in terms).astype(BF)
-        parts = part.reshape(shape[:axis] + (self.plan.n_col, -1) + shape[axis + 1 :])
-        if offload:
-            parts = self.plan.reorder(jnp.moveaxis(parts, axis, 0))
-            return lax.psum_scatter(parts, "col", scatter_dimension=0, tiled=False)
-        blocks = [lax.index_in_dim(parts, k, axis, keepdims=False) for k in range(self.plan.n_col)]
-        got = [blocks[0]] + [self.plan.shift(blocks[k], -k) for k in range(1, self.plan.n_col)]
-        return sum(g.astype(F32) for g in got).astype(BF)
-
-    def share_parts(self, part):
-        return lax.all_gather(part, "dp", axis=0)
+    def product(self, hidden, model):
+        grad = outer_sum(hidden, model).astype(BF)
+        return grad.reshape(self.n, -1, grad.shape[1])
+
+    def reduce_start(self, entries, first):
+        return self.hop(self.reduce_send(entries, first), first)
+
+    def reduce_send(self, entries, first):
+        a, b = (2, 4) if first == 1 else (1, 3)
+        sends = [grad[a:b, low:high] for grad, low, high in entries]
+        return sends[0] if len(sends) == 1 else jnp.concatenate(sends, axis=1)
+
+    def reduce_next(self, entries, first, got):
+        to_middle, to_base = (0, 1) if first == 1 else (1, 0)
+        place = 1 if first == 1 else 3
+        keeps = [grad[place, low:high] for grad, low, high in entries]
+        middle = keeps[0] if len(keeps) == 1 else jnp.concatenate(keeps, axis=0)
+        return got, self.hop(middle + got[to_middle], 3 - first)
+
+    def plain(self, hidden, model, groups, turned):
+        plan = self.plan
+        grad = outer_sum(hidden, model).astype(BF)
+        parts = grad.reshape(self.n, groups, -1, grad.shape[1])
+        natural = [
+            lax.dynamic_index_in_dim(parts, jnp.array([ORDER.index(j) for j in range(self.n)])[self.me ^ q], 0)
+            for q in range(self.n)
+        ]
+        grad = jnp.moveaxis(jnp.concatenate(natural, axis=0), 1, 0).reshape(grad.shape[0], plan.n_col, -1)
+        grad = lax.psum(plan.reorder(jnp.moveaxis(grad, 1, 0)), "dp")
+        grad = lax.psum_scatter(grad, "col", scatter_dimension=0, tiled=False).astype(F32)
+        return grad.T if turned else grad
 
 
 def total(values, mesh, axes):
@@ -752,6 +845,7 @@
         passages = lax.dynamic_index_in_dim(passage_length, plan.col, keepdims=False)
         valid = (plan.own_positions < answers).astype(F32)[:, None]
 
+        own_norms = jnp.concatenate([model_bias, norm_gain, norm_shift])
         group_one = Group([(0, 3, self_input.reshape(width, -1)), (1, 1, self_output)], n)
         group_two = Group(
             [(0, 1, cross_query), (0, 2, cross_memory.reshape(width, -1)), (1, 1, cross_output)], n
@@ -767,15 +861,18 @@
             w_self, w_self_out = (blocks.whole(w) for w in group_one.weights)
             w_query, w_memory, w_cross_out = (blocks.whole(w) for w in group_two.weights)
             w_expand, w_shrink = (blocks.whole(w) for w in group_three.weights)
-        x_takes = plan.spread(hidden)
+        x_takes = plan.spread(plan.sort(hidden))
+        encoder, cotangent = plan.sort(encoder), plan.sort(cotangent)
+
         if tiled:
             pieces = [group_two.pack(me), group_three.pack(me)]
-            x_takes, pieces = tie(x_takes, pieces)
-            others_two, others_three = (blocks.others_by_gather(p) for p in pieces)
-        own_norms = jnp.concatenate([model_bias, norm_gain, norm_shift])
-        norms = jnp.concatenate(
-            [own_norms] + [plan.shift(own_norms, k) for k in range(1, plan.n_col)], axis=1
-        )
+            others_one, pieces, carried = tie(others_one, pieces, split_float(own_norms))
+            others_two, extra = blocks.others_by_gather(pieces[0], carried)
+            others_three, _ = blocks.others_by_gather(pieces[1], None)
+            norms = plan.reorder(join_float(extra, own_norms.shape))
+        if not tiled:
+            norms = plan.reorder(lax.all_gather(own_norms, "col", axis=0))
+        norms = jnp.moveaxis(norms, 0, 1).reshape(own_norms.shape[0], -1)
         bias_rows, gain_rows, shift_rows = norms[:3], norms[3:6], norms[6:]
 
         head_parts = blocks.weave(head_bias)
@@ -789,21 +886,22 @@
         full_x = plan.gather_rows(own_x)
         packed = (dot(full_x, w_self) + self_bias).astype(BF)
         if tiled:
-            packed, encoder, others_two = tie(packed, encoder, others_two)
+            packed, others_two, encoder, cotangent = tie(packed, others_two, encoder, cotangent)
             over_two = blocks.hops(others_two)
         encoder_takes = plan.spread(encoder)
         mixture, self_logsum = self_attention(plan, packed, answers, n)
         if tiled:
-            mixture, encoder_takes, over_two = tie(mixture, encoder_takes, over_two)
+            mixture, over_two, others_three = tie(mixture, over_two, others_three)
             corner_two = blocks.corner(over_two)
+            over_three = blocks.hops(others_three)
         branch = plan.scatter_product(mixture, w_self_out) + bias_rows[0]
         normed, normal_one, inverse_one = normalize(own_x.astype(F32) + branch, gain_rows[0], shift_rows[0])
         own_first = normed.astype(BF)
         if tiled:
-            own_first, corner_two, others_three, cotangent = tie(
-                own_first, corner_two, others_three, cotangent
-            )
-            over_three = blocks.hops(others_three)
+            own_first, corner_two, over_three, encoder_takes, cotangent = tie(
+                own_first, corner_two, over_three, encoder_takes, cotangent
+            )
+            corner_three = blocks.corner(over_three)
         own_encoder = plan.spread_end(encoder_takes)
         full_encoder = plan.gather_rows(own_encoder)
         full_first = plan.gather_rows(own_first)
@@ -814,10 +912,11 @@
         memory = (dot(full_encoder, w_memory) + memory_bias).astype(BF)
         cross_q = (dot(full_first, w_query) + query_bias).astype(BF)
         cotangent_takes = plan.spread(cotangent)
+        if tiled:
+            cross_q, memory = tie(cross_q, memory)
         recall, cross_logsum = cross_attention(plan, cross_q, memory, answers, passages, n)
         if tiled:
-            recall, over_three, cotangent_takes = tie(recall, over_three, cotangent_takes)
-            corner_three = blocks.corner(over_three)
+            recall, corner_three, cotangent_takes = tie(recall, corner_three, cotangent_takes)
         branch = plan.scatter_product(recall, w_cross_out) + bias_rows[1]
         normed, normal_two, inverse_two = normalize(own_first.astype(F32) + branch, gain_rows[1], shift_rows[1])
         own_second = normed.astype(BF)
@@ -834,30 +933,19 @@
         )
         output_takes = plan.collect((normed * valid).astype(BF))
 
-        def across(*entries):
-            def product(a, b):
-                pieces = [
-                    outer_sum(left[:, a * size : b * size], right).astype(BF).reshape(b - a, size, -1)
-                    for left, size, right in entries
-                ]
-                whole = pieces[0] if len(pieces) == 1 else jnp.concatenate(pieces, axis=1)
-                return whole.reshape(-1, whole.shape[-1])
-
-            return product
-
-        def along(left, right, size):
-            return lambda a, b: outer_sum(left, right[:, a * size : b * size]).astype(BF)
-
         own_cotangent = plan.spread_end(cotangent_takes)
         up_three = own_cotangent.astype(F32) * valid
         resid_three = norm_back(up_three, normal_three, inverse_three, gain_rows[2])
         own_dshrink = resid_three.astype(BF)
         full_dshrink = plan.gather_rows(own_dshrink)
-        of_shrink = across((activated, hidden_part, full_dshrink))
-        got_shrink = blocks.reduce_start(of_shrink, 1)
+        if tiled:
+            of_shrink = [(blocks.product(activated, full_dshrink), 0, hidden_part)]
+            got_shrink = blocks.reduce_start(of_shrink, 1)
         d_expanded = (dot_flip(full_dshrink, w_shrink) * slope.astype(F32)).astype(BF)
-        of_expand = along(full_second, d_expanded, hidden_part)
-        got_expand = blocks.reduce_start(of_expand, 2)
+        (d_expanded,) = tie(d_expanded)
+        if tiled:
+            of_expand = [(blocks.product(d_expanded, full_second), 0, hidden_part)]
+            got_expand = blocks.reduce_start(of_expand, 2)
         up_two = resid_three + plan.scatter_product(d_expanded, w_expand, True)
         resid_two = norm_back(up_two, normal_two, inverse_two, gain_rows[1])
         own_dcross = resid_two.astype(BF)
@@ -866,50 +954,59 @@
         d_cross_q, d_memory = cross_attention_back(
             plan, cross_q, memory, answers, passages, n, cross_logsum, d_recall
         )
-        d_cross_q, d_memory, got_shrink, got_expand, output_takes = tie(
-            d_cross_q, d_memory, got_shrink, got_expand, output_takes
-        )
-        terms_shrink = blocks.reduce_next(of_shrink, 1, 0, got_shrink)
-        terms_expand = blocks.reduce_next(of_expand, 2, 1, got_expand)
+        if tiled:
+            d_cross_q, d_memory, got_shrink, got_expand, output_takes = tie(
+                d_cross_q, d_memory, got_shrink, got_expand, output_takes
+            )
+            chunk_shrink = blocks.reduce_next(of_shrink, 1, got_shrink)
+            chunk_expand = blocks.reduce_next(of_expand, 2, got_expand)
+            of_cross_a = [
+                (blocks.product(d_cross_q, full_first), 0, part),
+                (blocks.product(recall, full_dcross), 0, part),
+            ]
+            of_cross_b = [(blocks.product(d_memory, full_encoder), 0, 2 * part)]
+            got_cross_a = blocks.reduce_start(of_cross_a, 1)
+            got_cross_b = blocks.reduce_start(of_cross_b, 2)
         up_one = resid_two + plan.scatter_product(d_cross_q, w_query, True)
         resid_one = norm_back(up_one, normal_one, inverse_one, gain_rows[0])
         own_dself = resid_one.astype(BF)
         full_dself = plan.gather_rows(own_dself)
         d_mixture = dot_flip(full_dself, w_self_out).astype(BF)
         encoder_grad_takes = plan.collect(plan.scatter_product(d_memory, w_memory, True).astype(BF))
-        of_cross = across(
-            (d_cross_q, part, full_first),
-            (d_memory, 2 * part, full_encoder),
-            (recall, part, full_dcross),
-            (mixture, part, full_dself),
-        )
-        got_cross = blocks.reduce_start(of_cross, 1)
-        d_mixture, terms_shrink, terms_expand = tie(d_mixture, terms_shrink, terms_expand)
-        mine_shrink = blocks.reduce_col(terms_shrink, 1, True)
-        mine_expand = blocks.reduce_col(terms_expand, 0, True)
+        if tiled:
+            (sums,) = sum_chunks(
+                [as_chunk(of_shrink, 1, chunk_shrink), as_chunk(of_expand, 2, chunk_expand)],
+                plan.n_col,
+                plan.col,
+                False,
+            )
+            grad_self_out = blocks.product(mixture, full_dself)
+            d_mixture, sums, got_cross_a, got_cross_b, grad_self_out = tie(
+                d_mixture, sums, got_cross_a, got_cross_b, grad_self_out
+            )
+            mine_hidden = lax.psum_scatter(sums, "col", scatter_dimension=0, tiled=False)
+            chunk_cross_a = blocks.reduce_next(of_cross_a, 1, got_cross_a)
+            chunk_cross_b = blocks.reduce_next(of_cross_b, 2, got_cross_b)
         d_packed = self_attention_back(plan, packed, answers, n, self_logsum, d_mixture)
-        d_packed, got_cross, encoder_grad_takes = tie(d_packed, got_cross, encoder_grad_takes)
-        middle = full_x.shape[1] // 2
-        of_low = along(full_x[:, :middle], d_packed, 3 * part)
-        of_high = along(full_x[:, middle:], d_packed, 3 * part)
-        got_low, got_high = blocks.reduce_start(of_low, 1), blocks.reduce_start(of_high, 2)
-        hidden_takes = plan.collect(
-            (resid_one + plan.scatter_product(d_packed, w_self, True)).astype(BF)
-        )
-        got_low, got_high, got_cross = tie(got_low, got_high, got_cross)
-        terms_cross = blocks.reduce_next(of_cross, 1, 0, got_cross)
-        g_shrink = blocks.share_parts(mine_shrink)
-        g_expand = blocks.share_parts(mine_expand)
-        halves = zip(
-            blocks.reduce_next(of_low, 1, 1, got_low), blocks.reduce_next(of_high, 2, 1, got_high)
-        )
-        terms_self = [jnp.concatenate(h, axis=0) for h in halves]
-        terms_self, terms_cross = tie(terms_self, terms_cross)
-        g_cross = blocks.share_parts(blocks.reduce_col(terms_cross, 1, True))
-        g_self = blocks.share_parts(blocks.reduce_col(terms_self, 0, False))
-        output, g_encoder, g_hidden = (
-            plan.collect_end(t) for t in (output_takes, encoder_grad_takes, hidden_takes)
-        )
+        if tiled:
+            d_packed, chunk_cross_a, chunk_cross_b, mine_hidden, encoder_grad_takes = tie(
+                d_packed, chunk_cross_a, chunk_cross_b, mine_hidden, encoder_grad_takes
+            )
+            grad_self = blocks.product(d_packed, full_x)
+            of_low = [(grad_self, 0, 2 * part)]
+            of_high = [(grad_self, 2 * part, 3 * part), (grad_self_out, 0, part)]
+            send_low, send_high = blocks.reduce_send(of_low, 1), blocks.reduce_send(of_high, 2)
+            send_low, send_high, d_packed, chunk_cross_a, chunk_cross_b = tie(
+                send_low, send_high, d_packed, chunk_cross_a, chunk_cross_b
+            )
+            got_low, got_high = blocks.hop(send_low, 1), blocks.hop(send_high, 2)
+            (sums,) = sum_chunks(
+                [as_chunk(of_cross_a, 1, chunk_cross_a), as_chunk(of_cross_b, 2, chunk_cross_b)],
+                plan.n_col,
+                plan.col,
+                False,
+            )
+            mine_cross = lax.psum_scatter(sums, "col", scatter_dimension=0, tiled=False)
 
         def rows_of(values):
             return jnp.sum(values, axis=0, dtype=F32)
@@ -933,42 +1030,96 @@
                 )
             ]
         )
-        wide = total(wide.reshape(-1), mesh, ("row",))
-        small = total(jnp.concatenate([wide, narrow]), mesh, ("dp",))
-        wide = small[: wide.shape[0]].reshape(9, -1)
-        narrow = total(small[wide.size :], mesh, ("col",))
-        wide = sum(
-            [wide[:, :width]]
-            + [plan.shift(wide[:, k * width : (k + 1) * width], -k) for k in range(1, plan.n_col)]
+        wide = total(wide, mesh, ("row",))
+        wide = plan.reorder(jnp.moveaxis(wide.reshape(9, plan.n_col, width), 1, 0))
+        small = jnp.concatenate([wide.reshape(-1), narrow])
+
+        hidden_grad = (resid_one + plan.scatter_product(d_packed, w_self, True)).astype(BF)
+        if tiled:
+            small = small + blocks.hop(small, 1)
+        hidden_takes = plan.collect(hidden_grad)
+        if not tiled:
+            small = total(small, mesh, ("dp", "col"))
+        if tiled:
+            output, g_encoder = plan.collect_end(output_takes), plan.collect_end(encoder_grad_takes)
+            got_low, got_high, small, output, g_encoder = tie(got_low, got_high, small, output, g_encoder)
+            chunk_low = blocks.reduce_next(of_low, 1, got_low)
+            chunk_high = blocks.reduce_next(of_high, 2, got_high)
+            small = small + blocks.hop(small, 2)
+            ready = lax.all_gather(mine_hidden, "dp", axis=0)
+            g_shrink, g_expand = finish(
+                jnp.arange(n), [[((ready, q), 0)] for q in range(n)], [(1, False), (1, True)], hidden_part, width
+            )
+            g_hidden = plan.collect_end(hidden_takes)
+            chunk_low, chunk_high, mine_cross, g_shrink, g_expand = tie(
+                chunk_low, chunk_high, mine_cross, g_shrink, g_expand
+            )
+            own, *rest = sum_chunks(
+                [as_chunk(of_low, 1, chunk_low), as_chunk(of_high, 2, chunk_high)],
+                plan.n_col,
+                plan.col,
+                True,
+            )
+            arrived = [own] + [plan.shift(r, -1 - k) for k, r in enumerate(rest)]
+            small = small + lax.ppermute(small, "col", [(i, i ^ 1) for i in range(plan.n_col)])
+            arrived, g_hidden = tie(arrived, g_hidden)
+            mine_self = sum(r.astype(F32) for r in arrived).astype(BF)
+            over_self = blocks.hops(mine_self)
+            small = small + lax.ppermute(small, "col", [(i, i ^ 2) for i in range(plan.n_col)])
+            ready = lax.all_gather(mine_cross, "dp", axis=0)
+            g_query, g_cross_out, g_memory = finish(
+                jnp.arange(n),
+                [[((ready, q), 0)] for q in range(n)],
+                [(1, True), (1, False), (2, True)],
+                part,
+                width,
+            )
+            over_self, g_query, g_cross_out, g_memory = tie(over_self, g_query, g_cross_out, g_memory)
+            corner_self = blocks.corner(over_self)
+            g_self, g_self_out = finish(
+                jnp.stack([me ^ j for j in range(n)]),
+                [
+                    [(mine_self, 0)],
+                    [(over_self[0], 0)],
+                    [(over_self[1], 0)],
+                    [(corner_self[0], 0), (corner_self[1], 2 * part)],
+                ],
+                [(3, True), (1, False)],
+                part,
+                width,
+            )
+        else:
+            g_shrink = blocks.plain(activated, full_dshrink, 1, False)
+            g_expand = blocks.plain(d_expanded, full_second, 1, True)
+            g_query = blocks.plain(d_cross_q, full_first, 1, True)
+            g_memory = blocks.plain(d_memory, full_encoder, 2, True)
+            g_cross_out = blocks.plain(recall, full_dcross, 1, False)
+            g_self = blocks.plain(d_packed, full_x, 3, True)
+            g_self_out = blocks.plain(mixture, full_dself, 1, False)
+            output, g_encoder, g_hidden = (
+                plan.collect_end(t) for t in (output_takes, encoder_grad_takes, hidden_takes)
+            )
+
+        own_wide = lax.dynamic_index_in_dim(
+            small[: 9 * plan.n_col * width].reshape(plan.n_col, 9, width), plan.col, keepdims=False
         )
-
-        def turned(grad, count=1):
-            taken = grad.reshape(n, width, count, -1)
-            return jnp.transpose(taken, (1, 2, 0, 3)).reshape(width, count, -1).astype(F32)
-
-        def straight(grad):
-            return grad.reshape(-1, width).astype(F32)
-
-        def straight_turned(grad, count=1):
-            taken = grad.reshape(n, count, -1, width)
-            return jnp.transpose(taken, (3, 1, 0, 2)).reshape(width, count, -1).astype(F32)
-
+        narrow = small[9 * plan.n_col * width :]
         return (
             output,
             g_hidden,
             g_encoder,
-            turned(g_self, 3),
-            straight(g_cross[:, 4 * part :]),
-            straight_turned(g_cross[:, :part])[:, 0],
-            straight_turned(g_cross[:, part : 3 * part], 2),
-            straight(g_cross[:, 3 * part : 4 * part]),
-            turned(g_expand)[:, 0],
-            straight(g_shrink),
+            g_self.reshape(self_input.shape),
+            g_self_out,
+            g_query,
+            g_memory.reshape(cross_memory.shape),
+            g_cross_out,
+            g_expand,
+            g_shrink,
             narrow[: 4 * heads].reshape(4, heads),
             narrow[4 * heads :],
-            wide[:3],
-            wide[3:6],
-            wide[6:],
+            own_wide[:3],
+            own_wide[3:6],
+            own_wide[6:],
         )
 
     return body

time: 735 us -> 673 us (0.916)
  Pallas kernels: 118 us -> 187 us
  starting transfers between devices: 133 us -> 75.1 us
  waiting for transfers between devices: 218 us -> 162 us
  local copies, waits for them, and re-layouts: 47 us -> 70.4 us
  matrix products: 136 us -> 114 us
  blocking collectives: 11.2 us -> 0 us
    ppermute x22 -> x30, waiting for transfers between devices: 121 us -> 81.9 us  [hop(): return lax.ppermute(values, 'dp', [(i, i ^ step) for i in range(self.n)])]
    ppermute x24 -> x2, waiting for transfers between devices: 41.6 us -> 7.06 us  [the longest x1 4.12 us: body(): lax.ppermute(small, 'col', [(i, i ^ 1) for i in range(plan.n_col)])]
    pallas_call x2, Pallas kernels: 32.9 us -> 64.2 us  [attend_back(): pl.pallas_call(functools.partial(backward_kernel, causal), out_shape=out_...]
    ppermute x14 -> x20, starting transfers between devices: 33.6 us -> 3.04 us  [swap(): return lax.ppermute(values, 'row', [(0, 1), (1, 0)])]
    dot_general x24 -> x7, matrix products: 55.6 us -> 28.6 us  [outer_sum(): lax.dot_general(left, right, (((0,), (0,)), ((), ())), preferred_element_...]
    all_to_all x0 -> x6, starting transfers between devices: none -> 27 us  [the longest x3 13.8 us: collect(): return lax.all_to_all(blocks, 'col', 0, 0, tiled=True)]
    ppermute x24 -> x2, starting transfers between devices: 28.3 us -> 2.25 us  [the longest x1 2.18 us: body(): lax.ppermute(small, 'col', [(i, i ^ 2) for i in range(plan.n_col)])]
    all_to_all x0 -> x6, waiting for transfers between devices: none -> 21.8 us  [the longest x3 17.7 us: spread(): return lax.all_to_all(ordered, 'col', 0, 0, tiled=True)]
  transfers between devices with their start and end apart: 85 -> 71, of which waited for: 32 -> 25; matrix products, arithmetic and copies ran while one was open for 22% -> 22% of each run, Pallas kernels for 15% -> 27%
where the time goes in v3:
time: 673 us; the launch traced here: 664 us
  Pallas kernels  187 us (28%)
  waiting for transfers between devices  162 us (24%)
  matrix products  114 us (17%)
  starting transfers between devices  75.1 us (11%)
  local copies, waits for them, and re-layouts  70.4 us (10%)
  other arithmetic  31.8 us (5%)
  between operations  24.1 us (4%)
    ppermute x30, waiting for transfers between devices, hop(): return lax.ppermute(values, 'dp', [(i, i ^ step) for i in range(self.n)])  81.9 us
    pallas_call x21, Pallas kernels, in_vmem(): pl.pallas_call(kernel, out_shape=outs, grid_spec=pltpu.PrefetchScalarGrid...  74.5 us
    pallas_call x2, Pallas kernels, attend_back(): pl.pallas_call(functools.partial(backward_kernel, causal), out_shape=out_...  64.2 us
    dot_general x11, matrix products, dot_flip(): lax.dot_general(left, right, (((1,), (1,)), ((), ())), preferred_element_...  46.2 us
    pallas_call x2, Pallas kernels, attend(): pl.pallas_call(functools.partial(forward_kernel, causal), out_shape=(jax....  41.9 us
    dot_general x10, matrix products, dot(): return jnp.dot(left, right, preferred_element_type=F32)  39 us
    ppermute x30, starting transfers between devices, hop(): return lax.ppermute(values, 'dp', [(i, i ^ step) for i in range(self.n)])  32 us
    dot_general x7, matrix products, outer_sum(): lax.dot_general(left, right, (((0,), (0,)), ((), ())), preferred_element_...  28.6 us
  transfers between devices with their start and end apart: 71, of which 25 were waited for; matrix products, arithmetic and copies ran while one was open for 22% of the time, Pallas kernels for 27%

profile of v3, /device:TPU:0, one launch (start us, length us, event | category | flops | bytes accessed | tf_op | source)
XLA Modules:
  0.0 664.1 jit_solution(11617338838962826982)
XLA Ops:
  45.1 17.7 %all-to-all-done.refs_0_ = bf16[4,512,256]{2,1,0:T(8,128)(2,1)S(1)} async-done(((bf16[4,512,256]{2,1,0:T(8,128)(2,1)}), bf16[4,512,256]{2,1,0:T(8,128)(2,1)S(1)}, u32[]{:S(2)}, u32[]{:S(2)}) %all-to-all-start) | async-done | bytes 1048608 | tf_op jit(solution)/shard_map/all_to_all | solution.py:227
  87.2 5.6 assemble.3
  95.8 5.7 add_convert_fusion.query_ref.key_ref.value_ref
  103.8 18.1 %attend.2 = (bf16[1024,512]{1,0:T(8,128)(2,1)S(1)}, f32[4,2,1024]{2,1,0:T(2,128)S(1)}) custom-call(s32[3]{0:T(128)S(1)} %get-tuple-element.349.info, bf16[1024,1536]{1,0:T(8,128)(2,1)S(1)} %add_convert_fusion.query_ref.key_ref.value_ref, bf16[1024,1536]{1,0:T(8,128)(2,1)S(1)} %add_convert_fusion.query_ref.key_ref.value_ref, ...), custom_call_target="tpu_custom_call" | custom-call | flops 20000000000 | bytes 1048576 | tf_op jit(solution)/shard_map/attend/pallas_call | solution.py:455
  123.5 9.5 %all-gather.11.cloned.1.call-done = bf16[8192,128]{1,0:T(8,128)(2,1)} async-done(((bf16[2048,128]{1,0:T(8,128)(2,1)}), bf16[8192,128]{1,0:T(8,128)(2,1)}) %all-gather.11.cloned.1.call-update) | async-done | bytes 2097168 | tf_op jit(solution)/shard_map/all_gather | solution.py:752
  139.5 4.7 all-to-all-start.1
  154.7 34.7 %collective-permute-done.14.refs_6_ = bf16[1536,128]{1,0:T(8,128)(2,1)S(1)} collective-permute-done((bf16[1536,128]{1,0:T(8,128)(2,1)S(1)}, bf16[1536,128]{1,0:T(8,128)(2,1)S(1)}, u32[]{:S(2)}, u32[]{:S(2)}) %collective-permute-start.14) | collective-permute-done | bytes 393248 | tf_op jit(solution)/shard_map/ppermute | solution.py:726
  200.8 4.8 all-to-all-start.2
  205.6 5.9 assemble.4
  218.5 23.8 %attend.3 = (bf16[1024,512]{1,0:T(8,128)(2,1)S(1)}, f32[4,2,1024]{2,1,0:T(2,128)S(1)}) custom-call(s32[3]{0:T(128)S(1)} %get-tuple-element.350.info, bf16[1024,512]{1,0:T(8,128)(2,1)S(1)} %add_convert_fusion.5.query_ref, bf16[1024,1024]{1,0:T(8,128)(2,1)S(1)} %add_convert_fusion.1.key_ref.value_ref, bf16[1024,1024]{1,0:T(8,128)(2,1)S(1)} %add_convert_fusion.1.key_ref.value_ref), custom_call_target="tpu_custom_call" | custom-call | flops 20000000000 | bytes 1048576 | tf_op jit(solution)/shard_map/attend/pallas_call | solution.py:455
  252.9 9.7 %assemble.5 = (bf16[1024,2048]{1,0:T(8,128)(2,1)}, bf16[2048,1024]{1,0:T(8,128)(2,1)}) custom-call(s32[4]{0:T(128)} %pad_add_fusion.3.info, bf16[256,2048]{1,0:T(8,128)(2,1)} %refs_0_.7, bf16[2048,256]{1,0:T(8,128)(2,1)} %refs_1_.7, bf16[6144,128]{1,0:T(8,128)(2,1)} %pick_others.3.refs_2_, bf16[6144,128]{1,0:T(8,128)(2,1)} %collective-permute-done.16.refs_3_, ...), custom_call_target="tpu_custom_call" | custom-call | bytes 65536 | tf_op jit(solution)/shard_map/assemble/pallas_call | solution.py:48
  262.6 10.2 %multiply_convert_fusion.1 = (bf16[1024,2048]{1,0:T(8,128)(2,1)S(1)}, f32[1024,2048]{1,0:T(8,128)}) fusion(f32[2048]{0:T(1024)S(1)} %bitcast.321, bf16[1024,2048]{1,0:T(8,128)(2,1)} %get-tuple-element.139, bf16[512,1024]{1,0:T(8,128)(2,1)} %collective-permute-done.23, bf16[512,1024]{1,0:T(8,128)(2,1)S(1)} %add_convert_fusion.4), kind=kOutput, calls=%fused_computation.8 | convolution fusion | flops 4311744512 | bytes 18882560 | tf_op jit(solution)/shard_map/dot_general | solution.py:22
  281.0 4.7 fusion.91
  293.5 10.6 %multiply_convert_fusion = bf16[1024,2048]{1,0:T(8,128)(2,1)S(1)} fusion(bf16[2048,1024]{1,0:T(8,128)(2,1)S(1)} %copy-done.75, f32[1024,2048]{1,0:T(8,128)} %get-tuple-element.344, f32[2048]{0:T(1024)S(1)} %bitcast.322, bf16[512,1024]{1,0:T(8,128)(2,1)S(1)} %collective-permute-done.25, bf16[512,1024]{1,0:T(8,128)(2,1)S(1)} %get-tuple-element.276), kind=kOutput, calls=%fused_computation.7 | convolution fusion | flops 4326424576 | bytes 18882560 | tf_op jit(solution)/shard_map/dot_general | solution.py:26
  310.5 5.1 all-to-all-start.3
  315.6 7.5 %convolution_convert_fusion.1 = bf16[2048,1024]{1,0:T(8,128)(2,1)S(1)} fusion(bf16[1024,2048]{1,0:T(8,128)(2,1)} %copy-done.32, bf16[512,1024]{1,0:T(8,128)(2,1)} %collective-permute-done.23, bf16[512,1024]{1,0:T(8,128)(2,1)} %copy-done.53), kind=kOutput, calls=%fused_computation.15 | convolution fusion | flops 4301258752 | bytes 10485760 | tf_op jit(solution)/shard_map/dot_general | solution.py:30
  326.2 5.2 convolution_convert_fusion.2
  334.5 5.1 multiply_reduce_fusion.1
  345.7 37.2 %attend_back.2 = (bf16[1024,512]{1,0:T(8,128)(2,1)S(1)}, bf16[1024,1024]{1,0:T(8,128)(2,1)S(1)}) custom-call(s32[3]{0:T(128)S(1)} %get-tuple-element.350.info, bf16[1024,512]{1,0:T(8,128)(2,1)S(1)} %copy-done.4, bf16[1024,1024]{1,0:T(8,128)(2,1)} %copy-done, bf16[1024,1024]{1,0:T(8,128)(2,1)} %copy-done, ...), custom_call_target="tpu_custom_call" | custom-call | bytes 65536 | tf_op jit(solution)/shard_map/attend_back/pallas_call | solution.py:490
  407.8 5.0 collective-permute-done.33.refs_5_
  415.6 4.9 sum_chunks.3
  428.5 8.1 %collective-permute-done.35.refs_5_ = bf16[2,256,1024]{2,1,0:T(8,128)(2,1)} collective-permute-done((bf16[2,256,1024]{2,1,0:T(8,128)(2,1)}, bf16[2,256,1024]{2,1,0:T(8,128)(2,1)}, u32[]{:S(2)}, u32[]{:S(2)}) %collective-permute-start.35) | collective-permute-done | bytes 1048608 | tf_op jit(solution)/shard_map/ppermute | solution.py:726
  458.5 5.2 all-to-all-start.4
  469.9 27.0 %attend_back.3 = bf16[1024,1536]{1,0:T(8,128)(2,1)S(1)} custom-call(s32[3]{0:T(128)S(1)} %copy-done.10, bf16[1024,1536]{1,0:T(8,128)(2,1)} %copy-done.12, bf16[1024,1536]{1,0:T(8,128)(2,1)} %copy-done.12, bf16[1024,1536]{1,0:T(8,128)(2,1)} %copy-done.12, bf16[1024,512]{1,0:T(8,128)(2,1)S(1)} %copy-done.11, f32[4,2,1024]{2,1,0:T(2,128)S(1)} %get-tuple-element.150.logsum_ref), custom_call_target="tpu_custom_call" | custom-call | flops 20000000000 | bytes 1048576 | tf_op jit(solution)/shard_map/attend_back/pallas_call | solution.py:490
  508.8 5.6 convolution_convert_fusion
  523.1 5.3 fusion.16
  532.9 6.0 add_convert_fusion.2.refs_0_
  545.7 12.3 %collective-permute-done.42 = f32[13312]{0:T(1024)} collective-permute-done((f32[13312]{0:T(1024)S(1)}, f32[13312]{0:T(1024)}, u32[]{:S(2)}, u32[]{:S(2)}) %collective-permute-start.42) | collective-permute-done | bytes 53280 | tf_op jit(solution)/shard_map/ppermute | solution.py:726
  567.5 4.6 finish.3
  578.5 9.7 %reduce-scatter.5.cloned.1.call-done = bf16[1,512,256]{2,1,0:T(8,128)(2,1)} async-done(((bf16[4,512,256]{2,1,0:T(8,128)(2,1)}), bf16[1,512,256]{2,1,0:T(8,128)(2,1)}) %reduce-scatter.5.cloned.1.call-update) | async-done | bytes 262160 | tf_op jit(solution)/shard_map/reduce_scatter | solution.py:1009
  601.3 17.4 %collective-permute-done.48 = bf16[512,256]{1,0:T(8,128)(2,1)S(1)} collective-permute-done((bf16[512,256]{1,0:T(8,128)(2,1)}, bf16[512,256]{1,0:T(8,128)(2,1)S(1)}, u32[]{:S(2)}, u32[]{:S(2)}) %collective-permute-start.48) | collective-permute-done | bytes 262176 | tf_op jit(solution)/shard_map/ppermute | solution.py:190
  622.2 6.7 %collective-permute-done.56 = f32[13312]{0:T(1024)S(1)} collective-permute-done((f32[13312]{0:T(1024)S(1)}, f32[13312]{0:T(1024)S(1)}, u32[]{:S(2)}, u32[]{:S(2)}) %collective-permute-start.56) | collective-permute-done | bytes 53280 | tf_op jit(solution)/shard_map/ppermute | solution.py:726
  (510 shorter events, 296.4 us)
Async XLA Ops:
  27.0 35.8 %all-to-all-start = ((bf16[4,512,256]{2,1,0:T(8,128)(2,1)}), bf16[4,512,256]{2,1,0:T(8,128)(2,1)S(1)}, u32[]{:S(2)}, u32[]{:S(2)}) async-start(bf16[4,512,256]{2,1,0:T(8,128)(2,1)} %constant_dynamic-update-slice_fusion.2), calls=%async_computation | async-start | bytes 2097152 | tf_op jit(solution)/shard_map/all_to_all | solution.py:227
  30.7 62.2 %all-gather.9.cloned.1.call-start = ((), (), s32[]{:S(2)}) async-start(), calls=%async_computation.10 | async-start | bytes 1392640 | tf_op jit(solution)/shard_map/all_gather | solution.py:752
  39.0 93.9 %all-gather.11.cloned.1.call-start = ((), (), s32[]{:S(2)}) async-start(), calls=%async_computation.11 | async-start | bytes 2621440 | tf_op jit(solution)/shard_map/all_gather | solution.py:752
  40.0 39.1 %collective-permute-start.10 = (bf16[2,512,256]{2,1,0:T(8,128)(2,1)}, bf16[2,512,256]{2,1,0:T(8,128)(2,1)}, u32[]{:S(2)}, u32[]{:S(2)}) collective-permute-start(bf16[2,512,256]{2,1,0:T(8,128)(2,1)} %dynamic-slice_bitcast_fusion), channel_id=1, source_target_pairs={{0,4},{4,0},{1,5},{5,1},{2,6},{6,2},{3,7},{7,3},{8,12},{12,8},{9,1... | collective-permute-start | bytes 1572872 | tf_op jit(solution)/shard_map/ppermute | solution.py:186
  40.8 40.1 %collective-permute-start.9 = (bf16[2,512,256]{2,1,0:T(8,128)(2,1)}, bf16[2,512,256]{2,1,0:T(8,128)(2,1)S(1)}, u32[]{:S(2)}, u32[]{:S(2)}) collective-permute-start(bf16[2,512,256]{2,1,0:T(8,128)(2,1)} %dynamic-slice_bitcast_fusion.1), channel_id=1, source_target_pairs={{0,4},{4,0},{1,5},{5,1},{2,6},{6,2},{3,7},{7,3},{8,12},{12,8},{9,1... | collective-permute-start | bytes 1572872 | tf_op jit(solution)/shard_map/ppermute | solution.py:186
  101.5 34.8 %collective-permute-start.11 = (bf16[3072,128]{1,0:T(8,128)(2,1)S(1)}, bf16[3072,128]{1,0:T(8,128)(2,1)}, u32[]{:S(2)}, u32[]{:S(2)}) collective-permute-start(bf16[3072,128]{1,0:T(8,128)(2,1)S(1)} %copy-done.40), channel_id=1, source_target_pairs={{0,8},{8,0},{16,24},{24,16},{1,9},{9,1},{17,25},{25,17},{2,10},{10... | collective-permute-start | bytes 2359304 | tf_op jit(solution)/shard_map/ppermute | solution.py:726
  102.2 34.1 %collective-permute-start.12 = (bf16[3072,128]{1,0:T(8,128)(2,1)S(1)}, bf16[3072,128]{1,0:T(8,128)(2,1)}, u32[]{:S(2)}, u32[]{:S(2)}) collective-permute-start(bf16[3072,128]{1,0:T(8,128)(2,1)S(1)} %copy-done.40), channel_id=1, source_target_pairs={{0,16},{8,24},{16,0},{24,8},{1,17},{9,25},{17,1},{25,9},{2,18},{10... | collective-permute-start | bytes 2359304 | tf_op jit(solution)/shard_map/ppermute | solution.py:726
  139.5 51.2 %all-to-all-start.1 = ((bf16[4,512,256]{2,1,0:T(8,128)(2,1)}), bf16[4,512,256]{2,1,0:T(8,128)(2,1)}, u32[]{:S(2)}, u32[]{:S(2)}) async-start(bf16[4,512,256]{2,1,0:T(8,128)(2,1)} %copy-done.37), calls=%async_computation.1 | async-start | bytes 2097152 | tf_op jit(solution)/shard_map/all_to_all | solution.py:227
  144.2 46.5 %collective-permute-start.16 = (bf16[6144,128]{1,0:T(8,128)(2,1)S(1)}, bf16[6144,128]{1,0:T(8,128)(2,1)}, u32[]{:S(2)}, u32[]{:S(2)}) collective-permute-start(bf16[6144,128]{1,0:T(8,128)(2,1)S(1)} %copy-done.25), channel_id=1, source_target_pairs={{0,8},{8,0},{16,24},{24,16},{1,9},{9,1},{17,25},{25,17},{2,10},{10... | collective-permute-start | bytes 4718600 | tf_op jit(solution)/shard_map/ppermute | solution.py:726
  145.8 44.9 %collective-permute-start.17 = (bf16[6144,128]{1,0:T(8,128)(2,1)S(1)}, bf16[6144,128]{1,0:T(8,128)(2,1)}, u32[]{:S(2)}, u32[]{:S(2)}) collective-permute-start(bf16[6144,128]{1,0:T(8,128)(2,1)S(1)} %copy-done.25), channel_id=1, source_target_pairs={{0,16},{8,24},{16,0},{24,8},{1,17},{9,25},{17,1},{25,9},{2,18},{10... | collective-permute-start | bytes 4718600 | tf_op jit(solution)/shard_map/ppermute | solution.py:726
  148.3 41.1 %collective-permute-start.14 = (bf16[1536,128]{1,0:T(8,128)(2,1)S(1)}, bf16[1536,128]{1,0:T(8,128)(2,1)S(1)}, u32[]{:S(2)}, u32[]{:S(2)}) collective-permute-start(bf16[1536,128]{1,0:T(8,128)(2,1)S(1)} %slice.302), channel_id=1, source_target_pairs={{0,8},{8,0},{16,24},{24,16},{1,9},{9,1},{17,25},{25,17},{2,10},{10... | collective-permute-start | bytes 1179656 | tf_op jit(solution)/shard_map/ppermute | solution.py:726
  150.0 40.7 %collective-permute-start.15 = (bf16[1536,128]{1,0:T(8,128)(2,1)S(1)}, bf16[1536,128]{1,0:T(8,128)(2,1)}, u32[]{:S(2)}, u32[]{:S(2)}) collective-permute-start(bf16[1536,128]{1,0:T(8,128)(2,1)S(1)} %slice.303), channel_id=1, source_target_pairs={{0,16},{8,24},{16,0},{24,8},{1,17},{9,25},{17,1},{25,9},{2,18},{10... | collective-permute-start | bytes 1179656 | tf_op jit(solution)/shard_map/ppermute | solution.py:726
  196.4 46.0 %collective-permute-start.20 = (bf16[3072,128]{1,0:T(8,128)(2,1)}, bf16[3072,128]{1,0:T(8,128)(2,1)}, u32[]{:S(2)}, u32[]{:S(2)}) collective-permute-start(bf16[3072,128]{1,0:T(8,128)(2,1)} %slice.306), channel_id=1, source_target_pairs={{0,8},{8,0},{16,24},{24,16},{1,9},{9,1},{17,25},{25,17},{2,10},{10... | collective-permute-start | bytes 2359304 | tf_op jit(solution)/shard_map/ppermute | solution.py:726
  199.4 43.0 %collective-permute-start.21 = (bf16[3072,128]{1,0:T(8,128)(2,1)}, bf16[3072,128]{1,0:T(8,128)(2,1)}, u32[]{:S(2)}, u32[]{:S(2)}) collective-permute-start(bf16[3072,128]{1,0:T(8,128)(2,1)} %slice.307), channel_id=1, source_target_pairs={{0,16},{8,24},{16,0},{24,8},{1,17},{9,25},{17,1},{25,9},{2,18},{10... | collective-permute-start | bytes 2359304 | tf_op jit(solution)/shard_map/ppermute | solution.py:726
  200.8 41.6 %all-to-all-start.2 = ((bf16[4,512,256]{2,1,0:T(8,128)(2,1)}), bf16[4,512,256]{2,1,0:T(8,128)(2,1)S(1)}, u32[]{:S(2)}, u32[]{:S(2)}) async-start(bf16[4,512,256]{2,1,0:T(8,128)(2,1)} %constant_dynamic-update-slice_fusion), calls=%async_computation.2 | async-start | bytes 2097152 | tf_op jit(solution)/shard_map/all_to_all | solution.py:227
  310.5 72.4 %all-to-all-start.3 = ((bf16[4,512,256]{2,1,0:T(8,128)(2,1)}), bf16[4,512,256]{2,1,0:T(8,128)(2,1)}, u32[]{:S(2)}, u32[]{:S(2)}) async-start(bf16[4,512,256]{2,1,0:T(8,128)(2,1)} %cut_columns.3), calls=%async_computation.3 | async-start | bytes 2097152 | tf_op jit(solution)/shard_map/all_to_all | solution.py:240
  315.6 187.2 %reduce-scatter.3.cloned.1.call-start = ((), (), s32[]{:S(2)}) async-start(), calls=%async_computation.8 | async-start | bytes 2621440 | tf_op jit(solution)/shard_map/reduce_scatter | solution.py:987
  325.9 57.0 %collective-permute-start.29 = (bf16[2,512,1024]{2,1,0:T(8,128)(2,1)}, bf16[2,512,1024]{2,1,0:T(8,128)(2,1)}, u32[]{:S(2)}, u32[]{:S(2)}) collective-permute-start(bf16[2,512,1024]{2,1,0:T(8,128)(2,1)} %bitcast.33), channel_id=1, source_target_pairs={{0,16},{8,24},{16,0},{24,8},{1,17},{9,25},{17,1},{25,9},{2,18},{10... | collective-permute-start | bytes 6291464 | tf_op jit(solution)/shard_map/ppermute | solution.py:726
  334.2 48.7 %collective-permute-start.28 = (bf16[2,512,1024]{2,1,0:T(8,128)(2,1)}, bf16[2,512,1024]{2,1,0:T(8,128)(2,1)}, u32[]{:S(2)}, u32[]{:S(2)}) collective-permute-start(bf16[2,512,1024]{2,1,0:T(8,128)(2,1)} %bitcast.32), channel_id=1, source_target_pairs={{0,8},{8,0},{16,24},{24,16},{1,9},{9,1},{17,25},{25,17},{2,10},{10... | collective-permute-start | bytes 6291464 | tf_op jit(solution)/shard_map/ppermute | solution.py:726
  399.7 37.0 %collective-permute-start.35 = (bf16[2,256,1024]{2,1,0:T(8,128)(2,1)}, bf16[2,256,1024]{2,1,0:T(8,128)(2,1)}, u32[]{:S(2)}, u32[]{:S(2)}) collective-permute-start(bf16[2,256,1024]{2,1,0:T(8,128)(2,1)} %bitcast.40), channel_id=1, source_target_pairs={{0,16},{8,24},{16,0},{24,8},{1,17},{9,25},{17,1},{25,9},{2,18},{10... | collective-permute-start | bytes 3145736 | tf_op jit(solution)/shard_map/ppermute | solution.py:726
  403.5 33.1 %collective-permute-start.34 = (bf16[2,256,1024]{2,1,0:T(8,128)(2,1)}, bf16[2,256,1024]{2,1,0:T(8,128)(2,1)}, u32[]{:S(2)}, u32[]{:S(2)}) collective-permute-start(bf16[2,256,1024]{2,1,0:T(8,128)(2,1)} %pad_maximum_fusion.18), channel_id=1, source_target_pairs={{0,8},{8,0},{16,24},{24,16},{1,9},{9,1},{17,25},{25,17},{2,10},{10... | collective-permute-start | bytes 3145736 | tf_op jit(solution)/shard_map/ppermute | solution.py:726
  412.8 39.4 %collective-permute-start.38 = (f32[512,1024]{1,0:T(8,128)}, f32[512,1024]{1,0:T(8,128)}, u32[]{:S(2)}, u32[]{:S(2)}) collective-permute-start(f32[512,1024]{1,0:T(8,128)} %fusion.27), channel_id=1, source_target_pairs={{0,4},{4,0},{1,5},{5,1},{2,6},{6,2},{3,7},{7,3},{8,12},{12,8},{9,1... | collective-permute-start | bytes 6291464 | tf_op jit(solution)/shard_map/ppermute | solution.py:186
  452.2 51.5 %collective-permute-start.43 = (bf16[2,512,256]{2,1,0:T(8,128)(2,1)}, bf16[2,512,256]{2,1,0:T(8,128)(2,1)}, u32[]{:S(2)}, u32[]{:S(2)}) collective-permute-start(bf16[2,512,256]{2,1,0:T(8,128)(2,1)} %get-tuple-element.288), channel_id=1, source_target_pairs={{0,4},{4,0},{1,5},{5,1},{2,6},{6,2},{3,7},{7,3},{8,12},{12,8},{9,1... | collective-permute-start | bytes 1572872 | tf_op jit(solution)/shard_map/ppermute | solution.py:186
  458.5 44.3 %all-to-all-start.4 = ((bf16[4,512,256]{2,1,0:T(8,128)(2,1)}), bf16[4,512,256]{2,1,0:T(8,128)(2,1)}, u32[]{:S(2)}, u32[]{:S(2)}) async-start(bf16[4,512,256]{2,1,0:T(8,128)(2,1)} %cut_columns.4), calls=%async_computation.5 | async-start | bytes 2097152 | tf_op jit(solution)/shard_map/all_to_all | solution.py:240
  463.7 103.3 %all-gather.13.cloned.1.call-start = ((), (), s32[]{:S(2)}) async-start(), calls=%async_computation.12 | async-start | bytes 2621440 | tf_op jit(solution)/shard_map/all_gather | solution.py:1049
  465.9 36.9 %collective-permute-start.37 = (bf16[256,1024]{1,0:T(8,128)(2,1)}, bf16[256,1024]{1,0:T(8,128)(2,1)}, u32[]{:S(2)}, u32[]{:S(2)}) collective-permute-start(bf16[256,1024]{1,0:T(8,128)(2,1)} %slice_add_fusion.3), channel_id=1, source_target_pairs={{0,8},{8,0},{16,24},{24,16},{1,9},{9,1},{17,25},{25,17},{2,10},{10... | collective-permute-start | bytes 1572872 | tf_op jit(solution)/shard_map/ppermute | solution.py:726
  502.8 85.4 %reduce-scatter.5.cloned.1.call-start = ((), (), s32[]{:S(2)}) async-start(), calls=%async_computation.9 | async-start | bytes 1310720 | tf_op jit(solution)/shard_map/reduce_scatter | solution.py:1009
  518.1 40.7 %collective-permute-start.44 = (bf16[2,512,256]{2,1,0:T(8,128)(2,1)}, bf16[2,512,256]{2,1,0:T(8,128)(2,1)}, u32[]{:S(2)}, u32[]{:S(2)}) collective-permute-start(bf16[2,512,256]{2,1,0:T(8,128)(2,1)} %get-tuple-element.286), channel_id=1, source_target_pairs={{0,4},{4,0},{1,5},{5,1},{2,6},{6,2},{3,7},{7,3},{8,12},{12,8},{9,1... | collective-permute-start | bytes 1572872 | tf_op jit(solution)/shard_map/ppermute | solution.py:186
  520.1 41.4 %collective-permute-start.39 = (bf16[2,256,1024]{2,1,0:T(8,128)(2,1)}, bf16[2,256,1024]{2,1,0:T(8,128)(2,1)}, u32[]{:S(2)}, u32[]{:S(2)}) collective-permute-start(bf16[2,256,1024]{2,1,0:T(8,128)(2,1)} %slice.403), channel_id=1, source_target_pairs={{0,8},{8,0},{16,24},{24,16},{1,9},{9,1},{17,25},{25,17},{2,10},{10... | collective-permute-start | bytes 3145736 | tf_op jit(solution)/shard_map/ppermute | solution.py:726
  521.6 39.9 %collective-permute-start.40 = (bf16[2,256,1024]{2,1,0:T(8,128)(2,1)}, bf16[2,256,1024]{2,1,0:T(8,128)(2,1)}, u32[]{:S(2)}, u32[]{:S(2)}) collective-permute-start(bf16[2,256,1024]{2,1,0:T(8,128)(2,1)} %pad_maximum_fusion.19), channel_id=1, source_target_pairs={{0,16},{8,24},{16,0},{24,8},{1,17},{9,25},{17,1},{25,9},{2,18},{10... | collective-permute-start | bytes 3145736 | tf_op jit(solution)/shard_map/ppermute | solution.py:726
  541.1 47.1 %all-to-all-start.5 = ((bf16[4,512,256]{2,1,0:T(8,128)(2,1)}), bf16[4,512,256]{2,1,0:T(8,128)(2,1)S(1)}, u32[]{:S(2)}, u32[]{:S(2)}) async-start(bf16[4,512,256]{2,1,0:T(8,128)(2,1)} %cut_columns.5), calls=%async_computation.7 | async-start | bytes 2097152 | tf_op jit(solution)/shard_map/all_to_all | solution.py:240
  544.7 93.6 %all-gather.15.cloned.1.call-start = ((), (), s32[]{:S(2)}) async-start(), calls=%async_computation.13 | async-start | bytes 1310720 | tf_op jit(solution)/shard_map/all_gather | solution.py:1069
  (127 other events, 1322.5 us)
Sparse Core Ops, SparseCore 0:
  39.2 46.1 all-gather.8
  87.5 45.4 all-gather.10
  436.8 55.7 reduce-scatter.2
  502.9 45.6 all-gather.12
  550.9 37.3 reduce-scatter.4
  589.9 24.7 all-gather.14

commit v4 on v3

--- a/solution.py
+++ b/solution.py
@@ -148,7 +148,8 @@
     operands = [o for part in parts for o, _ in part]
     outs = []
     for groups, turned in layout:
-        outs.append(jax.ShapeDtypeStruct((width, groups * n * size) if turned else (n * size, width), F32))
+        shape = (width, groups, n * size) if groups > 1 else (width, n * size)
+        outs.append(jax.ShapeDtypeStruct(shape if turned else (n * size, width), F32))
 
     def body(info, ins, outs):
         used = 0
@@ -161,8 +162,10 @@
                     at = max(x for x in range(len(part)) if part[x][1] <= row)
                     block = refs[at][row - part[at][1] : row - part[at][1] + size, :].astype(F32)
                     start = pl.multiple_of(info[i] * size, size)
-                    if turned:
-                        target[:, pl.ds(g * n * size + start, size)] = block.T
+                    if turned and groups > 1:
+                        target[:, g, pl.ds(start, size)] = block.T
+                    elif turned:
+                        target[:, pl.ds(start, size)] = block.T
                     else:
                         target[pl.ds(start, size), :] = block
                     row += size
@@ -232,11 +235,15 @@
         return jnp.transpose(self.reorder(takes), (1, 0, 2)).reshape(self.share, -1)
 
     def collect(self, values):
+        return self.deal(self.cut(values))
+
+    def cut(self, values):
         width = values.shape[1] // self.n_col
         if self.share % 128 == 0:
-            blocks = cut_columns(values, self.n_col, self.col)
-        else:
-            blocks = self.reorder(jnp.transpose(values.reshape(self.share, self.n_col, width), (1, 0, 2)))
+            return cut_columns(values, self.n_col, self.col)
+        return self.reorder(jnp.transpose(values.reshape(self.share, self.n_col, width), (1, 0, 2)))
+
+    def deal(self, blocks):
         return lax.all_to_all(blocks, "col", 0, 0, tiled=True)
 
     def collect_end(self, moved):
@@ -643,39 +650,51 @@
         out = jax.ShapeDtypeStruct((self.rows, 128), BF)
         return in_vmem(body, "pack", me[None], [w[2] for w in self.weights], [out])[0]
 
-    def assemble(self, me, n_col, moved):
-        half = self.rows * (n_col - 1) // 2
-        count_w = len(self.weights)
+    def outputs(self, n_col):
         outs = []
         for axis, groups, local in self.weights:
             shape = (local.shape[0] * n_col, local.shape[1]) if axis == 0 else (local.shape[0], local.shape[1] * n_col)
             outs.append(jax.ShapeDtypeStruct(shape, BF))
-
-        def body(info, ins, outs):
-            local_refs, moved_refs = ins[:count_w], ins[count_w:]
-            for at, (row, tall, count) in enumerate(self.plans):
-                axis = self.weights[at][0]
-                width = self.weights[at][2].shape[1]
-                for place, j in enumerate(ORDER):
-                    for k in range(n_col):
-                        for block in range(count):
-                            if k == 0:
-                                value = self.local_block(local_refs[at], at, info[j], block)
-                            else:
-                                start = (k - 1) * self.rows + row + block * tall
-                                ref = moved_refs[j]
-                                if j == 3 and start >= half:
-                                    ref, start = moved_refs[4], start - half
-                                value = ref[start : start + tall, :]
-                            if axis == 0:
-                                column = (place * count + block) * 128
-                                outs[at][k * tall : (k + 1) * tall, column : column + 128] = value
-                            else:
-                                column = k * width + block * 128
-                                outs[at][place * tall : (place + 1) * tall, column : column + 128] = value
-
-        which = jnp.stack([me ^ j for j in range(self.n)])
-        return in_vmem(body, "assemble", which, [w[2] for w in self.weights] + list(moved), outs)
+        return outs
+
+    def fill(self, info, n_col, local_refs, moved_refs, outs):
+        half = self.rows * (n_col - 1) // 2
+        for at, (row, tall, count) in enumerate(self.plans):
+            axis = self.weights[at][0]
+            width = self.weights[at][2].shape[1]
+            for place, j in enumerate(ORDER):
+                for k in range(n_col):
+                    for block in range(count):
+                        if k == 0:
+                            value = self.local_block(local_refs[at], at, info[j], block)
+                        else:
+                            start = (k - 1) * self.rows + row + block * tall
+                            ref = moved_refs[j]
+                            if j == 3 and start >= half:
+                                ref, start = moved_refs[4], start - half
+                            value = ref[start : start + tall, :]
+                        if axis == 0:
+                            column = (place * count + block) * 128
+                            outs[at][k * tall : (k + 1) * tall, column : column + 128] = value
+                        else:
+                            column = k * width + block * 128
+                            outs[at][place * tall : (place + 1) * tall, column : column + 128] = value
+
+
+def assemble(me, n_col, *groups):
+    operands, outs = [], []
+    for group, moved in groups:
+        operands += [w[2] for w in group.weights] + list(moved)
+        outs += group.outputs(n_col)
+
+    def body(info, ins, outs):
+        for group, moved in groups:
+            count = len(group.weights)
+            group.fill(info, n_col, ins[:count], ins[count : count + len(moved)], outs[:count])
+            ins, outs = ins[count + len(moved) :], outs[count:]
+
+    which = jnp.stack([me ^ j for j in range(len(ORDER))])
+    return in_vmem(body, "assemble", which, operands, outs)
 
 
 def split_float(values):
@@ -695,7 +714,7 @@
     return jnp.moveaxis(whole, 1, 2).reshape(rows.shape[0], n, width)
 
 
-def pick_others(every, rows, n_col, col):
+def pick_others(every, at, rows, n_col, col):
     width = every.shape[2]
     return pl.pallas_call(
         lambda info, source, target: target.__setitem__(Ellipsis, source[...]),
@@ -705,7 +724,7 @@
             grid=(n_col - 1,),
             in_specs=[
                 pl.BlockSpec(
-                    (None, rows, width), lambda k, info: (lax.rem(info[0] - k - 1 + n_col, n_col), 0, 0)
+                    (None, rows, width), lambda k, info: (lax.rem(info[0] - k - 1 + n_col, n_col), at, 0)
                 )
             ],
             out_specs=pl.BlockSpec((rows, width), lambda k, info: (k, 0)),
@@ -745,12 +764,14 @@
     def others_by_shift(self, piece):
         return jnp.concatenate([self.plan.shift(piece, k) for k in range(1, self.plan.n_col)], axis=0)
 
-    def others_by_gather(self, piece, extra):
-        rows = piece.shape[0]
+    def others_by_gather(self, piece, count, extra):
+        total_rows = piece.shape[0]
         if extra is not None:
             piece = jnp.concatenate([piece, extra], axis=0)
         every = lax.all_gather(piece, "col", axis=0)
-        return pick_others(every, rows, self.plan.n_col, self.plan.col), every[:, rows:]
+        rows = total_rows // count
+        picked = [pick_others(every, i, rows, self.plan.n_col, self.plan.col) for i in range(count)]
+        return picked, every[:, total_rows:]
 
     def hops(self, others):
         return self.hop(others, 1), self.hop(others, 2)
@@ -851,24 +872,27 @@
             [(0, 1, cross_query), (0, 2, cross_memory.reshape(width, -1)), (1, 1, cross_output)], n
         )
         group_three = Group([(0, 1, expand_weight), (1, 1, shrink_weight)], n)
-        tiled = group_one.fits() and group_two.fits() and group_three.fits()
+        group_expand, group_shrink = Group([(0, 1, expand_weight)], n), Group([(1, 1, shrink_weight)], n)
+        tiled = plan.pair and all(g.fits() for g in (group_one, group_two, group_expand, group_shrink))
         if tiled:
             others_one = blocks.others_by_shift(group_one.pack(me))
+            hidden = plan.sort(hidden)
             over_one = blocks.hops(others_one)
             corner_one = blocks.corner(over_one)
-            w_self, w_self_out = group_one.assemble(me, plan.n_col, (others_one, *over_one, *corner_one))
+            w_self, w_self_out = assemble(me, plan.n_col, (group_one, (others_one, *over_one, *corner_one)))
         else:
+            hidden = plan.sort(hidden)
             w_self, w_self_out = (blocks.whole(w) for w in group_one.weights)
             w_query, w_memory, w_cross_out = (blocks.whole(w) for w in group_two.weights)
-            w_expand, w_shrink = (blocks.whole(w) for w in group_three.weights)
-        x_takes = plan.spread(plan.sort(hidden))
+            w_expand, w_shrink = (blocks.whole(g.weights[0]) for g in (group_expand, group_shrink))
+        x_takes = plan.spread(hidden)
         encoder, cotangent = plan.sort(encoder), plan.sort(cotangent)
 
         if tiled:
             pieces = [group_two.pack(me), group_three.pack(me)]
             others_one, pieces, carried = tie(others_one, pieces, split_float(own_norms))
-            others_two, extra = blocks.others_by_gather(pieces[0], carried)
-            others_three, _ = blocks.others_by_gather(pieces[1], None)
+            (others_two,), extra = blocks.others_by_gather(pieces[0], 1, carried)
+            (others_a, others_b), _ = blocks.others_by_gather(pieces[1], 2, None)
             norms = plan.reorder(join_float(extra, own_norms.shape))
         if not tiled:
             norms = plan.reorder(lax.all_gather(own_norms, "col", axis=0))
@@ -891,39 +915,46 @@
         encoder_takes = plan.spread(encoder)
         mixture, self_logsum = self_attention(plan, packed, answers, n)
         if tiled:
-            mixture, over_two, others_three = tie(mixture, over_two, others_three)
+            mixture, over_two = tie(mixture, over_two)
             corner_two = blocks.corner(over_two)
-            over_three = blocks.hops(others_three)
         branch = plan.scatter_product(mixture, w_self_out) + bias_rows[0]
+        if tiled:
+            branch, others_a = tie(branch, others_a)
+            over_a = blocks.hops(others_a)
         normed, normal_one, inverse_one = normalize(own_x.astype(F32) + branch, gain_rows[0], shift_rows[0])
         own_first = normed.astype(BF)
         if tiled:
-            own_first, corner_two, over_three, encoder_takes, cotangent = tie(
-                own_first, corner_two, over_three, encoder_takes, cotangent
-            )
-            corner_three = blocks.corner(over_three)
+            own_first, corner_two, over_a, others_b, encoder_takes, cotangent = tie(
+                own_first, corner_two, over_a, others_b, encoder_takes, cotangent
+            )
+            corner_a = blocks.corner(over_a)
+            over_b = blocks.hops(others_b)
         own_encoder = plan.spread_end(encoder_takes)
         full_encoder = plan.gather_rows(own_encoder)
         full_first = plan.gather_rows(own_first)
         if tiled:
-            w_query, w_memory, w_cross_out = group_two.assemble(
-                me, plan.n_col, (others_two, *over_two, *corner_two)
+            w_query, w_memory, w_cross_out = assemble(
+                me, plan.n_col, (group_two, (others_two, *over_two, *corner_two))
             )
         memory = (dot(full_encoder, w_memory) + memory_bias).astype(BF)
         cross_q = (dot(full_first, w_query) + query_bias).astype(BF)
         cotangent_takes = plan.spread(cotangent)
         if tiled:
-            cross_q, memory = tie(cross_q, memory)
+            cross_q, memory, over_b, corner_a = tie(cross_q, memory, over_b, corner_a)
+            corner_b = blocks.corner(over_b)
         recall, cross_logsum = cross_attention(plan, cross_q, memory, answers, passages, n)
         if tiled:
-            recall, corner_three, cotangent_takes = tie(recall, corner_three, cotangent_takes)
+            recall, corner_b, cotangent_takes = tie(recall, corner_b, cotangent_takes)
         branch = plan.scatter_product(recall, w_cross_out) + bias_rows[1]
         normed, normal_two, inverse_two = normalize(own_first.astype(F32) + branch, gain_rows[1], shift_rows[1])
         own_second = normed.astype(BF)
         full_second = plan.gather_rows(own_second)
         if tiled:
-            w_expand, w_shrink = group_three.assemble(
-                me, plan.n_col, (others_three, *over_three, *corner_three)
+            w_expand, w_shrink = assemble(
+                me,
+                plan.n_col,
+                (group_expand, (others_a, *over_a, *corner_a)),
+                (group_shrink, (others_b, *over_b, *corner_b)),
             )
         expanded = dot(full_second, w_expand) + hidden_bias
         activated, slope = gelu_and_slope(expanded)
@@ -940,7 +971,9 @@
         full_dshrink = plan.gather_rows(own_dshrink)
         if tiled:
             of_shrink = [(blocks.product(activated, full_dshrink), 0, hidden_part)]
-            got_shrink = blocks.reduce_start(of_shrink, 1)
+            send_shrink = blocks.reduce_send(of_shrink, 1)
+            full_dshrink, send_shrink = tie(full_dshrink, send_shrink)
+            got_shrink = blocks.hop(send_shrink, 1)
         d_expanded = (dot_flip(full_dshrink, w_shrink) * slope.astype(F32)).astype(BF)
         (d_expanded,) = tie(d_expanded)
         if tiled:
@@ -1037,22 +1070,25 @@
         hidden_grad = (resid_one + plan.scatter_product(d_packed, w_self, True)).astype(BF)
         if tiled:
             small = small + blocks.hop(small, 1)
-        hidden_takes = plan.collect(hidden_grad)
+        hidden_grad = plan.cut(hidden_grad)
+        if tiled:
+            hidden_grad, got_low, got_high = tie(hidden_grad, got_low, got_high)
+        hidden_takes = plan.deal(hidden_grad)
         if not tiled:
             small = total(small, mesh, ("dp", "col"))
         if tiled:
-            output, g_encoder = plan.collect_end(output_takes), plan.collect_end(encoder_grad_takes)
-            got_low, got_high, small, output, g_encoder = tie(got_low, got_high, small, output, g_encoder)
+            g_encoder = plan.collect_end(encoder_grad_takes)
+            small, output_takes, g_encoder = tie(small, output_takes, g_encoder)
             chunk_low = blocks.reduce_next(of_low, 1, got_low)
             chunk_high = blocks.reduce_next(of_high, 2, got_high)
             small = small + blocks.hop(small, 2)
+            output = plan.collect_end(output_takes)
             ready = lax.all_gather(mine_hidden, "dp", axis=0)
             g_shrink, g_expand = finish(
                 jnp.arange(n), [[((ready, q), 0)] for q in range(n)], [(1, False), (1, True)], hidden_part, width
             )
-            g_hidden = plan.collect_end(hidden_takes)
-            chunk_low, chunk_high, mine_cross, g_shrink, g_expand = tie(
-                chunk_low, chunk_high, mine_cross, g_shrink, g_expand
+            chunk_low, chunk_high, small, output, hidden_takes = tie(
+                chunk_low, chunk_high, small, output, hidden_takes
             )
             own, *rest = sum_chunks(
                 [as_chunk(of_low, 1, chunk_low), as_chunk(of_high, 2, chunk_high)],
@@ -1062,11 +1098,14 @@
             )
             arrived = [own] + [plan.shift(r, -1 - k) for k, r in enumerate(rest)]
             small = small + lax.ppermute(small, "col", [(i, i ^ 1) for i in range(plan.n_col)])
-            arrived, g_hidden = tie(arrived, g_hidden)
+            g_hidden = plan.collect_end(hidden_takes)
+            ready = lax.all_gather(mine_cross, "dp", axis=0)
+            arrived, g_hidden, g_shrink, g_expand, small, ready = tie(
+                arrived, g_hidden, g_shrink, g_expand, small, ready
+            )
             mine_self = sum(r.astype(F32) for r in arrived).astype(BF)
             over_self = blocks.hops(mine_self)
             small = small + lax.ppermute(small, "col", [(i, i ^ 2) for i in range(plan.n_col)])
-            ready = lax.all_gather(mine_cross, "dp", axis=0)
             g_query, g_cross_out, g_memory = finish(
                 jnp.arange(n),
                 [[((ready, q), 0)] for q in range(n)],

time: 673 us -> 654 us (0.972)
  Pallas kernels: 187 us -> 149 us
  starting transfers between devices: 75.1 us -> 98.4 us
    pallas_call x2, Pallas kernels: 64.2 us -> 37.8 us  [attend_back(): pl.pallas_call(functools.partial(backward_kernel, causal), out_shape=out_...]
    ppermute x6, waiting for transfers between devices: 21.8 us -> 5.28 us  [shift(): return lax.ppermute(values, 'col', [(i, (i + k) % n) for i in range(n)])]
    pallas_call x2, Pallas kernels: 41.9 us -> 26.6 us  [attend(): pl.pallas_call(functools.partial(forward_kernel, causal), out_shape=(jax....]
    ppermute x30 -> x34, waiting for transfers between devices: 81.9 us -> 94.7 us  [hop(): return lax.ppermute(values, 'dp', [(i, i ^ step) for i in range(self.n)])]
    all_to_all x3, starting transfers between devices: 13.8 us -> 25.1 us  [deal(): return lax.all_to_all(blocks, 'col', 0, 0, tiled=True)]
    reduce_scatter x1, waiting for transfers between devices: 9.72 us -> 0.01 us  [body(): mine_cross = lax.psum_scatter(sums, 'col', scatter_dimension=0, tiled=False)]
    all_gather x2, waiting for transfers between devices: 9.45 us -> 0.02 us  [others_by_gather(): every = lax.all_gather(piece, 'col', axis=0)]
    all_to_all x3, waiting for transfers between devices: 4.16 us -> 13.4 us  [deal(): return lax.all_to_all(blocks, 'col', 0, 0, tiled=True)]
  transfers between devices with their start and end apart: 71 -> 75, of which waited for: 25 -> 32; matrix products, arithmetic and copies ran while one was open for 22% -> 21% of each run, Pallas kernels for 27% -> 21%
where the time goes in v4:
time: 654 us; the launch traced here: 644 us
  waiting for transfers between devices  157 us (24%)
  Pallas kernels  149 us (23%)
  matrix products  112 us (17%)
  starting transfers between devices  98.4 us (15%)
  local copies, waits for them, and re-layouts  71.4 us (11%)
  other arithmetic  32.4 us (5%)
  between operations  24.1 us (4%)
    ppermute x34, waiting for transfers between devices, hop(): return lax.ppermute(values, 'dp', [(i, i ^ step) for i in range(self.n)])  94.7 us
    pallas_call x21, Pallas kernels, in_vmem(): pl.pallas_call(kernel, out_shape=outs, grid_spec=pltpu.PrefetchScalarGrid...  76.4 us
    dot_general x11, matrix products, dot_flip(): lax.dot_general(left, right, (((1,), (1,)), ((), ())), preferred_element_...  44.2 us
    dot_general x10, matrix products, dot(): return jnp.dot(left, right, preferred_element_type=F32)  39 us
    pallas_call x2, Pallas kernels, attend_back(): pl.pallas_call(functools.partial(backward_kernel, causal), out_shape=out_...  37.8 us
    ppermute x34, starting transfers between devices, hop(): return lax.ppermute(values, 'dp', [(i, i ^ step) for i in range(self.n)])  35 us
    dot_general x7, matrix products, outer_sum(): lax.dot_general(left, right, (((0,), (0,)), ((), ())), preferred_element_...  28.4 us
    pallas_call x2, Pallas kernels, attend(): pl.pallas_call(functools.partial(forward_kernel, causal), out_shape=(jax....  26.6 us
  transfers between devices with their start and end apart: 75, of which 32 were waited for; matrix products, arithmetic and copies ran while one was open for 21% of the time, Pallas kernels for 21%

profile of v4, /device:TPU:0, one launch (start us, length us, event | category | flops | bytes accessed | tf_op | source)
XLA Modules:
  0.0 644.1 jit_solution(14316013688112104719)
XLA Ops:
  48.0 16.6 %all-to-all-done.refs_0_ = bf16[4,512,256]{2,1,0:T(8,128)(2,1)S(1)} async-done(((bf16[4,512,256]{2,1,0:T(8,128)(2,1)}), bf16[4,512,256]{2,1,0:T(8,128)(2,1)S(1)}, u32[]{:S(2)}, u32[]{:S(2)}) %all-to-all-start) | async-done | bytes 1048608 | tf_op jit(solution)/shard_map/all_to_all | solution.py:230
  89.0 5.7 assemble.3
  97.6 5.7 add_convert_fusion.query_ref.key_ref.value_ref
  105.4 12.9 %attend.2 = (bf16[1024,512]{1,0:T(8,128)(2,1)S(1)}, f32[4,2,1024]{2,1,0:T(2,128)S(1)}) custom-call(s32[3]{0:T(128)S(1)} %get-tuple-element.390.info, bf16[1024,1536]{1,0:T(8,128)(2,1)S(1)} %add_convert_fusion.query_ref.key_ref.value_ref, bf16[1024,1536]{1,0:T(8,128)(2,1)S(1)} %add_convert_fusion.query_ref.key_ref.value_ref, ...), custom_call_target="tpu_custom_call" | custom-call | flops 20000000000 | bytes 1048576 | tf_op jit(solution)/shard_map/attend/pallas_call | solution.py:462
  127.1 9.8 %all-to-all-start.1 = ((bf16[4,512,256]{2,1,0:T(8,128)(2,1)}), bf16[4,512,256]{2,1,0:T(8,128)(2,1)}, u32[]{:S(2)}, u32[]{:S(2)}) async-start(bf16[4,512,256]{2,1,0:T(8,128)(2,1)} %copy-done.36), calls=%async_computation.1 | async-start | bytes 2097152 | tf_op jit(solution)/shard_map/all_to_all | solution.py:230
  158.6 4.8 all-to-all-done.1.refs_0_
  163.4 8.5 %collective-permute-done.16.refs_2_ = bf16[3072,128]{1,0:T(8,128)(2,1)S(1)} collective-permute-done((bf16[3072,128]{1,0:T(8,128)(2,1)}, bf16[3072,128]{1,0:T(8,128)(2,1)S(1)}, u32[]{:S(2)}, u32[]{:S(2)}) %collective-permute-start.16) | collective-permute-done | bytes 786464 | tf_op jit(solution)/shard_map/ppermute | solution.py:745
  183.0 4.8 all-to-all-start.2
  187.8 5.9 assemble.4
  210.4 13.7 %attend.3 = (bf16[1024,512]{1,0:T(8,128)(2,1)S(1)}, f32[4,2,1024]{2,1,0:T(2,128)S(1)}) custom-call(s32[3]{0:T(128)S(1)} %get-tuple-element.391.info, bf16[1024,512]{1,0:T(8,128)(2,1)S(1)} %add_convert_fusion.5.query_ref, bf16[1024,1024]{1,0:T(8,128)(2,1)S(1)} %add_convert_fusion.1.key_ref.value_ref, bf16[1024,1024]{1,0:T(8,128)(2,1)S(1)} %add_convert_fusion.1.key_ref.value_ref), custom_call_target="tpu_custom_call" | custom-call | flops 20000000000 | bytes 1048576 | tf_op jit(solution)/shard_map/attend/pallas_call | solution.py:462
  235.1 9.7 %assemble.5 = (bf16[1024,2048]{1,0:T(8,128)(2,1)}, bf16[2048,1024]{1,0:T(8,128)(2,1)}) custom-call(s32[4]{0:T(128)} %pad_add_fusion.3.info, bf16[256,2048]{1,0:T(8,128)(2,1)} %refs_0_.7, bf16[3072,128]{1,0:T(8,128)(2,1)} %pick_others.4.refs_1_, bf16[3072,128]{1,0:T(8,128)(2,1)} %copy-done.42, bf16[3072,128]{1,0:T(8,128)(2,1)} %collective-permute-done.17.refs_3_, ...), custom_call_target="tpu_custom_call" | custom-call | bytes 65536 | tf_op jit(solution)/shard_map/assemble/pallas_call | solution.py:48
  244.8 10.2 %multiply_convert_fusion.1 = (bf16[1024,2048]{1,0:T(8,128)(2,1)S(1)}, f32[1024,2048]{1,0:T(8,128)}) fusion(f32[2048]{0:T(1024)S(1)} %bitcast.314, bf16[1024,2048]{1,0:T(8,128)(2,1)} %get-tuple-element.158, bf16[512,1024]{1,0:T(8,128)(2,1)} %collective-permute-done.27, bf16[512,1024]{1,0:T(8,128)(2,1)S(1)} %add_convert_fusion.4), kind=kOutput, calls=%fused_computation.8 | convolution fusion | flops 4311744512 | bytes 18882560 | tf_op jit(solution)/shard_map/dot_general | solution.py:22
  263.3 4.7 fusion.89
  275.7 4.9 convolution_convert_fusion.2
  284.4 7.8 %multiply_convert_fusion = bf16[1024,2048]{1,0:T(8,128)(2,1)S(1)} fusion(f32[1024,2048]{1,0:T(8,128)S(1)} %bitcast.326, f32[2048]{0:T(1024)S(1)} %bitcast.315, bf16[1024,1024]{1,0:T(8,128)(2,1)S(1)} %pad_maximum_fusion.3, bf16[2048,1024]{1,0:T(8,128)(2,1)S(1)} %copy-done.80), kind=kOutput, calls=%fused_computation.7 | convolution fusion | flops 4322230272 | bytes 18882560 | tf_op jit(solution)/shard_map/dot_general | solution.py:26
  298.6 15.0 %all-to-all-start.3 = ((bf16[4,512,256]{2,1,0:T(8,128)(2,1)}), bf16[4,512,256]{2,1,0:T(8,128)(2,1)}, u32[]{:S(2)}, u32[]{:S(2)}) async-start(bf16[4,512,256]{2,1,0:T(8,128)(2,1)} %cut_columns.3), calls=%async_computation.3 | async-start | bytes 2097152 | tf_op jit(solution)/shard_map/all_to_all | solution.py:247
  313.6 7.5 %convolution_convert_fusion.1 = bf16[2048,1024]{1,0:T(8,128)(2,1)S(1)} fusion(bf16[1024,2048]{1,0:T(8,128)(2,1)} %copy-done.33, bf16[512,1024]{1,0:T(8,128)(2,1)} %collective-permute-done.27, bf16[512,1024]{1,0:T(8,128)(2,1)} %copy-done.56), kind=kOutput, calls=%fused_computation.15 | convolution fusion | flops 4301258752 | bytes 10485760 | tf_op jit(solution)/shard_map/dot_general | solution.py:30
  324.2 5.6 multiply_reduce_fusion.1
  335.8 19.1 %attend_back.2 = (bf16[1024,512]{1,0:T(8,128)(2,1)S(1)}, bf16[1024,1024]{1,0:T(8,128)(2,1)S(1)}) custom-call(s32[3]{0:T(128)S(1)} %get-tuple-element.391.info, bf16[1024,512]{1,0:T(8,128)(2,1)S(1)} %copy-done.6, bf16[1024,1024]{1,0:T(8,128)(2,1)} %copy-done, bf16[1024,1024]{1,0:T(8,128)(2,1)} %copy-done, ...), custom_call_target="tpu_custom_call" | custom-call | bytes 65536 | tf_op jit(solution)/shard_map/attend_back/pallas_call | solution.py:497
  354.9 16.7 %collective-permute-done.33.refs_4_ = bf16[2,512,1024]{2,1,0:T(8,128)(2,1)} collective-permute-done((bf16[2,512,1024]{2,1,0:T(8,128)(2,1)}, bf16[2,512,1024]{2,1,0:T(8,128)(2,1)}, u32[]{:S(2)}, u32[]{:S(2)}) %collective-permute-start.33) | collective-permute-done | bytes 2097184 | tf_op jit(solution)/shard_map/ppermute | solution.py:745
  404.4 4.9 sum_chunks.3
  417.3 8.1 %collective-permute-done.39.refs_5_ = bf16[2,256,1024]{2,1,0:T(8,128)(2,1)} collective-permute-done((bf16[2,256,1024]{2,1,0:T(8,128)(2,1)}, bf16[2,256,1024]{2,1,0:T(8,128)(2,1)}, u32[]{:S(2)}, u32[]{:S(2)}) %collective-permute-start.39) | collective-permute-done | bytes 1048608 | tf_op jit(solution)/shard_map/ppermute | solution.py:745
  445.5 6.6 %all-to-all-start.4 = ((bf16[4,512,256]{2,1,0:T(8,128)(2,1)}), bf16[4,512,256]{2,1,0:T(8,128)(2,1)}, u32[]{:S(2)}, u32[]{:S(2)}) async-start(bf16[4,512,256]{2,1,0:T(8,128)(2,1)} %cut_columns.4), calls=%async_computation.5 | async-start | bytes 2097152 | tf_op jit(solution)/shard_map/all_to_all | solution.py:247
  458.3 18.7 %attend_back.3 = bf16[1024,1536]{1,0:T(8,128)(2,1)S(1)} custom-call(s32[3]{0:T(128)S(1)} %copy-done.10, bf16[1024,1536]{1,0:T(8,128)(2,1)} %copy-done.12, bf16[1024,1536]{1,0:T(8,128)(2,1)} %copy-done.12, bf16[1024,1536]{1,0:T(8,128)(2,1)} %copy-done.12, bf16[1024,512]{1,0:T(8,128)(2,1)S(1)} %copy-done.11, f32[4,2,1024]{2,1,0:T(2,128)S(1)} %get-tuple-element.171.logsum_ref), custom_call_target="tpu_custom_call" | custom-call | flops 20000000000 | bytes 1048576 | tf_op jit(solution)/shard_map/attend_back/pallas_call | solution.py:497
  479.5 13.4 %all-to-all-done.4 = bf16[4,512,256]{2,1,0:T(8,128)(2,1)} async-done(((bf16[4,512,256]{2,1,0:T(8,128)(2,1)}), bf16[4,512,256]{2,1,0:T(8,128)(2,1)}, u32[]{:S(2)}, u32[]{:S(2)}) %all-to-all-start.4) | async-done | bytes 1048608 | tf_op jit(solution)/shard_map/all_to_all | solution.py:247
  492.9 6.0 convolution_convert_fusion
  510.8 5.0 fusion.16
  520.4 6.0 add_convert_fusion.2.refs_0_
  528.7 13.9 %collective-permute-done.44.refs_1_ = bf16[2,256,1024]{2,1,0:T(8,128)(2,1)} collective-permute-done((bf16[2,256,1024]{2,1,0:T(8,128)(2,1)}, bf16[2,256,1024]{2,1,0:T(8,128)(2,1)}, u32[]{:S(2)}, u32[]{:S(2)}) %collective-permute-start.44) | collective-permute-done | bytes 1048608 | tf_op jit(solution)/shard_map/ppermute | solution.py:745
  562.9 15.8 %collective-permute-done.51 = f32[13312]{0:T(1024)S(1)} collective-permute-done((f32[13312]{0:T(1024)S(1)}, f32[13312]{0:T(1024)S(1)}, u32[]{:S(2)}, u32[]{:S(2)}) %collective-permute-start.51) | collective-permute-done | bytes 53280 | tf_op jit(solution)/shard_map/ppermute | solution.py:745
  598.3 10.3 %collective-permute-done.57 = f32[13312]{0:T(1024)S(1)} collective-permute-done((f32[13312]{0:T(1024)S(1)}, f32[13312]{0:T(1024)S(1)}, u32[]{:S(2)}, u32[]{:S(2)}) %collective-permute-start.57) | collective-permute-done | bytes 53280 | tf_op jit(solution)/shard_map/ppermute | solution.py:1100
  628.8 4.8 finish.5
  (528 shorter events, 316.9 us)
Async XLA Ops:
  22.6 41.9 %all-to-all-start = ((bf16[4,512,256]{2,1,0:T(8,128)(2,1)}), bf16[4,512,256]{2,1,0:T(8,128)(2,1)S(1)}, u32[]{:S(2)}, u32[]{:S(2)}) async-start(bf16[4,512,256]{2,1,0:T(8,128)(2,1)} %constant_dynamic-update-slice_fusion.2), calls=%async_computation | async-start | bytes 2097152 | tf_op jit(solution)/shard_map/all_to_all | solution.py:230
  26.2 68.5 %all-gather.10.cloned.1.call-start = ((), (), s32[]{:S(2)}) async-start(), calls=%async_computation.11 | async-start | bytes 1392640 | tf_op jit(solution)/shard_map/all_gather | solution.py:771
  40.7 96.2 %all-gather.12.cloned.1.call-start = ((), (), s32[]{:S(2)}) async-start(), calls=%async_computation.12 | async-start | bytes 2621440 | tf_op jit(solution)/shard_map/all_gather | solution.py:771
  41.7 39.1 %collective-permute-start.10 = (bf16[2,512,256]{2,1,0:T(8,128)(2,1)}, bf16[2,512,256]{2,1,0:T(8,128)(2,1)}, u32[]{:S(2)}, u32[]{:S(2)}) collective-permute-start(bf16[2,512,256]{2,1,0:T(8,128)(2,1)} %dynamic-slice_bitcast_fusion), channel_id=1, source_target_pairs={{0,4},{4,0},{1,5},{5,1},{2,6},{6,2},{3,7},{7,3},{8,12},{12,8},{9,1... | collective-permute-start | bytes 1572872 | tf_op jit(solution)/shard_map/ppermute | solution.py:189
  43.5 39.1 %collective-permute-start.9 = (bf16[2,512,256]{2,1,0:T(8,128)(2,1)}, bf16[2,512,256]{2,1,0:T(8,128)(2,1)}, u32[]{:S(2)}, u32[]{:S(2)}) collective-permute-start(bf16[2,512,256]{2,1,0:T(8,128)(2,1)} %dynamic-slice_bitcast_fusion.1), channel_id=1, source_target_pairs={{0,4},{4,0},{1,5},{5,1},{2,6},{6,2},{3,7},{7,3},{8,12},{12,8},{9,1... | collective-permute-start | bytes 1572872 | tf_op jit(solution)/shard_map/ppermute | solution.py:189
  44.2 30.2 %collective-permute-start.6 = (bf16[3072,128]{1,0:T(8,128)(2,1)S(1)}, bf16[3072,128]{1,0:T(8,128)(2,1)S(1)}, u32[]{:S(2)}, u32[]{:S(2)}) collective-permute-start(bf16[3072,128]{1,0:T(8,128)(2,1)S(1)} %constant_dynamic-update-slice_fusion.3.refs_2_), channel_id=1, source_target_pairs={{0,16},{8,24},{16,0},{24,8},{1,17},{9,25},{17,1},{25,9},{2,18},{10... | collective-permute-start | bytes 2359304 | tf_op jit(solution)/shard_map/ppermute | solution.py:745
  45.9 30.8 %collective-permute-start.5 = (bf16[3072,128]{1,0:T(8,128)(2,1)S(1)}, bf16[3072,128]{1,0:T(8,128)(2,1)S(1)}, u32[]{:S(2)}, u32[]{:S(2)}) collective-permute-start(bf16[3072,128]{1,0:T(8,128)(2,1)S(1)} %constant_dynamic-update-slice_fusion.3.refs_2_), channel_id=1, source_target_pairs={{0,8},{8,0},{16,24},{24,16},{1,9},{9,1},{17,25},{25,17},{2,10},{10... | collective-permute-start | bytes 2359304 | tf_op jit(solution)/shard_map/ppermute | solution.py:745
  68.5 29.0 %collective-permute-start.1 = (bf16[512,1024]{1,0:T(8,128)(2,1)}, bf16[512,1024]{1,0:T(8,128)(2,1)}, u32[]{:S(2)}, u32[]{:S(2)}) collective-permute-start(bf16[512,1024]{1,0:T(8,128)(2,1)} %join_columns.3), channel_id=1, source_target_pairs={{0,4},{4,0},{1,5},{5,1},{2,6},{6,2},{3,7},{7,3},{8,12},{12,8},{9,1... | collective-permute-start | bytes 3145736 | tf_op jit(solution)/shard_map/ppermute | solution.py:189
  127.1 36.3 %all-to-all-start.1 = ((bf16[4,512,256]{2,1,0:T(8,128)(2,1)}), bf16[4,512,256]{2,1,0:T(8,128)(2,1)}, u32[]{:S(2)}, u32[]{:S(2)}) async-start(bf16[4,512,256]{2,1,0:T(8,128)(2,1)} %copy-done.36), calls=%async_computation.1 | async-start | bytes 2097152 | tf_op jit(solution)/shard_map/all_to_all | solution.py:230
  178.1 28.1 %collective-permute-start.20 = (bf16[3072,128]{1,0:T(8,128)(2,1)S(1)}, bf16[3072,128]{1,0:T(8,128)(2,1)}, u32[]{:S(2)}, u32[]{:S(2)}) collective-permute-start(bf16[3072,128]{1,0:T(8,128)(2,1)S(1)} %copy-done.40), channel_id=1, source_target_pairs={{0,8},{8,0},{16,24},{24,16},{1,9},{9,1},{17,25},{25,17},{2,10},{10... | collective-permute-start | bytes 2359304 | tf_op jit(solution)/shard_map/ppermute | solution.py:745
  178.5 27.6 %collective-permute-start.21 = (bf16[3072,128]{1,0:T(8,128)(2,1)S(1)}, bf16[3072,128]{1,0:T(8,128)(2,1)}, u32[]{:S(2)}, u32[]{:S(2)}) collective-permute-start(bf16[3072,128]{1,0:T(8,128)(2,1)S(1)} %copy-done.40), channel_id=1, source_target_pairs={{0,16},{8,24},{16,0},{24,8},{1,17},{9,25},{17,1},{25,9},{2,18},{10... | collective-permute-start | bytes 2359304 | tf_op jit(solution)/shard_map/ppermute | solution.py:745
  183.0 41.9 %all-to-all-start.2 = ((bf16[4,512,256]{2,1,0:T(8,128)(2,1)}), bf16[4,512,256]{2,1,0:T(8,128)(2,1)S(1)}, u32[]{:S(2)}, u32[]{:S(2)}) async-start(bf16[4,512,256]{2,1,0:T(8,128)(2,1)} %constant_dynamic-update-slice_fusion), calls=%async_computation.2 | async-start | bytes 2097152 | tf_op jit(solution)/shard_map/all_to_all | solution.py:230
  295.9 27.9 %collective-permute-start.30 = (f32[512,1024]{1,0:T(8,128)}, f32[512,1024]{1,0:T(8,128)}, u32[]{:S(2)}, u32[]{:S(2)}) collective-permute-start(f32[512,1024]{1,0:T(8,128)} %fusion.5), channel_id=1, source_target_pairs={{0,4},{4,0},{1,5},{5,1},{2,6},{6,2},{3,7},{7,3},{8,12},{12,8},{9,1... | collective-permute-start | bytes 6291464 | tf_op jit(solution)/shard_map/ppermute | solution.py:189
  298.6 56.3 %all-to-all-start.3 = ((bf16[4,512,256]{2,1,0:T(8,128)(2,1)}), bf16[4,512,256]{2,1,0:T(8,128)(2,1)}, u32[]{:S(2)}, u32[]{:S(2)}) async-start(bf16[4,512,256]{2,1,0:T(8,128)(2,1)} %cut_columns.3), calls=%async_computation.3 | async-start | bytes 2097152 | tf_op jit(solution)/shard_map/all_to_all | solution.py:247
  313.5 179.3 %reduce-scatter.3.cloned.1.call-start = ((), (), s32[]{:S(2)}) async-start(), calls=%async_computation.8 | async-start | bytes 2621440 | tf_op jit(solution)/shard_map/reduce_scatter | solution.py:1020
  323.9 47.8 %collective-permute-start.33 = (bf16[2,512,1024]{2,1,0:T(8,128)(2,1)}, bf16[2,512,1024]{2,1,0:T(8,128)(2,1)}, u32[]{:S(2)}, u32[]{:S(2)}) collective-permute-start(bf16[2,512,1024]{2,1,0:T(8,128)(2,1)} %bitcast.33), channel_id=1, source_target_pairs={{0,16},{8,24},{16,0},{24,8},{1,17},{9,25},{17,1},{25,9},{2,18},{10... | collective-permute-start | bytes 6291464 | tf_op jit(solution)/shard_map/ppermute | solution.py:745
  323.9 47.8 %collective-permute-start.32 = (bf16[2,512,1024]{2,1,0:T(8,128)(2,1)}, bf16[2,512,1024]{2,1,0:T(8,128)(2,1)}, u32[]{:S(2)}, u32[]{:S(2)}) collective-permute-start(bf16[2,512,1024]{2,1,0:T(8,128)(2,1)} %bitcast.32), channel_id=1, source_target_pairs={{0,8},{8,0},{16,24},{24,16},{1,9},{9,1},{17,25},{25,17},{2,10},{10... | collective-permute-start | bytes 6291464 | tf_op jit(solution)/shard_map/ppermute | solution.py:745
  375.4 26.0 %collective-permute-start.37 = (bf16[512,1024]{1,0:T(8,128)(2,1)S(1)}, bf16[512,1024]{1,0:T(8,128)(2,1)S(1)}, u32[]{:S(2)}, u32[]{:S(2)}) collective-permute-start(bf16[512,1024]{1,0:T(8,128)(2,1)S(1)} %slice_add_fusion), channel_id=1, source_target_pairs={{0,8},{8,0},{16,24},{24,16},{1,9},{9,1},{17,25},{25,17},{2,10},{10... | collective-permute-start | bytes 3145736 | tf_op jit(solution)/shard_map/ppermute | solution.py:745
  377.4 26.0 %collective-permute-start.36 = (bf16[512,1024]{1,0:T(8,128)(2,1)S(1)}, bf16[512,1024]{1,0:T(8,128)(2,1)S(1)}, u32[]{:S(2)}, u32[]{:S(2)}) collective-permute-start(bf16[512,1024]{1,0:T(8,128)(2,1)S(1)} %slice_add_fusion.1), channel_id=1, source_target_pairs={{0,16},{8,24},{16,0},{24,8},{1,17},{9,25},{17,1},{25,9},{2,18},{10... | collective-permute-start | bytes 3145736 | tf_op jit(solution)/shard_map/ppermute | solution.py:745
  389.2 36.2 %collective-permute-start.39 = (bf16[2,256,1024]{2,1,0:T(8,128)(2,1)}, bf16[2,256,1024]{2,1,0:T(8,128)(2,1)}, u32[]{:S(2)}, u32[]{:S(2)}) collective-permute-start(bf16[2,256,1024]{2,1,0:T(8,128)(2,1)} %bitcast.40), channel_id=1, source_target_pairs={{0,16},{8,24},{16,0},{24,8},{1,17},{9,25},{17,1},{25,9},{2,18},{10... | collective-permute-start | bytes 3145736 | tf_op jit(solution)/shard_map/ppermute | solution.py:745
  393.2 32.2 %collective-permute-start.38 = (bf16[2,256,1024]{2,1,0:T(8,128)(2,1)}, bf16[2,256,1024]{2,1,0:T(8,128)(2,1)}, u32[]{:S(2)}, u32[]{:S(2)}) collective-permute-start(bf16[2,256,1024]{2,1,0:T(8,128)(2,1)} %pad_maximum_fusion.16), channel_id=1, source_target_pairs={{0,8},{8,0},{16,24},{24,16},{1,9},{9,1},{17,25},{25,17},{2,10},{10... | collective-permute-start | bytes 3145736 | tf_op jit(solution)/shard_map/ppermute | solution.py:745
  401.4 37.2 %collective-permute-start.42 = (f32[512,1024]{1,0:T(8,128)}, f32[512,1024]{1,0:T(8,128)}, u32[]{:S(2)}, u32[]{:S(2)}) collective-permute-start(f32[512,1024]{1,0:T(8,128)} %fusion.27), channel_id=1, source_target_pairs={{0,4},{4,0},{1,5},{5,1},{2,6},{6,2},{3,7},{7,3},{8,12},{12,8},{9,1... | collective-permute-start | bytes 6291464 | tf_op jit(solution)/shard_map/ppermute | solution.py:189
  445.5 47.4 %all-to-all-start.4 = ((bf16[4,512,256]{2,1,0:T(8,128)(2,1)}), bf16[4,512,256]{2,1,0:T(8,128)(2,1)}, u32[]{:S(2)}, u32[]{:S(2)}) async-start(bf16[4,512,256]{2,1,0:T(8,128)(2,1)} %cut_columns.4), calls=%async_computation.5 | async-start | bytes 2097152 | tf_op jit(solution)/shard_map/all_to_all | solution.py:247
  452.1 105.5 %reduce-scatter.5.cloned.1.call-start = ((), (), s32[]{:S(2)}) async-start(), calls=%async_computation.9 | async-start | bytes 1310720 | tf_op jit(solution)/shard_map/reduce_scatter | solution.py:1042
  454.3 38.6 %collective-permute-start.41 = (bf16[256,1024]{1,0:T(8,128)(2,1)}, bf16[256,1024]{1,0:T(8,128)(2,1)}, u32[]{:S(2)}, u32[]{:S(2)}) collective-permute-start(bf16[256,1024]{1,0:T(8,128)(2,1)} %slice_add_fusion.3), channel_id=1, source_target_pairs={{0,8},{8,0},{16,24},{24,16},{1,9},{9,1},{17,25},{25,17},{2,10},{10... | collective-permute-start | bytes 1572872 | tf_op jit(solution)/shard_map/ppermute | solution.py:745
  458.1 34.8 %collective-permute-start.40 = (bf16[256,1024]{1,0:T(8,128)(2,1)}, bf16[256,1024]{1,0:T(8,128)(2,1)}, u32[]{:S(2)}, u32[]{:S(2)}) collective-permute-start(bf16[256,1024]{1,0:T(8,128)(2,1)} %maximum_add_fusion), channel_id=1, source_target_pairs={{0,16},{8,24},{16,0},{24,8},{1,17},{9,25},{17,1},{25,9},{2,18},{10... | collective-permute-start | bytes 1572872 | tf_op jit(solution)/shard_map/ppermute | solution.py:745
  504.6 88.6 %all-gather.14.cloned.1.call-start = ((), (), s32[]{:S(2)}) async-start(), calls=%async_computation.13 | async-start | bytes 2621440 | tf_op jit(solution)/shard_map/all_gather | solution.py:1086
  510.1 42.7 %collective-permute-start.50 = (bf16[2,512,256]{2,1,0:T(8,128)(2,1)}, bf16[2,512,256]{2,1,0:T(8,128)(2,1)}, u32[]{:S(2)}, u32[]{:S(2)}) collective-permute-start(bf16[2,512,256]{2,1,0:T(8,128)(2,1)} %get-tuple-element.331), channel_id=1, source_target_pairs={{0,4},{4,0},{1,5},{5,1},{2,6},{6,2},{3,7},{7,3},{8,12},{12,8},{9,1... | collective-permute-start | bytes 1572872 | tf_op jit(solution)/shard_map/ppermute | solution.py:189
  516.1 26.4 %collective-permute-start.44 = (bf16[2,256,1024]{2,1,0:T(8,128)(2,1)}, bf16[2,256,1024]{2,1,0:T(8,128)(2,1)}, u32[]{:S(2)}, u32[]{:S(2)}) collective-permute-start(bf16[2,256,1024]{2,1,0:T(8,128)(2,1)} %slice.411), channel_id=1, source_target_pairs={{0,8},{8,0},{16,24},{24,16},{1,9},{9,1},{17,25},{25,17},{2,10},{10... | collective-permute-start | bytes 3145736 | tf_op jit(solution)/shard_map/ppermute | solution.py:745
  517.6 27.4 %collective-permute-start.45 = (bf16[2,256,1024]{2,1,0:T(8,128)(2,1)}, bf16[2,256,1024]{2,1,0:T(8,128)(2,1)}, u32[]{:S(2)}, u32[]{:S(2)}) collective-permute-start(bf16[2,256,1024]{2,1,0:T(8,128)(2,1)} %pad_maximum_fusion.17), channel_id=1, source_target_pairs={{0,16},{8,24},{16,0},{24,8},{1,17},{9,25},{17,1},{25,9},{2,18},{10... | collective-permute-start | bytes 3145736 | tf_op jit(solution)/shard_map/ppermute | solution.py:745
  545.0 37.1 %all-to-all-start.5 = ((bf16[4,512,256]{2,1,0:T(8,128)(2,1)}), bf16[4,512,256]{2,1,0:T(8,128)(2,1)S(1)}, u32[]{:S(2)}, u32[]{:S(2)}) async-start(bf16[4,512,256]{2,1,0:T(8,128)(2,1)} %cut_columns.5), calls=%async_computation.6 | async-start | bytes 2097152 | tf_op jit(solution)/shard_map/all_to_all | solution.py:247
  548.5 63.6 %all-gather.8.cloned.1.call-start = ((), (), s32[]{:S(2)}) async-start(), calls=%async_computation.10 | async-start | bytes 1310720 | tf_op jit(solution)/shard_map/all_gather | solution.py:1102
  (134 other events, 1372.1 us)
Sparse Core Ops, SparseCore 0:
  40.9 45.2 all-gather.9
  88.3 45.4 all-gather.11
  425.6 59.4 reduce-scatter.2
  504.7 26.1 reduce-scatter.4
  532.6 38.2 all-gather.13
  572.7 25.6 all-gather.7

commit v5 on v4

--- a/solution.py
+++ b/solution.py
@@ -317,26 +317,29 @@
     return parts
 
 
-def for_each_block(causal, query_length, key_length, run, skip):
+def for_each_block(causal, whole, query_length, key_length, run, skip):
     blocks = SLOT // SPAN
-    if causal:
-        for i in range(blocks):
-            pl.when(i * SPAN < query_length)(functools.partial(run, i * SPAN, i + 1))
-            pl.when(i * SPAN >= query_length)(functools.partial(skip, i * SPAN))
-        return
-    live = lax.div(query_length + (SPAN - 1), SPAN)
+    half = blocks // 2
     spans = lax.div(key_length + (SPAN - 1), SPAN)
-    for count in range(1, blocks + 1):
-
-        @pl.when(spans == count)
+    short = query_length <= half * SPAN
+    for count in (None,) if causal else range(1, blocks + 1):
+        chosen = True if causal else spans == count
+        items = [(i * SPAN, i + 1 if causal else count) for i in range(blocks)]
+        if whole:
+            pl.when(short & chosen)(functools.partial(run, *items[:half]))
+            pl.when(jnp.logical_not(short) & chosen)(functools.partial(run, *items))
+            continue
+
+        @pl.when(chosen)
         def _(count=count):
-            @pl.loop(0, live)
+            @pl.loop(0, jnp.where(short, 1, 2))
             def _(i):
-                run(pl.multiple_of(i * SPAN, SPAN), count)
-
-    @pl.loop(live, blocks)
-    def _(i):
-        skip(pl.multiple_of(i * SPAN, SPAN))
+                run(*[(pl.multiple_of((2 * i + k) * SPAN, SPAN), count) for k in range(2)])
+
+    @pl.when(short)
+    def _():
+        for i in range(half, blocks):
+            skip(i * SPAN)
 
 
 def forward_kernel(causal, info, query_ref, key_ref, value_ref, out_ref, logsum_ref, keys, values_t):
@@ -347,12 +350,21 @@
         keys[start : start + half, :] = key_ref[pl.ds(stored, half), :]
         values_t[:, start : start + half] = value_ref[pl.ds(stored, half), :].T
 
-    def run(start, count):
-        stored = place_of(start, offset)
-        scaled = query_ref[pl.ds(stored, SPAN), :] * (1.0 / math.sqrt(HEAD_DIM))
+    def run(*items):
+        tasks = []
+        for start, count in items:
+            scaled = query_ref[pl.ds(place_of(start, offset), SPAN), :] * (1.0 / math.sqrt(HEAD_DIM))
+            tasks += [(start, count, head, query) for head, query in enumerate(heads_apart(scaled))]
+
+        def scores_of(task):
+            return score_spans(keys, task[3], task[1], None if causal else key_length)
+
         outs = []
-        for head, query in enumerate(heads_apart(scaled)):
-            parts = score_spans(keys, query, count, None if causal else key_length)
+        ahead = scores_of(tasks[0])
+        for at, (start, count, head, _) in enumerate(tasks):
+            parts = ahead
+            if at + 1 < len(tasks):
+                ahead = scores_of(tasks[at + 1])
             highest = functools.reduce(jnp.maximum, [jnp.max(s, axis=0, keepdims=True) for s in parts])
             raised = [jnp.exp(s - highest) for s in parts]
             below = sum(jnp.sum(e, axis=0, keepdims=True) for e in raised)
@@ -366,12 +378,14 @@
             )
             outs.append(mixed * (1.0 / below))
             logsum_ref[0, head : head + 1, pl.ds(start, SPAN)] = highest + jnp.log(below)
-        out_ref[pl.ds(stored, SPAN), :] = jnp.concatenate(outs, axis=0).T.astype(BF)
+            if head == 1:
+                both = jnp.concatenate(outs[at - 1 : at + 1], axis=0)
+                out_ref[pl.ds(place_of(start, offset), SPAN), :] = both.T.astype(BF)
 
     def skip(start):
         out_ref[pl.ds(place_of(start, offset), SPAN), :] = jnp.zeros((SPAN, LANES), BF)
 
-    for_each_block(causal, query_length, key_length, run, skip)
+    for_each_block(causal, True, query_length, key_length, run, skip)
 
 
 def backward_kernel(
@@ -396,17 +410,27 @@
     value_sum[...] = jnp.zeros_like(value_sum)
     factor = 1.0 / math.sqrt(HEAD_DIM)
 
-    def run(start, count):
-        stored = place_of(start, offset)
-        queries = heads_apart(query_ref[pl.ds(stored, SPAN), :] * factor)
-        ups = heads_apart(up_ref[pl.ds(stored, SPAN), :])
-        spans = key_spans(count)
-        weights, grads, outs = [], [], []
-        for head in range(2):
+    def run(*items):
+        tasks = []
+        for start, count in items:
+            stored = place_of(start, offset)
+            queries = heads_apart(query_ref[pl.ds(stored, SPAN), :] * factor)
+            ups = heads_apart(up_ref[pl.ds(stored, SPAN), :])
+            tasks += [(start, count, head, queries[head], ups[head]) for head in range(2)]
+
+        def products_of(task):
+            _, count, _, query, up = task
+            parts = score_spans(keys, query, count, None if causal else key_length)
+            return parts, [dot_last(values[a:b, :], up) for a, b in key_spans(count)]
+
+        outs, weights, grads = [], [], []
+        ahead = products_of(tasks[0])
+        for at, (start, count, head, _, _) in enumerate(tasks):
+            parts, pulls = ahead
+            if at + 1 < len(tasks):
+                ahead = products_of(tasks[at + 1])
             logsum = logsum_ref[0, head : head + 1, pl.ds(start, SPAN)]
-            parts = score_spans(keys, queries[head], count, None if causal else key_length)
             parts = [jnp.exp(s - logsum) for s in parts]
-            pulls = [dot_last(values[a:b, :], ups[head]) for a, b in spans]
             inner = sum(jnp.sum(p * g, axis=0, keepdims=True) for p, g in zip(parts, pulls))
             pulls = [(p * (g - inner)).astype(BF) for p, g in zip(parts, pulls)]
             outs.append(
@@ -416,23 +440,27 @@
                         g,
                         preferred_element_type=F32,
                     )
-                    for (a, b), g in zip(spans, pulls)
+                    for (a, b), g in zip(key_spans(count), pulls)
                 )
             )
             weights.append([p.astype(BF) for p in parts])
             grads.append(pulls)
-        query_out[pl.ds(stored, SPAN), 0:LANES] = (
-            jnp.concatenate(outs, axis=0) * factor
-        ).T.astype(BF)
-        for at, (a, b) in enumerate(spans):
-            for head in range(2):
-                value_sum[a:b, :] += jnp.dot(weights[head][at], ups[head], preferred_element_type=F32)
-                key_sum[a:b, :] += jnp.dot(grads[head][at], queries[head], preferred_element_type=F32)
+            if head == 0:
+                continue
+            both = jnp.concatenate(outs[at - 1 : at + 1], axis=0) * factor
+            query_out[pl.ds(place_of(start, offset), SPAN), 0:LANES] = both.T.astype(BF)
+            for part, (a, b) in enumerate(key_spans(count)):
+                value_sum[a:b, :] += sum(
+                    jnp.dot(weights[t][part], tasks[t][4], preferred_element_type=F32) for t in (at - 1, at)
+                )
+                key_sum[a:b, :] += sum(
+                    jnp.dot(grads[t][part], tasks[t][3], preferred_element_type=F32) for t in (at - 1, at)
+                )
 
     def skip(start):
         query_out[pl.ds(place_of(start, offset), SPAN), 0:LANES] = jnp.zeros((SPAN, LANES), BF)
 
-    for_each_block(causal, query_length, key_length, run, skip)
+    for_each_block(causal, causal, query_length, key_length, run, skip)
     for start in (0, half):
         stored = place_of(start, offset)
         other_out[pl.ds(stored, half), base : base + LANES] = key_sum[start : start + half, :].astype(BF)

time: 654 us -> 644 us (0.985)
  Pallas kernels: 149 us -> 124 us
  waiting for transfers between devices: 157 us -> 178 us
  starting transfers between devices: 98.4 us -> 91.2 us
    pallas_call x2, Pallas kernels: 37.8 us -> 23.3 us  [attend_back(): pl.pallas_call(functools.partial(backward_kernel, causal), out_shape=out_...]
    ppermute x34, waiting for transfers between devices: 94.7 us -> 107 us  [hop(): return lax.ppermute(values, 'dp', [(i, i ^ step) for i in range(self.n)])]
    pallas_call x2, Pallas kernels: 26.6 us -> 15.3 us  [attend(): pl.pallas_call(functools.partial(forward_kernel, causal), out_shape=(jax....]
    all_to_all x3, waiting for transfers between devices: 13.4 us -> 22.6 us  [deal(): return lax.all_to_all(blocks, 'col', 0, 0, tiled=True)]
    all_to_all x3, starting transfers between devices: 25.1 us -> 17.1 us  [deal(): return lax.all_to_all(blocks, 'col', 0, 0, tiled=True)]
  transfers between devices with their start and end apart: 75 -> 75, of which waited for: 32 -> 33; matrix products, arithmetic and copies ran while one was open for 21% -> 22% of each run, Pallas kernels for 21% -> 18%
where the time goes in v5:
time: 644 us; the launch traced here: 633 us
  waiting for transfers between devices  178 us (28%)
  Pallas kernels  124 us (19%)
  matrix products  111 us (17%)
  starting transfers between devices  91.2 us (14%)
  local copies, waits for them, and re-layouts  71.6 us (11%)
  other arithmetic  32.4 us (5%)
  between operations  24 us (4%)
    ppermute x34, waiting for transfers between devices, hop(): return lax.ppermute(values, 'dp', [(i, i ^ step) for i in range(self.n)])  107 us
    pallas_call x21, Pallas kernels, in_vmem(): pl.pallas_call(kernel, out_shape=outs, grid_spec=pltpu.PrefetchScalarGrid...  76.4 us
    dot_general x11, matrix products, dot_flip(): lax.dot_general(left, right, (((1,), (1,)), ((), ())), preferred_element_...  44 us
    dot_general x10, matrix products, dot(): return jnp.dot(left, right, preferred_element_type=F32)  38.9 us
    ppermute x34, starting transfers between devices, hop(): return lax.ppermute(values, 'dp', [(i, i ^ step) for i in range(self.n)])  38.8 us
    dot_general x7, matrix products, outer_sum(): lax.dot_general(left, right, (((0,), (0,)), ((), ())), preferred_element_...  28.6 us
    unnamed x217, local copies, waits for them, and re-layouts  25.4 us
    pallas_call x2, Pallas kernels, attend_back(): pl.pallas_call(functools.partial(backward_kernel, causal), out_shape=out_...  23.3 us
  transfers between devices with their start and end apart: 75, of which 33 were waited for; matrix products, arithmetic and copies ran while one was open for 22% of the time, Pallas kernels for 18%

profile of v5, /device:TPU:0, one launch (start us, length us, event | category | flops | bytes accessed | tf_op | source)
XLA Modules:
  0.0 632.5 jit_solution(13766171801489498166)
XLA Ops:
  48.0 16.6 %all-to-all-done.refs_0_ = bf16[4,512,256]{2,1,0:T(8,128)(2,1)S(1)} async-done(((bf16[4,512,256]{2,1,0:T(8,128)(2,1)}), bf16[4,512,256]{2,1,0:T(8,128)(2,1)S(1)}, u32[]{:S(2)}, u32[]{:S(2)}) %all-to-all-start) | async-done | bytes 1048608 | tf_op jit(solution)/shard_map/all_to_all | solution.py:230
  89.0 5.7 assemble.3
  97.6 5.7 add_convert_fusion.query_ref.key_ref.value_ref
  105.4 5.9 attend.2
  111.3 10.8 %collective-permute-done.11.refs_4_ = bf16[3072,128]{1,0:T(8,128)(2,1)S(1)} collective-permute-done((bf16[3072,128]{1,0:T(8,128)(2,1)S(1)}, bf16[3072,128]{1,0:T(8,128)(2,1)S(1)}, u32[]{:S(2)}, u32[]{:S(2)}) %collective-permute-start.11) | collective-permute-done | bytes 786464 | tf_op jit(solution)/shard_map/ppermute | solution.py:773
  127.1 6.9 %all-to-all-start.1 = ((bf16[4,512,256]{2,1,0:T(8,128)(2,1)}), bf16[4,512,256]{2,1,0:T(8,128)(2,1)}, u32[]{:S(2)}, u32[]{:S(2)}) async-start(bf16[4,512,256]{2,1,0:T(8,128)(2,1)} %copy-done.36), calls=%async_computation.1 | async-start | bytes 2097152 | tf_op jit(solution)/shard_map/all_to_all | solution.py:230
  155.2 5.3 all-to-all-done.1.refs_0_
  160.5 8.5 %collective-permute-done.16.refs_2_ = bf16[3072,128]{1,0:T(8,128)(2,1)S(1)} collective-permute-done((bf16[3072,128]{1,0:T(8,128)(2,1)}, bf16[3072,128]{1,0:T(8,128)(2,1)S(1)}, u32[]{:S(2)}, u32[]{:S(2)}) %collective-permute-start.16) | collective-permute-done | bytes 786464 | tf_op jit(solution)/shard_map/ppermute | solution.py:773
  180.5 4.8 all-to-all-start.2
  185.3 5.9 assemble.4
  207.9 9.4 %attend.3 = (bf16[1024,512]{1,0:T(8,128)(2,1)S(1)}, f32[4,2,1024]{2,1,0:T(2,128)S(1)}) custom-call(s32[3]{0:T(128)S(1)} %get-tuple-element.391.info, bf16[1024,512]{1,0:T(8,128)(2,1)S(1)} %add_convert_fusion.5.query_ref, bf16[1024,1024]{1,0:T(8,128)(2,1)S(1)} %add_convert_fusion.1.key_ref.value_ref, bf16[1024,1024]{1,0:T(8,128)(2,1)S(1)} %add_convert_fusion.1.key_ref.value_ref), custom_call_target="tpu_custom_call" | custom-call | flops 20000000000 | bytes 1048576 | tf_op jit(solution)/shard_map/attend/pallas_call | solution.py:490
  228.3 9.7 %assemble.5 = (bf16[1024,2048]{1,0:T(8,128)(2,1)}, bf16[2048,1024]{1,0:T(8,128)(2,1)}) custom-call(s32[4]{0:T(128)} %pad_add_fusion.3.info, bf16[256,2048]{1,0:T(8,128)(2,1)} %refs_0_.7, bf16[3072,128]{1,0:T(8,128)(2,1)} %pick_others.4.refs_1_, bf16[3072,128]{1,0:T(8,128)(2,1)} %copy-done.42, bf16[3072,128]{1,0:T(8,128)(2,1)} %collective-permute-done.17.refs_3_, ...), custom_call_target="tpu_custom_call" | custom-call | bytes 65536 | tf_op jit(solution)/shard_map/assemble/pallas_call | solution.py:48
  238.0 10.1 %multiply_convert_fusion.1 = (bf16[1024,2048]{1,0:T(8,128)(2,1)S(1)}, f32[1024,2048]{1,0:T(8,128)}) fusion(f32[2048]{0:T(1024)S(1)} %bitcast.314, bf16[1024,2048]{1,0:T(8,128)(2,1)} %get-tuple-element.158, bf16[512,1024]{1,0:T(8,128)(2,1)} %collective-permute-done.27, bf16[512,1024]{1,0:T(8,128)(2,1)S(1)} %add_convert_fusion.4), kind=kOutput, calls=%fused_computation.8 | convolution fusion | flops 4311744512 | bytes 18882560 | tf_op jit(solution)/shard_map/dot_general | solution.py:22
  268.8 5.1 convolution_convert_fusion.2
  277.6 7.6 %multiply_convert_fusion = bf16[1024,2048]{1,0:T(8,128)(2,1)S(1)} fusion(f32[1024,2048]{1,0:T(8,128)S(1)} %bitcast.326, f32[2048]{0:T(1024)S(1)} %bitcast.315, bf16[1024,1024]{1,0:T(8,128)(2,1)S(1)} %pad_maximum_fusion.3, bf16[2048,1024]{1,0:T(8,128)(2,1)S(1)} %copy-done.80), kind=kOutput, calls=%fused_computation.7 | convolution fusion | flops 4322230272 | bytes 18882560 | tf_op jit(solution)/shard_map/dot_general | solution.py:26
  291.6 8.7 %all-to-all-start.3 = ((bf16[4,512,256]{2,1,0:T(8,128)(2,1)}), bf16[4,512,256]{2,1,0:T(8,128)(2,1)}, u32[]{:S(2)}, u32[]{:S(2)}) async-start(bf16[4,512,256]{2,1,0:T(8,128)(2,1)} %cut_columns.3), calls=%async_computation.3 | async-start | bytes 2097152 | tf_op jit(solution)/shard_map/all_to_all | solution.py:247
  300.3 7.5 %convolution_convert_fusion.1 = bf16[2048,1024]{1,0:T(8,128)(2,1)S(1)} fusion(bf16[1024,2048]{1,0:T(8,128)(2,1)} %copy-done.33, bf16[512,1024]{1,0:T(8,128)(2,1)} %collective-permute-done.27, bf16[512,1024]{1,0:T(8,128)(2,1)} %copy-done.56), kind=kOutput, calls=%fused_computation.15 | convolution fusion | flops 4301258752 | bytes 10485760 | tf_op jit(solution)/shard_map/dot_general | solution.py:30
  314.2 5.6 multiply_reduce_fusion.1
  325.9 13.9 %attend_back.2 = (bf16[1024,512]{1,0:T(8,128)(2,1)S(1)}, bf16[1024,1024]{1,0:T(8,128)(2,1)S(1)}) custom-call(s32[3]{0:T(128)S(1)} %get-tuple-element.391.info, bf16[1024,512]{1,0:T(8,128)(2,1)S(1)} %copy-done.6, bf16[1024,1024]{1,0:T(8,128)(2,1)} %copy-done, bf16[1024,1024]{1,0:T(8,128)(2,1)} %copy-done, ...), custom_call_target="tpu_custom_call" | custom-call | bytes 65536 | tf_op jit(solution)/shard_map/attend_back/pallas_call | solution.py:525
  339.8 20.2 %collective-permute-done.33.refs_4_ = bf16[2,512,1024]{2,1,0:T(8,128)(2,1)} collective-permute-done((bf16[2,512,1024]{2,1,0:T(8,128)(2,1)}, bf16[2,512,1024]{2,1,0:T(8,128)(2,1)}, u32[]{:S(2)}, u32[]{:S(2)}) %collective-permute-start.33) | collective-permute-done | bytes 2097184 | tf_op jit(solution)/shard_map/ppermute | solution.py:773
  394.7 4.9 sum_chunks.3
  407.6 8.0 %collective-permute-done.39.refs_5_ = bf16[2,256,1024]{2,1,0:T(8,128)(2,1)} collective-permute-done((bf16[2,256,1024]{2,1,0:T(8,128)(2,1)}, bf16[2,256,1024]{2,1,0:T(8,128)(2,1)}, u32[]{:S(2)}, u32[]{:S(2)}) %collective-permute-start.39) | collective-permute-done | bytes 1048608 | tf_op jit(solution)/shard_map/ppermute | solution.py:773
  435.6 4.9 all-to-all-start.4
  446.9 9.3 %attend_back.3 = bf16[1024,1536]{1,0:T(8,128)(2,1)S(1)} custom-call(s32[3]{0:T(128)S(1)} %copy-done.10, bf16[1024,1536]{1,0:T(8,128)(2,1)} %copy-done.12, bf16[1024,1536]{1,0:T(8,128)(2,1)} %copy-done.12, bf16[1024,1536]{1,0:T(8,128)(2,1)} %copy-done.12, bf16[1024,512]{1,0:T(8,128)(2,1)S(1)} %copy-done.11, f32[4,2,1024]{2,1,0:T(2,128)S(1)} %get-tuple-element.171.logsum_ref), custom_call_target="tpu_custom_call" | custom-call | flops 20000000000 | bytes 1048576 | tf_op jit(solution)/shard_map/attend_back/pallas_call | solution.py:525
  458.7 22.6 %all-to-all-done.4 = bf16[4,512,256]{2,1,0:T(8,128)(2,1)} async-done(((bf16[4,512,256]{2,1,0:T(8,128)(2,1)}), bf16[4,512,256]{2,1,0:T(8,128)(2,1)}, u32[]{:S(2)}, u32[]{:S(2)}) %all-to-all-start.4) | async-done | bytes 1048608 | tf_op jit(solution)/shard_map/all_to_all | solution.py:247
  481.3 6.0 convolution_convert_fusion
  499.2 5.0 fusion.16
  508.8 6.0 add_convert_fusion.2.refs_0_
  517.1 13.9 %collective-permute-done.44.refs_1_ = bf16[2,256,1024]{2,1,0:T(8,128)(2,1)} collective-permute-done((bf16[2,256,1024]{2,1,0:T(8,128)(2,1)}, bf16[2,256,1024]{2,1,0:T(8,128)(2,1)}, u32[]{:S(2)}, u32[]{:S(2)}) %collective-permute-start.44) | collective-permute-done | bytes 1048608 | tf_op jit(solution)/shard_map/ppermute | solution.py:773
  551.3 15.8 %collective-permute-done.51 = f32[13312]{0:T(1024)S(1)} collective-permute-done((f32[13312]{0:T(1024)S(1)}, f32[13312]{0:T(1024)S(1)}, u32[]{:S(2)}, u32[]{:S(2)}) %collective-permute-start.51) | collective-permute-done | bytes 53280 | tf_op jit(solution)/shard_map/ppermute | solution.py:773
  586.7 10.3 %collective-permute-done.57 = f32[13312]{0:T(1024)S(1)} collective-permute-done((f32[13312]{0:T(1024)S(1)}, f32[13312]{0:T(1024)S(1)}, u32[]{:S(2)}, u32[]{:S(2)}) %collective-permute-start.57) | collective-permute-done | bytes 53280 | tf_op jit(solution)/shard_map/ppermute | solution.py:1128
  617.3 4.8 finish.5
  (528 shorter events, 323.3 us)
Async XLA Ops:
  22.6 41.9 %all-to-all-start = ((bf16[4,512,256]{2,1,0:T(8,128)(2,1)}), bf16[4,512,256]{2,1,0:T(8,128)(2,1)S(1)}, u32[]{:S(2)}, u32[]{:S(2)}) async-start(bf16[4,512,256]{2,1,0:T(8,128)(2,1)} %constant_dynamic-update-slice_fusion.2), calls=%async_computation | async-start | bytes 2097152 | tf_op jit(solution)/shard_map/all_to_all | solution.py:230
  26.2 68.5 %all-gather.10.cloned.1.call-start = ((), (), s32[]{:S(2)}) async-start(), calls=%async_computation.11 | async-start | bytes 1392640 | tf_op jit(solution)/shard_map/all_gather | solution.py:799
  40.7 93.3 %all-gather.12.cloned.1.call-start = ((), (), s32[]{:S(2)}) async-start(), calls=%async_computation.12 | async-start | bytes 2621440 | tf_op jit(solution)/shard_map/all_gather | solution.py:799
  41.7 39.1 %collective-permute-start.10 = (bf16[2,512,256]{2,1,0:T(8,128)(2,1)}, bf16[2,512,256]{2,1,0:T(8,128)(2,1)}, u32[]{:S(2)}, u32[]{:S(2)}) collective-permute-start(bf16[2,512,256]{2,1,0:T(8,128)(2,1)} %dynamic-slice_bitcast_fusion), channel_id=1, source_target_pairs={{0,4},{4,0},{1,5},{5,1},{2,6},{6,2},{3,7},{7,3},{8,12},{12,8},{9,1... | collective-permute-start | bytes 1572872 | tf_op jit(solution)/shard_map/ppermute | solution.py:189
  43.5 39.1 %collective-permute-start.9 = (bf16[2,512,256]{2,1,0:T(8,128)(2,1)}, bf16[2,512,256]{2,1,0:T(8,128)(2,1)}, u32[]{:S(2)}, u32[]{:S(2)}) collective-permute-start(bf16[2,512,256]{2,1,0:T(8,128)(2,1)} %dynamic-slice_bitcast_fusion.1), channel_id=1, source_target_pairs={{0,4},{4,0},{1,5},{5,1},{2,6},{6,2},{3,7},{7,3},{8,12},{12,8},{9,1... | collective-permute-start | bytes 1572872 | tf_op jit(solution)/shard_map/ppermute | solution.py:189
  44.2 30.2 %collective-permute-start.6 = (bf16[3072,128]{1,0:T(8,128)(2,1)S(1)}, bf16[3072,128]{1,0:T(8,128)(2,1)S(1)}, u32[]{:S(2)}, u32[]{:S(2)}) collective-permute-start(bf16[3072,128]{1,0:T(8,128)(2,1)S(1)} %constant_dynamic-update-slice_fusion.3.refs_2_), channel_id=1, source_target_pairs={{0,16},{8,24},{16,0},{24,8},{1,17},{9,25},{17,1},{25,9},{2,18},{10... | collective-permute-start | bytes 2359304 | tf_op jit(solution)/shard_map/ppermute | solution.py:773
  45.9 30.8 %collective-permute-start.5 = (bf16[3072,128]{1,0:T(8,128)(2,1)S(1)}, bf16[3072,128]{1,0:T(8,128)(2,1)S(1)}, u32[]{:S(2)}, u32[]{:S(2)}) collective-permute-start(bf16[3072,128]{1,0:T(8,128)(2,1)S(1)} %constant_dynamic-update-slice_fusion.3.refs_2_), channel_id=1, source_target_pairs={{0,8},{8,0},{16,24},{24,16},{1,9},{9,1},{17,25},{25,17},{2,10},{10... | collective-permute-start | bytes 2359304 | tf_op jit(solution)/shard_map/ppermute | solution.py:773
  68.5 29.0 %collective-permute-start.1 = (bf16[512,1024]{1,0:T(8,128)(2,1)}, bf16[512,1024]{1,0:T(8,128)(2,1)}, u32[]{:S(2)}, u32[]{:S(2)}) collective-permute-start(bf16[512,1024]{1,0:T(8,128)(2,1)} %join_columns.3), channel_id=1, source_target_pairs={{0,4},{4,0},{1,5},{5,1},{2,6},{6,2},{3,7},{7,3},{8,12},{12,8},{9,1... | collective-permute-start | bytes 3145736 | tf_op jit(solution)/shard_map/ppermute | solution.py:189
  127.1 33.4 %all-to-all-start.1 = ((bf16[4,512,256]{2,1,0:T(8,128)(2,1)}), bf16[4,512,256]{2,1,0:T(8,128)(2,1)}, u32[]{:S(2)}, u32[]{:S(2)}) async-start(bf16[4,512,256]{2,1,0:T(8,128)(2,1)} %copy-done.36), calls=%async_computation.1 | async-start | bytes 2097152 | tf_op jit(solution)/shard_map/all_to_all | solution.py:230
  174.3 28.8 %collective-permute-start.20 = (bf16[3072,128]{1,0:T(8,128)(2,1)S(1)}, bf16[3072,128]{1,0:T(8,128)(2,1)}, u32[]{:S(2)}, u32[]{:S(2)}) collective-permute-start(bf16[3072,128]{1,0:T(8,128)(2,1)S(1)} %copy-done.40), channel_id=1, source_target_pairs={{0,8},{8,0},{16,24},{24,16},{1,9},{9,1},{17,25},{25,17},{2,10},{10... | collective-permute-start | bytes 2359304 | tf_op jit(solution)/shard_map/ppermute | solution.py:773
  175.6 27.6 %collective-permute-start.21 = (bf16[3072,128]{1,0:T(8,128)(2,1)S(1)}, bf16[3072,128]{1,0:T(8,128)(2,1)}, u32[]{:S(2)}, u32[]{:S(2)}) collective-permute-start(bf16[3072,128]{1,0:T(8,128)(2,1)S(1)} %copy-done.40), channel_id=1, source_target_pairs={{0,16},{8,24},{16,0},{24,8},{1,17},{9,25},{17,1},{25,9},{2,18},{10... | collective-permute-start | bytes 2359304 | tf_op jit(solution)/shard_map/ppermute | solution.py:773
  180.5 37.6 %all-to-all-start.2 = ((bf16[4,512,256]{2,1,0:T(8,128)(2,1)}), bf16[4,512,256]{2,1,0:T(8,128)(2,1)S(1)}, u32[]{:S(2)}, u32[]{:S(2)}) async-start(bf16[4,512,256]{2,1,0:T(8,128)(2,1)} %constant_dynamic-update-slice_fusion), calls=%async_computation.2 | async-start | bytes 2097152 | tf_op jit(solution)/shard_map/all_to_all | solution.py:230
  291.6 48.2 %all-to-all-start.3 = ((bf16[4,512,256]{2,1,0:T(8,128)(2,1)}), bf16[4,512,256]{2,1,0:T(8,128)(2,1)}, u32[]{:S(2)}, u32[]{:S(2)}) async-start(bf16[4,512,256]{2,1,0:T(8,128)(2,1)} %cut_columns.3), calls=%async_computation.3 | async-start | bytes 2097152 | tf_op jit(solution)/shard_map/all_to_all | solution.py:247
  300.3 181.0 %reduce-scatter.3.cloned.1.call-start = ((), (), s32[]{:S(2)}) async-start(), calls=%async_computation.8 | async-start | bytes 2621440 | tf_op jit(solution)/shard_map/reduce_scatter | solution.py:1048
  310.6 49.4 %collective-permute-start.33 = (bf16[2,512,1024]{2,1,0:T(8,128)(2,1)}, bf16[2,512,1024]{2,1,0:T(8,128)(2,1)}, u32[]{:S(2)}, u32[]{:S(2)}) collective-permute-start(bf16[2,512,1024]{2,1,0:T(8,128)(2,1)} %bitcast.33), channel_id=1, source_target_pairs={{0,16},{8,24},{16,0},{24,8},{1,17},{9,25},{17,1},{25,9},{2,18},{10... | collective-permute-start | bytes 6291464 | tf_op jit(solution)/shard_map/ppermute | solution.py:773
  314.0 47.5 %collective-permute-start.32 = (bf16[2,512,1024]{2,1,0:T(8,128)(2,1)}, bf16[2,512,1024]{2,1,0:T(8,128)(2,1)}, u32[]{:S(2)}, u32[]{:S(2)}) collective-permute-start(bf16[2,512,1024]{2,1,0:T(8,128)(2,1)} %bitcast.32), channel_id=1, source_target_pairs={{0,8},{8,0},{16,24},{24,16},{1,9},{9,1},{17,25},{25,17},{2,10},{10... | collective-permute-start | bytes 6291464 | tf_op jit(solution)/shard_map/ppermute | solution.py:773
  365.1 26.0 %collective-permute-start.37 = (bf16[512,1024]{1,0:T(8,128)(2,1)S(1)}, bf16[512,1024]{1,0:T(8,128)(2,1)S(1)}, u32[]{:S(2)}, u32[]{:S(2)}) collective-permute-start(bf16[512,1024]{1,0:T(8,128)(2,1)S(1)} %slice_add_fusion), channel_id=1, source_target_pairs={{0,8},{8,0},{16,24},{24,16},{1,9},{9,1},{17,25},{25,17},{2,10},{10... | collective-permute-start | bytes 3145736 | tf_op jit(solution)/shard_map/ppermute | solution.py:773
  367.6 26.1 %collective-permute-start.36 = (bf16[512,1024]{1,0:T(8,128)(2,1)S(1)}, bf16[512,1024]{1,0:T(8,128)(2,1)S(1)}, u32[]{:S(2)}, u32[]{:S(2)}) collective-permute-start(bf16[512,1024]{1,0:T(8,128)(2,1)S(1)} %slice_add_fusion.1), channel_id=1, source_target_pairs={{0,16},{8,24},{16,0},{24,8},{1,17},{9,25},{17,1},{25,9},{2,18},{10... | collective-permute-start | bytes 3145736 | tf_op jit(solution)/shard_map/ppermute | solution.py:773
  379.4 36.1 %collective-permute-start.39 = (bf16[2,256,1024]{2,1,0:T(8,128)(2,1)}, bf16[2,256,1024]{2,1,0:T(8,128)(2,1)}, u32[]{:S(2)}, u32[]{:S(2)}) collective-permute-start(bf16[2,256,1024]{2,1,0:T(8,128)(2,1)} %bitcast.40), channel_id=1, source_target_pairs={{0,16},{8,24},{16,0},{24,8},{1,17},{9,25},{17,1},{25,9},{2,18},{10... | collective-permute-start | bytes 3145736 | tf_op jit(solution)/shard_map/ppermute | solution.py:773
  383.4 32.2 %collective-permute-start.38 = (bf16[2,256,1024]{2,1,0:T(8,128)(2,1)}, bf16[2,256,1024]{2,1,0:T(8,128)(2,1)}, u32[]{:S(2)}, u32[]{:S(2)}) collective-permute-start(bf16[2,256,1024]{2,1,0:T(8,128)(2,1)} %pad_maximum_fusion.16), channel_id=1, source_target_pairs={{0,8},{8,0},{16,24},{24,16},{1,9},{9,1},{17,25},{25,17},{2,10},{10... | collective-permute-start | bytes 3145736 | tf_op jit(solution)/shard_map/ppermute | solution.py:773
  391.2 37.6 %collective-permute-start.42 = (f32[512,1024]{1,0:T(8,128)}, f32[512,1024]{1,0:T(8,128)}, u32[]{:S(2)}, u32[]{:S(2)}) collective-permute-start(f32[512,1024]{1,0:T(8,128)} %fusion.27), channel_id=1, source_target_pairs={{0,4},{4,0},{1,5},{5,1},{2,6},{6,2},{3,7},{7,3},{8,12},{12,8},{9,1... | collective-permute-start | bytes 6291464 | tf_op jit(solution)/shard_map/ppermute | solution.py:189
  435.6 45.7 %all-to-all-start.4 = ((bf16[4,512,256]{2,1,0:T(8,128)(2,1)}), bf16[4,512,256]{2,1,0:T(8,128)(2,1)}, u32[]{:S(2)}, u32[]{:S(2)}) async-start(bf16[4,512,256]{2,1,0:T(8,128)(2,1)} %cut_columns.4), calls=%async_computation.5 | async-start | bytes 2097152 | tf_op jit(solution)/shard_map/all_to_all | solution.py:247
  440.5 105.6 %reduce-scatter.5.cloned.1.call-start = ((), (), s32[]{:S(2)}) async-start(), calls=%async_computation.9 | async-start | bytes 1310720 | tf_op jit(solution)/shard_map/reduce_scatter | solution.py:1070
  442.6 38.7 %collective-permute-start.41 = (bf16[256,1024]{1,0:T(8,128)(2,1)}, bf16[256,1024]{1,0:T(8,128)(2,1)}, u32[]{:S(2)}, u32[]{:S(2)}) collective-permute-start(bf16[256,1024]{1,0:T(8,128)(2,1)} %slice_add_fusion.3), channel_id=1, source_target_pairs={{0,8},{8,0},{16,24},{24,16},{1,9},{9,1},{17,25},{25,17},{2,10},{10... | collective-permute-start | bytes 1572872 | tf_op jit(solution)/shard_map/ppermute | solution.py:773
  446.1 35.2 %collective-permute-start.40 = (bf16[256,1024]{1,0:T(8,128)(2,1)}, bf16[256,1024]{1,0:T(8,128)(2,1)}, u32[]{:S(2)}, u32[]{:S(2)}) collective-permute-start(bf16[256,1024]{1,0:T(8,128)(2,1)} %maximum_add_fusion), channel_id=1, source_target_pairs={{0,16},{8,24},{16,0},{24,8},{1,17},{9,25},{17,1},{25,9},{2,18},{10... | collective-permute-start | bytes 1572872 | tf_op jit(solution)/shard_map/ppermute | solution.py:773
  493.0 88.6 %all-gather.14.cloned.1.call-start = ((), (), s32[]{:S(2)}) async-start(), calls=%async_computation.13 | async-start | bytes 2621440 | tf_op jit(solution)/shard_map/all_gather | solution.py:1114
  498.5 42.8 %collective-permute-start.50 = (bf16[2,512,256]{2,1,0:T(8,128)(2,1)}, bf16[2,512,256]{2,1,0:T(8,128)(2,1)}, u32[]{:S(2)}, u32[]{:S(2)}) collective-permute-start(bf16[2,512,256]{2,1,0:T(8,128)(2,1)} %get-tuple-element.331), channel_id=1, source_target_pairs={{0,4},{4,0},{1,5},{5,1},{2,6},{6,2},{3,7},{7,3},{8,12},{12,8},{9,1... | collective-permute-start | bytes 1572872 | tf_op jit(solution)/shard_map/ppermute | solution.py:189
  504.6 26.4 %collective-permute-start.44 = (bf16[2,256,1024]{2,1,0:T(8,128)(2,1)}, bf16[2,256,1024]{2,1,0:T(8,128)(2,1)}, u32[]{:S(2)}, u32[]{:S(2)}) collective-permute-start(bf16[2,256,1024]{2,1,0:T(8,128)(2,1)} %slice.411), channel_id=1, source_target_pairs={{0,8},{8,0},{16,24},{24,16},{1,9},{9,1},{17,25},{25,17},{2,10},{10... | collective-permute-start | bytes 3145736 | tf_op jit(solution)/shard_map/ppermute | solution.py:773
  506.0 27.4 %collective-permute-start.45 = (bf16[2,256,1024]{2,1,0:T(8,128)(2,1)}, bf16[2,256,1024]{2,1,0:T(8,128)(2,1)}, u32[]{:S(2)}, u32[]{:S(2)}) collective-permute-start(bf16[2,256,1024]{2,1,0:T(8,128)(2,1)} %pad_maximum_fusion.17), channel_id=1, source_target_pairs={{0,16},{8,24},{16,0},{24,8},{1,17},{9,25},{17,1},{25,9},{2,18},{10... | collective-permute-start | bytes 3145736 | tf_op jit(solution)/shard_map/ppermute | solution.py:773
  533.4 37.1 %all-to-all-start.5 = ((bf16[4,512,256]{2,1,0:T(8,128)(2,1)}), bf16[4,512,256]{2,1,0:T(8,128)(2,1)S(1)}, u32[]{:S(2)}, u32[]{:S(2)}) async-start(bf16[4,512,256]{2,1,0:T(8,128)(2,1)} %cut_columns.5), calls=%async_computation.6 | async-start | bytes 2097152 | tf_op jit(solution)/shard_map/all_to_all | solution.py:247
  537.0 63.5 %all-gather.8.cloned.1.call-start = ((), (), s32[]{:S(2)}) async-start(), calls=%async_computation.10 | async-start | bytes 1310720 | tf_op jit(solution)/shard_map/all_gather | solution.py:1130
  574.8 25.7 %collective-permute-start.53 = (bf16[512,256]{1,0:T(8,128)(2,1)}, bf16[512,256]{1,0:T(8,128)(2,1)S(1)}, u32[]{:S(2)}, u32[]{:S(2)}) collective-permute-start(bf16[512,256]{1,0:T(8,128)(2,1)} %get-tuple-element.197), channel_id=1, source_target_pairs={{0,3},{1,0},{2,1},{3,2},{4,7},{5,4},{6,5},{7,6},{8,11},{9,8},{10,9... | collective-permute-start | bytes 786440 | tf_op jit(solution)/shard_map/ppermute | solution.py:193
  (134 other events, 1350.4 us)
Sparse Core Ops, SparseCore 0:
  40.9 45.2 all-gather.9
  88.3 45.4 all-gather.11
  415.7 57.8 reduce-scatter.2
  493.2 26.1 reduce-scatter.4
  521.1 38.2 all-gather.13
  561.1 25.6 all-gather.7

commit v6 on v5

--- a/solution.py
+++ b/solution.py
@@ -952,10 +952,9 @@
         normed, normal_one, inverse_one = normalize(own_x.astype(F32) + branch, gain_rows[0], shift_rows[0])
         own_first = normed.astype(BF)
         if tiled:
-            own_first, corner_two, over_a, others_b, encoder_takes, cotangent = tie(
-                own_first, corner_two, over_a, others_b, encoder_takes, cotangent
-            )
-            corner_a = blocks.corner(over_a)
+            own_first, corner_two, others_b, encoder_takes, cotangent = tie(
+                own_first, corner_two, others_b, encoder_takes, cotangent
+            )
             over_b = blocks.hops(others_b)
         own_encoder = plan.spread_end(encoder_takes)
         full_encoder = plan.gather_rows(own_encoder)
@@ -968,11 +967,12 @@
         cross_q = (dot(full_first, w_query) + query_bias).astype(BF)
         cotangent_takes = plan.spread(cotangent)
         if tiled:
-            cross_q, memory, over_b, corner_a = tie(cross_q, memory, over_b, corner_a)
+            cross_q, memory, over_a, over_b = tie(cross_q, memory, over_a, over_b)
+            corner_a = blocks.corner(over_a)
             corner_b = blocks.corner(over_b)
         recall, cross_logsum = cross_attention(plan, cross_q, memory, answers, passages, n)
         if tiled:
-            recall, corner_b, cotangent_takes = tie(recall, corner_b, cotangent_takes)
+            recall, corner_a, corner_b, cotangent_takes = tie(recall, corner_a, corner_b, cotangent_takes)
         branch = plan.scatter_product(recall, w_cross_out) + bias_rows[1]
         normed, normal_two, inverse_two = normalize(own_first.astype(F32) + branch, gain_rows[1], shift_rows[1])
         own_second = normed.astype(BF)
@@ -1042,9 +1042,7 @@
                 False,
             )
             grad_self_out = blocks.product(mixture, full_dself)
-            d_mixture, sums, got_cross_a, got_cross_b, grad_self_out = tie(
-                d_mixture, sums, got_cross_a, got_cross_b, grad_self_out
-            )
+            d_mixture, sums, grad_self_out = tie(d_mixture, sums, grad_self_out)
             mine_hidden = lax.psum_scatter(sums, "col", scatter_dimension=0, tiled=False)
             chunk_cross_a = blocks.reduce_next(of_cross_a, 1, got_cross_a)
             chunk_cross_b = blocks.reduce_next(of_cross_b, 2, got_cross_b)

time: 644 us -> 642 us (level)
  Pallas kernels: 124 us -> 151 us
  waiting for transfers between devices: 178 us -> 154 us
    all_to_all x3, waiting for transfers between devices: 22.6 us -> 1.24 us  [deal(): return lax.all_to_all(blocks, 'col', 0, 0, tiled=True)]
    pallas_call x2, Pallas kernels: 23.3 us -> 42.8 us  [attend_back(): pl.pallas_call(functools.partial(backward_kernel, causal), out_shape=out_...]
    pallas_call x2, Pallas kernels: 15.3 us -> 23.7 us  [attend(): pl.pallas_call(functools.partial(forward_kernel, causal), out_shape=(jax....]
  transfers between devices with their start and end apart: 75 -> 75, of which waited for: 33 -> 32; matrix products, arithmetic and copies ran while one was open for 22% -> 22% of each run, Pallas kernels for 18% -> 23%
where the time goes in v6:
time: 642 us; the launch traced here: 632 us
  waiting for transfers between devices  154 us (24%)
  Pallas kernels  151 us (24%)
  matrix products  113 us (18%)
  starting transfers between devices  88.3 us (14%)
  local copies, waits for them, and re-layouts  68.7 us (11%)
  other arithmetic  32.8 us (5%)
  between operations  24.1 us (4%)
    ppermute x34, waiting for transfers between devices, hop(): return lax.ppermute(values, 'dp', [(i, i ^ step) for i in range(self.n)])  101 us
    pallas_call x21, Pallas kernels, in_vmem(): pl.pallas_call(kernel, out_shape=outs, grid_spec=pltpu.PrefetchScalarGrid...  76.2 us
    dot_general x11, matrix products, dot_flip(): lax.dot_general(left, right, (((1,), (1,)), ((), ())), preferred_element_...  42.9 us
    pallas_call x2, Pallas kernels, attend_back(): pl.pallas_call(functools.partial(backward_kernel, causal), out_shape=out_...  42.8 us
    ppermute x34, starting transfers between devices, hop(): return lax.ppermute(values, 'dp', [(i, i ^ step) for i in range(self.n)])  41.5 us
    dot_general x10, matrix products, dot(): return jnp.dot(left, right, preferred_element_type=F32)  38.2 us
    dot_general x7, matrix products, outer_sum(): lax.dot_general(left, right, (((0,), (0,)), ((), ())), preferred_element_...  32.1 us
    unnamed x217, local copies, waits for them, and re-layouts  26.5 us
  transfers between devices with their start and end apart: 75, of which 32 were waited for; matrix products, arithmetic and copies ran while one was open for 22% of the time, Pallas kernels for 23%

profile of v6, /device:TPU:0, one launch (start us, length us, event | category | flops | bytes accessed | tf_op | source)
XLA Modules:
  0.0 631.9 jit_solution(15438984987115026198)
XLA Ops:
  48.0 16.5 %all-to-all-done.refs_0_ = bf16[4,512,256]{2,1,0:T(8,128)(2,1)S(1)} async-done(((bf16[4,512,256]{2,1,0:T(8,128)(2,1)}), bf16[4,512,256]{2,1,0:T(8,128)(2,1)S(1)}, u32[]{:S(2)}, u32[]{:S(2)}) %all-to-all-start) | async-done | bytes 1048608 | tf_op jit(solution)/shard_map/all_to_all | solution.py:230
  89.0 5.7 assemble.3
  97.6 5.7 add_convert_fusion.query_ref.key_ref.value_ref
  105.4 10.4 %attend.2 = (bf16[1024,512]{1,0:T(8,128)(2,1)S(1)}, f32[4,2,1024]{2,1,0:T(2,128)S(1)}) custom-call(s32[3]{0:T(128)S(1)} %get-tuple-element.386.info, bf16[1024,1536]{1,0:T(8,128)(2,1)S(1)} %add_convert_fusion.query_ref.key_ref.value_ref, bf16[1024,1536]{1,0:T(8,128)(2,1)S(1)} %add_convert_fusion.query_ref.key_ref.value_ref, ...), custom_call_target="tpu_custom_call" | custom-call | flops 20000000000 | bytes 1048576 | tf_op jit(solution)/shard_map/attend/pallas_call | solution.py:490
  115.9 6.3 collective-permute-done.11.refs_4_
  127.1 6.9 %all-to-all-start.1 = ((bf16[4,512,256]{2,1,0:T(8,128)(2,1)}), bf16[4,512,256]{2,1,0:T(8,128)(2,1)}, u32[]{:S(2)}, u32[]{:S(2)}) async-start(bf16[4,512,256]{2,1,0:T(8,128)(2,1)} %copy-done.35), calls=%async_computation.1 | async-start | bytes 2097152 | tf_op jit(solution)/shard_map/all_to_all | solution.py:230
  153.8 6.7 %all-to-all-done.1.refs_0_ = bf16[4,512,256]{2,1,0:T(8,128)(2,1)} async-done(((bf16[4,512,256]{2,1,0:T(8,128)(2,1)}), bf16[4,512,256]{2,1,0:T(8,128)(2,1)}, u32[]{:S(2)}, u32[]{:S(2)}) %all-to-all-start.1) | async-done | bytes 1048608 | tf_op jit(solution)/shard_map/all_to_all | solution.py:230
  171.1 5.9 assemble.4
  185.5 15.1 %collective-permute-done.18.refs_2_ = bf16[3072,128]{1,0:T(8,128)(2,1)} collective-permute-done((bf16[3072,128]{1,0:T(8,128)(2,1)S(1)}, bf16[3072,128]{1,0:T(8,128)(2,1)}, u32[]{:S(2)}, u32[]{:S(2)}) %collective-permute-start.18) | collective-permute-done | bytes 786464 | tf_op jit(solution)/shard_map/ppermute | solution.py:773
  208.5 13.2 %attend.3 = (bf16[1024,512]{1,0:T(8,128)(2,1)S(1)}, f32[4,2,1024]{2,1,0:T(2,128)S(1)}) custom-call(s32[3]{0:T(128)S(1)} %get-tuple-element.387.info, bf16[1024,512]{1,0:T(8,128)(2,1)S(1)} %add_convert_fusion.5.query_ref, bf16[1024,1024]{1,0:T(8,128)(2,1)S(1)} %add_convert_fusion.1.key_ref.value_ref, bf16[1024,1024]{1,0:T(8,128)(2,1)S(1)} %add_convert_fusion.1.key_ref.value_ref), custom_call_target="tpu_custom_call" | custom-call | flops 20000000000 | bytes 1048576 | tf_op jit(solution)/shard_map/attend/pallas_call | solution.py:490
  233.7 9.7 %assemble.5 = (bf16[1024,2048]{1,0:T(8,128)(2,1)}, bf16[2048,1024]{1,0:T(8,128)(2,1)}) custom-call(s32[4]{0:T(128)} %pad_add_fusion.3.info, bf16[256,2048]{1,0:T(8,128)(2,1)} %refs_0_.7, bf16[3072,128]{1,0:T(8,128)(2,1)} %pick_others.4.refs_1_, bf16[3072,128]{1,0:T(8,128)(2,1)} %collective-permute-done.18.refs_2_, bf16[3072,128]{1,0:T(8,128)(2,1)} %copy-done.43, ...), custom_call_target="tpu_custom_call" | custom-call | bytes 65536 | tf_op jit(solution)/shard_map/assemble/pallas_call | solution.py:48
  243.4 10.1 %multiply_convert_fusion.1 = (bf16[1024,2048]{1,0:T(8,128)(2,1)S(1)}, f32[1024,2048]{1,0:T(8,128)}) fusion(f32[2048]{0:T(1024)S(1)} %bitcast.318, bf16[1024,2048]{1,0:T(8,128)(2,1)} %get-tuple-element.156, bf16[512,1024]{1,0:T(8,128)(2,1)} %collective-permute-done.27, bf16[512,1024]{1,0:T(8,128)(2,1)S(1)} %add_convert_fusion.4), kind=kOutput, calls=%fused_computation.8 | convolution fusion | flops 4311744512 | bytes 18882560 | tf_op jit(solution)/shard_map/dot_general | solution.py:22
  261.6 4.7 fusion.91
  274.1 5.1 convolution_convert_fusion.2
  282.9 7.6 %multiply_convert_fusion = bf16[1024,2048]{1,0:T(8,128)(2,1)S(1)} fusion(f32[1024,2048]{1,0:T(8,128)S(1)} %bitcast.330, f32[2048]{0:T(1024)S(1)} %bitcast.319, bf16[1024,1024]{1,0:T(8,128)(2,1)S(1)} %pad_maximum_fusion.3, bf16[2048,1024]{1,0:T(8,128)(2,1)S(1)} %copy-done.78), kind=kOutput, calls=%fused_computation.7 | convolution fusion | flops 4322230272 | bytes 18882560 | tf_op jit(solution)/shard_map/dot_general | solution.py:26
  301.2 7.5 %convolution_convert_fusion.1 = bf16[2048,1024]{1,0:T(8,128)(2,1)S(1)} fusion(bf16[1024,2048]{1,0:T(8,128)(2,1)} %copy-done.32, bf16[512,1024]{1,0:T(8,128)(2,1)} %collective-permute-done.27, bf16[512,1024]{1,0:T(8,128)(2,1)} %copy-done.55), kind=kOutput, calls=%fused_computation.15 | convolution fusion | flops 4301258752 | bytes 10485760 | tf_op jit(solution)/shard_map/dot_general | solution.py:30
  315.9 5.6 multiply_reduce_fusion.1
  327.5 24.0 %attend_back.2 = (bf16[1024,512]{1,0:T(8,128)(2,1)S(1)}, bf16[1024,1024]{1,0:T(8,128)(2,1)S(1)}) custom-call(s32[3]{0:T(128)S(1)} %get-tuple-element.387.info, bf16[1024,512]{1,0:T(8,128)(2,1)S(1)} %copy-done.5, bf16[1024,1024]{1,0:T(8,128)(2,1)} %copy-done, bf16[1024,1024]{1,0:T(8,128)(2,1)} %copy-done, ...), custom_call_target="tpu_custom_call" | custom-call | bytes 65536 | tf_op jit(solution)/shard_map/attend_back/pallas_call | solution.py:525
  351.5 10.7 %collective-permute-done.33.refs_4_ = bf16[2,512,1024]{2,1,0:T(8,128)(2,1)} collective-permute-done((bf16[2,512,1024]{2,1,0:T(8,128)(2,1)}, bf16[2,512,1024]{2,1,0:T(8,128)(2,1)}, u32[]{:S(2)}, u32[]{:S(2)}) %collective-permute-start.33) | collective-permute-done | bytes 2097184 | tf_op jit(solution)/shard_map/ppermute | solution.py:773
  378.1 5.0 convolution_convert_fusion.3
  383.1 10.0 %collective-permute-done.37.refs_5_ = bf16[512,1024]{1,0:T(8,128)(2,1)S(1)} collective-permute-done((bf16[512,1024]{1,0:T(8,128)(2,1)S(1)}, bf16[512,1024]{1,0:T(8,128)(2,1)S(1)}, u32[]{:S(2)}, u32[]{:S(2)}) %collective-permute-start.37) | collective-permute-done | bytes 1048608 | tf_op jit(solution)/shard_map/ppermute | solution.py:773
  396.0 4.9 sum_chunks.3
  430.1 7.8 %collective-permute-done.40.refs_5_ = bf16[2,256,1024]{2,1,0:T(8,128)(2,1)} collective-permute-done((bf16[2,256,1024]{2,1,0:T(8,128)(2,1)}, bf16[2,256,1024]{2,1,0:T(8,128)(2,1)}, u32[]{:S(2)}, u32[]{:S(2)}) %collective-permute-start.40) | collective-permute-done | bytes 1048608 | tf_op jit(solution)/shard_map/ppermute | solution.py:773
  451.7 4.7 all-to-all-start.4
  457.6 18.8 %attend_back.3 = bf16[1024,1536]{1,0:T(8,128)(2,1)S(1)} custom-call(s32[3]{0:T(128)S(1)} %copy-done.9, bf16[1024,1536]{1,0:T(8,128)(2,1)} %copy-done.11, bf16[1024,1536]{1,0:T(8,128)(2,1)} %copy-done.11, bf16[1024,1536]{1,0:T(8,128)(2,1)} %copy-done.11, bf16[1024,512]{1,0:T(8,128)(2,1)S(1)} %copy-done.10, f32[4,2,1024]{2,1,0:T(2,128)S(1)} %get-tuple-element.168.logsum_ref), custom_call_target="tpu_custom_call" | custom-call | flops 20000000000 | bytes 1048576 | tf_op jit(solution)/shard_map/attend_back/pallas_call | solution.py:525
  480.2 6.0 convolution_convert_fusion
  498.1 5.0 fusion.16
  507.7 6.0 add_convert_fusion.2.refs_0_
  516.0 13.1 %collective-permute-done.44.refs_1_ = bf16[2,256,1024]{2,1,0:T(8,128)(2,1)} collective-permute-done((bf16[2,256,1024]{2,1,0:T(8,128)(2,1)}, bf16[2,256,1024]{2,1,0:T(8,128)(2,1)}, u32[]{:S(2)}, u32[]{:S(2)}) %collective-permute-start.44) | collective-permute-done | bytes 1048608 | tf_op jit(solution)/shard_map/ppermute | solution.py:773
  548.7 17.9 %collective-permute-done.51 = f32[13312]{0:T(1024)S(1)} collective-permute-done((f32[13312]{0:T(1024)S(1)}, f32[13312]{0:T(1024)S(1)}, u32[]{:S(2)}, u32[]{:S(2)}) %collective-permute-start.51) | collective-permute-done | bytes 53280 | tf_op jit(solution)/shard_map/ppermute | solution.py:773
  586.1 10.3 %collective-permute-done.57 = f32[13312]{0:T(1024)S(1)} collective-permute-done((f32[13312]{0:T(1024)S(1)}, f32[13312]{0:T(1024)S(1)}, u32[]{:S(2)}, u32[]{:S(2)}) %collective-permute-start.57) | collective-permute-done | bytes 53280 | tf_op jit(solution)/shard_map/ppermute | solution.py:1126
  616.7 4.8 finish.5
  (529 shorter events, 316.2 us)
Async XLA Ops:
  22.6 41.9 %all-to-all-start = ((bf16[4,512,256]{2,1,0:T(8,128)(2,1)}), bf16[4,512,256]{2,1,0:T(8,128)(2,1)S(1)}, u32[]{:S(2)}, u32[]{:S(2)}) async-start(bf16[4,512,256]{2,1,0:T(8,128)(2,1)} %constant_dynamic-update-slice_fusion.2), calls=%async_computation | async-start | bytes 2097152 | tf_op jit(solution)/shard_map/all_to_all | solution.py:230
  26.2 68.5 %all-gather.10.cloned.1.call-start = ((), (), s32[]{:S(2)}) async-start(), calls=%async_computation.11 | async-start | bytes 1392640 | tf_op jit(solution)/shard_map/all_gather | solution.py:799
  40.7 93.3 %all-gather.12.cloned.1.call-start = ((), (), s32[]{:S(2)}) async-start(), calls=%async_computation.12 | async-start | bytes 2621440 | tf_op jit(solution)/shard_map/all_gather | solution.py:799
  41.7 39.2 %collective-permute-start.10 = (bf16[2,512,256]{2,1,0:T(8,128)(2,1)}, bf16[2,512,256]{2,1,0:T(8,128)(2,1)}, u32[]{:S(2)}, u32[]{:S(2)}) collective-permute-start(bf16[2,512,256]{2,1,0:T(8,128)(2,1)} %dynamic-slice_bitcast_fusion), channel_id=1, source_target_pairs={{0,4},{4,0},{1,5},{5,1},{2,6},{6,2},{3,7},{7,3},{8,12},{12,8},{9,1... | collective-permute-start | bytes 1572872 | tf_op jit(solution)/shard_map/ppermute | solution.py:189
  43.5 39.2 %collective-permute-start.9 = (bf16[2,512,256]{2,1,0:T(8,128)(2,1)}, bf16[2,512,256]{2,1,0:T(8,128)(2,1)}, u32[]{:S(2)}, u32[]{:S(2)}) collective-permute-start(bf16[2,512,256]{2,1,0:T(8,128)(2,1)} %dynamic-slice_bitcast_fusion.1), channel_id=1, source_target_pairs={{0,4},{4,0},{1,5},{5,1},{2,6},{6,2},{3,7},{7,3},{8,12},{12,8},{9,1... | collective-permute-start | bytes 1572872 | tf_op jit(solution)/shard_map/ppermute | solution.py:189
  44.1 30.2 %collective-permute-start.6 = (bf16[3072,128]{1,0:T(8,128)(2,1)S(1)}, bf16[3072,128]{1,0:T(8,128)(2,1)S(1)}, u32[]{:S(2)}, u32[]{:S(2)}) collective-permute-start(bf16[3072,128]{1,0:T(8,128)(2,1)S(1)} %constant_dynamic-update-slice_fusion.3.refs_2_), channel_id=1, source_target_pairs={{0,16},{8,24},{16,0},{24,8},{1,17},{9,25},{17,1},{25,9},{2,18},{10... | collective-permute-start | bytes 2359304 | tf_op jit(solution)/shard_map/ppermute | solution.py:773
  45.9 30.8 %collective-permute-start.5 = (bf16[3072,128]{1,0:T(8,128)(2,1)S(1)}, bf16[3072,128]{1,0:T(8,128)(2,1)S(1)}, u32[]{:S(2)}, u32[]{:S(2)}) collective-permute-start(bf16[3072,128]{1,0:T(8,128)(2,1)S(1)} %constant_dynamic-update-slice_fusion.3.refs_2_), channel_id=1, source_target_pairs={{0,8},{8,0},{16,24},{24,16},{1,9},{9,1},{17,25},{25,17},{2,10},{10... | collective-permute-start | bytes 2359304 | tf_op jit(solution)/shard_map/ppermute | solution.py:773
  68.5 29.0 %collective-permute-start.1 = (bf16[512,1024]{1,0:T(8,128)(2,1)}, bf16[512,1024]{1,0:T(8,128)(2,1)}, u32[]{:S(2)}, u32[]{:S(2)}) collective-permute-start(bf16[512,1024]{1,0:T(8,128)(2,1)} %join_columns.3), channel_id=1, source_target_pairs={{0,4},{4,0},{1,5},{5,1},{2,6},{6,2},{3,7},{7,3},{8,12},{12,8},{9,1... | collective-permute-start | bytes 3145736 | tf_op jit(solution)/shard_map/ppermute | solution.py:189
  127.1 33.4 %all-to-all-start.1 = ((bf16[4,512,256]{2,1,0:T(8,128)(2,1)}), bf16[4,512,256]{2,1,0:T(8,128)(2,1)}, u32[]{:S(2)}, u32[]{:S(2)}) async-start(bf16[4,512,256]{2,1,0:T(8,128)(2,1)} %copy-done.35), calls=%async_computation.1 | async-start | bytes 2097152 | tf_op jit(solution)/shard_map/all_to_all | solution.py:230
  166.3 34.4 %collective-permute-start.18 = (bf16[3072,128]{1,0:T(8,128)(2,1)S(1)}, bf16[3072,128]{1,0:T(8,128)(2,1)}, u32[]{:S(2)}, u32[]{:S(2)}) collective-permute-start(bf16[3072,128]{1,0:T(8,128)(2,1)S(1)} %copy-done.39), channel_id=1, source_target_pairs={{0,8},{8,0},{16,24},{24,16},{1,9},{9,1},{17,25},{25,17},{2,10},{10... | collective-permute-start | bytes 2359304 | tf_op jit(solution)/shard_map/ppermute | solution.py:773
  167.5 56.0 %all-to-all-start.2 = ((bf16[4,512,256]{2,1,0:T(8,128)(2,1)}), bf16[4,512,256]{2,1,0:T(8,128)(2,1)S(1)}, u32[]{:S(2)}, u32[]{:S(2)}) async-start(bf16[4,512,256]{2,1,0:T(8,128)(2,1)} %constant_dynamic-update-slice_fusion), calls=%async_computation.2 | async-start | bytes 2097152 | tf_op jit(solution)/shard_map/all_to_all | solution.py:230
  296.9 54.6 %all-to-all-start.3 = ((bf16[4,512,256]{2,1,0:T(8,128)(2,1)}), bf16[4,512,256]{2,1,0:T(8,128)(2,1)}, u32[]{:S(2)}, u32[]{:S(2)}) async-start(bf16[4,512,256]{2,1,0:T(8,128)(2,1)} %cut_columns.3), calls=%async_computation.3 | async-start | bytes 2097152 | tf_op jit(solution)/shard_map/all_to_all | solution.py:247
  301.1 179.1 %reduce-scatter.3.cloned.1.call-start = ((), (), s32[]{:S(2)}) async-start(), calls=%async_computation.8 | async-start | bytes 2621440 | tf_op jit(solution)/shard_map/reduce_scatter | solution.py:1046
  311.5 50.7 %collective-permute-start.33 = (bf16[2,512,1024]{2,1,0:T(8,128)(2,1)}, bf16[2,512,1024]{2,1,0:T(8,128)(2,1)}, u32[]{:S(2)}, u32[]{:S(2)}) collective-permute-start(bf16[2,512,1024]{2,1,0:T(8,128)(2,1)} %bitcast.33), channel_id=1, source_target_pairs={{0,16},{8,24},{16,0},{24,8},{1,17},{9,25},{17,1},{25,9},{2,18},{10... | collective-permute-start | bytes 6291464 | tf_op jit(solution)/shard_map/ppermute | solution.py:773
  315.9 47.8 %collective-permute-start.32 = (bf16[2,512,1024]{2,1,0:T(8,128)(2,1)}, bf16[2,512,1024]{2,1,0:T(8,128)(2,1)}, u32[]{:S(2)}, u32[]{:S(2)}) collective-permute-start(bf16[2,512,1024]{2,1,0:T(8,128)(2,1)} %bitcast.32), channel_id=1, source_target_pairs={{0,8},{8,0},{16,24},{24,16},{1,9},{9,1},{17,25},{25,17},{2,10},{10... | collective-permute-start | bytes 6291464 | tf_op jit(solution)/shard_map/ppermute | solution.py:773
  367.5 25.6 %collective-permute-start.37 = (bf16[512,1024]{1,0:T(8,128)(2,1)S(1)}, bf16[512,1024]{1,0:T(8,128)(2,1)S(1)}, u32[]{:S(2)}, u32[]{:S(2)}) collective-permute-start(bf16[512,1024]{1,0:T(8,128)(2,1)S(1)} %slice_add_fusion), channel_id=1, source_target_pairs={{0,8},{8,0},{16,24},{24,16},{1,9},{9,1},{17,25},{25,17},{2,10},{10... | collective-permute-start | bytes 3145736 | tf_op jit(solution)/shard_map/ppermute | solution.py:773
  369.7 25.3 %collective-permute-start.36 = (bf16[512,1024]{1,0:T(8,128)(2,1)S(1)}, bf16[512,1024]{1,0:T(8,128)(2,1)S(1)}, u32[]{:S(2)}, u32[]{:S(2)}) collective-permute-start(bf16[512,1024]{1,0:T(8,128)(2,1)S(1)} %slice_add_fusion.1), channel_id=1, source_target_pairs={{0,16},{8,24},{16,0},{24,8},{1,17},{9,25},{17,1},{25,9},{2,18},{10... | collective-permute-start | bytes 3145736 | tf_op jit(solution)/shard_map/ppermute | solution.py:773
  375.0 25.9 %collective-permute-start.35 = (bf16[512,1024]{1,0:T(8,128)(2,1)}, bf16[512,1024]{1,0:T(8,128)(2,1)}, u32[]{:S(2)}, u32[]{:S(2)}) collective-permute-start(bf16[512,1024]{1,0:T(8,128)(2,1)} %get-tuple-element.318), channel_id=1, source_target_pairs={{0,4},{4,0},{1,5},{5,1},{2,6},{6,2},{3,7},{7,3},{8,12},{12,8},{9,1... | collective-permute-start | bytes 3145736 | tf_op jit(solution)/shard_map/ppermute | solution.py:189
  377.6 67.8 %collective-permute-start.42 = (f32[512,1024]{1,0:T(8,128)}, f32[512,1024]{1,0:T(8,128)}, u32[]{:S(2)}, u32[]{:S(2)}) collective-permute-start(f32[512,1024]{1,0:T(8,128)} %fusion.27), channel_id=1, source_target_pairs={{0,4},{4,0},{1,5},{5,1},{2,6},{6,2},{3,7},{7,3},{8,12},{12,8},{9,1... | collective-permute-start | bytes 6291464 | tf_op jit(solution)/shard_map/ppermute | solution.py:189
  440.0 39.0 %collective-permute-start.41 = (bf16[256,1024]{1,0:T(8,128)(2,1)}, bf16[256,1024]{1,0:T(8,128)(2,1)}, u32[]{:S(2)}, u32[]{:S(2)}) collective-permute-start(bf16[256,1024]{1,0:T(8,128)(2,1)} %fusion.31), channel_id=1, source_target_pairs={{0,8},{8,0},{16,24},{24,16},{1,9},{9,1},{17,25},{25,17},{2,10},{10... | collective-permute-start | bytes 1572872 | tf_op jit(solution)/shard_map/ppermute | solution.py:773
  444.2 34.8 %collective-permute-start.39 = (bf16[256,1024]{1,0:T(8,128)(2,1)}, bf16[256,1024]{1,0:T(8,128)(2,1)}, u32[]{:S(2)}, u32[]{:S(2)}) collective-permute-start(bf16[256,1024]{1,0:T(8,128)(2,1)} %fusion.32), channel_id=1, source_target_pairs={{0,16},{8,24},{16,0},{24,8},{1,17},{9,25},{17,1},{25,9},{2,18},{10... | collective-permute-start | bytes 1572872 | tf_op jit(solution)/shard_map/ppermute | solution.py:773
  451.7 28.5 %all-to-all-start.4 = ((bf16[4,512,256]{2,1,0:T(8,128)(2,1)}), bf16[4,512,256]{2,1,0:T(8,128)(2,1)}, u32[]{:S(2)}, u32[]{:S(2)}) async-start(bf16[4,512,256]{2,1,0:T(8,128)(2,1)} %cut_columns.4), calls=%async_computation.5 | async-start | bytes 2097152 | tf_op jit(solution)/shard_map/all_to_all | solution.py:247
  456.4 86.8 %reduce-scatter.5.cloned.1.call-start = ((), (), s32[]{:S(2)}) async-start(), calls=%async_computation.9 | async-start | bytes 1310720 | tf_op jit(solution)/shard_map/reduce_scatter | solution.py:1068
  491.9 89.1 %all-gather.14.cloned.1.call-start = ((), (), s32[]{:S(2)}) async-start(), calls=%async_computation.13 | async-start | bytes 2621440 | tf_op jit(solution)/shard_map/all_gather | solution.py:1112
  497.4 41.0 %collective-permute-start.50 = (bf16[2,512,256]{2,1,0:T(8,128)(2,1)}, bf16[2,512,256]{2,1,0:T(8,128)(2,1)}, u32[]{:S(2)}, u32[]{:S(2)}) collective-permute-start(bf16[2,512,256]{2,1,0:T(8,128)(2,1)} %get-tuple-element.327), channel_id=1, source_target_pairs={{0,4},{4,0},{1,5},{5,1},{2,6},{6,2},{3,7},{7,3},{8,12},{12,8},{9,1... | collective-permute-start | bytes 1572872 | tf_op jit(solution)/shard_map/ppermute | solution.py:189
  503.4 25.6 %collective-permute-start.44 = (bf16[2,256,1024]{2,1,0:T(8,128)(2,1)}, bf16[2,256,1024]{2,1,0:T(8,128)(2,1)}, u32[]{:S(2)}, u32[]{:S(2)}) collective-permute-start(bf16[2,256,1024]{2,1,0:T(8,128)(2,1)} %slice.413), channel_id=1, source_target_pairs={{0,8},{8,0},{16,24},{24,16},{1,9},{9,1},{17,25},{25,17},{2,10},{10... | collective-permute-start | bytes 3145736 | tf_op jit(solution)/shard_map/ppermute | solution.py:773
  504.2 26.5 %collective-permute-start.45 = (bf16[2,256,1024]{2,1,0:T(8,128)(2,1)}, bf16[2,256,1024]{2,1,0:T(8,128)(2,1)}, u32[]{:S(2)}, u32[]{:S(2)}) collective-permute-start(bf16[2,256,1024]{2,1,0:T(8,128)(2,1)} %pad_maximum_fusion.17), channel_id=1, source_target_pairs={{0,16},{8,24},{16,0},{24,8},{1,17},{9,25},{17,1},{25,9},{2,18},{10... | collective-permute-start | bytes 3145736 | tf_op jit(solution)/shard_map/ppermute | solution.py:773
  530.6 39.5 %all-to-all-start.5 = ((bf16[4,512,256]{2,1,0:T(8,128)(2,1)}), bf16[4,512,256]{2,1,0:T(8,128)(2,1)S(1)}, u32[]{:S(2)}, u32[]{:S(2)}) async-start(bf16[4,512,256]{2,1,0:T(8,128)(2,1)} %cut_columns.5), calls=%async_computation.6 | async-start | bytes 2097152 | tf_op jit(solution)/shard_map/all_to_all | solution.py:247
  534.1 65.8 %all-gather.8.cloned.1.call-start = ((), (), s32[]{:S(2)}) async-start(), calls=%async_computation.10 | async-start | bytes 1310720 | tf_op jit(solution)/shard_map/all_gather | solution.py:1128
  544.4 25.6 %collective-permute-start.47 = (bf16[256,1024]{1,0:T(8,128)(2,1)S(1)}, bf16[256,1024]{1,0:T(8,128)(2,1)S(1)}, u32[]{:S(2)}, u32[]{:S(2)}) collective-permute-start(bf16[256,1024]{1,0:T(8,128)(2,1)S(1)} %maximum_add_fusion), channel_id=1, source_target_pairs={{0,8},{8,0},{16,24},{24,16},{1,9},{9,1},{17,25},{25,17},{2,10},{10... | collective-permute-start | bytes 1572872 | tf_op jit(solution)/shard_map/ppermute | solution.py:773
  571.0 25.4 %collective-permute-start.56 = (bf16[2,512,256]{2,1,0:T(8,128)(2,1)S(1)}, bf16[2,512,256]{2,1,0:T(8,128)(2,1)S(1)}, u32[]{:S(2)}, u32[]{:S(2)}) collective-permute-start(bf16[2,512,256]{2,1,0:T(8,128)(2,1)S(1)} %get-tuple-element.323), channel_id=1, source_target_pairs={{0,4},{4,0},{1,5},{5,1},{2,6},{6,2},{3,7},{7,3},{8,12},{12,8},{9,1... | collective-permute-start | bytes 1572872 | tf_op jit(solution)/shard_map/ppermute | solution.py:189
  574.2 25.7 %collective-permute-start.53 = (bf16[512,256]{1,0:T(8,128)(2,1)}, bf16[512,256]{1,0:T(8,128)(2,1)S(1)}, u32[]{:S(2)}, u32[]{:S(2)}) collective-permute-start(bf16[512,256]{1,0:T(8,128)(2,1)} %get-tuple-element.193), channel_id=1, source_target_pairs={{0,3},{1,0},{2,1},{3,2},{4,7},{5,4},{6,5},{7,6},{8,11},{9,8},{10,9... | collective-permute-start | bytes 786440 | tf_op jit(solution)/shard_map/ppermute | solution.py:193
  (135 other events, 1386.8 us)
Sparse Core Ops, SparseCore 0:
  40.9 45.2 all-gather.9
  88.2 45.4 all-gather.11
  409.1 44.0 reduce-scatter.2
  492.0 26.7 reduce-scatter.4
  520.5 40.6 all-gather.13
  562.9 25.5 all-gather.7
